TPU v7x, 256 devices: a whole 4x4x8 slice. The times are simulated.
256 devices in a mesh: tm: 8 (over y, z_hi), blk: 32 (over z_lo, x, core).
Axes of the slice: x: 4, y: 4, z: 8 (z_hi: 2, z_lo: 4; z = z_hi * 4 + z_lo), core: 2. Of those that a mesh axis runs over, the one named last changes fastest.
Arguments:
- frames_x: bfloat16 [512, 64, 2048], P('tm', 'blk'), may hold values from -6 to 6
- bc_weight: bfloat16 [2048, 256], replicated, may hold values from -0.125 to 0.125
- decay_codes: int32 [512, 64, 32], P('tm', 'blk'), may hold values from 32 to 32768
- decay_rates: float32 [32], replicated, may hold values from 0.025 to 2
- skip_gain: float32 [32], replicated, may hold values from 0.5 to 1.5
- queries: bfloat16 [512, 64, 2048], P('tm', 'blk')
- keys: bfloat16 [512, 64, 2048], P('tm', 'blk')
- values: bfloat16 [512, 64, 2048], P('tm', 'blk'), may hold values from -6 to 6
- cotangent: bfloat16 [512, 64, 2048], P('tm', 'blk'), may hold values from -6 to 6
Outputs:
- grad_x: bfloat16 [512, 64, 2048], P('tm', 'blk')
- grad_q: bfloat16 [512, 64, 2048], P('tm', 'blk')
- grad_k: bfloat16 [512, 64, 2048], P('tm', 'blk')
- grad_v: bfloat16 [512, 64, 2048], P('tm', 'blk')
- grad_bc: float32 [2048, 256], P(('tm', 'blk'))
All inputs are finite; a program needn't handle non-finite values.
Results may differ from a plain program's by a relative error of at most 0.025.
Values may be sent and summed in bfloat16 or wider, within the bound.
No kernel may reach another device: no remote copies, remote signals or barrier semaphores. Data moves between devices by JAX's collectives and lax.ppermute only.
A program may use at most 192 MiB of HBM per device.

v0:
```python
import jax
import jax.numpy as jnp
from jax import lax
from jax.sharding import PartitionSpec as P

WIN = 64


INJECT = 0.015625
CODE_UNIT = 4096.0
SCALE = 0.125
EXACT = lax.Precision.HIGHEST


def carried_in(shard, axis, combine, identity, reverse):
    devices, here = (lax.axis_size(axis), lax.axis_index(axis))
    everything = jax.tree.map(
        lambda part, kind: lax.all_gather(part.astype(kind), axis),
        shard,
        (jnp.bfloat16, jnp.bfloat16),
    )
    start = jax.tree.map(
        lambda part, zero: jnp.broadcast_to(jnp.asarray(zero, part.dtype), part.shape),
        shard,
        identity,
    )

    def hop(k, before):
        at = devices - 1 - k if reverse else k
        reached = at > here if reverse else at < here
        new = combine(
            before, jax.tree.map(lambda part, own: part[at].astype(own.dtype), everything, shard)
        )
        return jax.tree.map(lambda a, b: jnp.where(reached, a, b), new, before)

    return lax.fori_loop(0, devices, hop, start)


def from_behind(shard, axis, by):
    devices = lax.axis_size(axis)
    pairs = [(i, i + by) for i in range(devices) if 0 <= i + by < devices]
    return lax.ppermute(shard, axis, pairs)


def forward_join(earlier, later):
    return (earlier[0] * later[0], later[0][:, :, None, None] * earlier[1] + later[1])


def backward_join(earlier, later):
    return (earlier[0] * later[0], later[1] + later[0][:, :, None, None] * earlier[1])


def local(
    frames_x, bc_weight, decay_codes, decay_rates, skip_gain, queries, keys, values, cotangent
):
    length, blocks, model_width = frames_x.shape
    head_count = decay_rates.shape[0]
    head_size = model_width // head_count
    state_size = bc_weight.shape[1] // 2
    window = WIN
    shape_heads = (length, blocks, head_count, head_size)
    flat_x = frames_x.reshape(length * blocks, model_width)
    bc_rows = jnp.dot(flat_x, bc_weight, preferred_element_type=jnp.float32).astype(jnp.bfloat16)
    bc_rows = bc_rows.reshape(length, blocks, 2 * state_size)
    b_half = bc_rows[:, :, :state_size]
    c_half = bc_rows[:, :, state_size:]
    b_float = b_half.astype(jnp.float32)
    c_float = c_half.astype(jnp.float32)
    x_heads = frames_x.reshape(shape_heads)
    g_heads = cotangent.reshape(shape_heads)
    x_float = x_heads.astype(jnp.float32)
    g_float = g_heads.astype(jnp.float32)
    log_decay = -decay_rates * decay_codes.astype(jnp.float32) / CODE_UNIT
    cumulative = jnp.cumsum(log_decay, axis=0)
    log_total = cumulative[-1]
    cum_bht = jnp.transpose(cumulative, (1, 2, 0))
    log_gap = cum_bht[:, :, None, :] - cum_bht[:, :, :, None]
    positions = jnp.arange(length)
    forward_mask = positions[:, None] <= positions[None, :]
    decay_mat = jnp.where(forward_mask, jnp.exp(jnp.where(forward_mask, log_gap, 0.0)), 0.0)
    inner_xg = jnp.einsum("tbhp,sbhp->bhts", x_heads, g_heads, preferred_element_type=jnp.float32)
    mixing = INJECT * jnp.sum(decay_mat * inner_xg, axis=1)
    grad_b_local = jnp.einsum("bts,sbn->tbn", mixing, c_float, precision=EXACT)
    grad_c_local = jnp.einsum("bts,tbn->sbn", mixing, b_float, precision=EXACT)
    kernel = jnp.einsum("tbn,sbn->bts", b_half, c_half, preferred_element_type=jnp.float32)
    grad_x_local = INJECT * jnp.einsum(
        "bhts,sbhp->tbhp", decay_mat * kernel[:, None], g_float, precision=EXACT
    )
    to_end = jnp.exp(log_total[None] - cumulative)
    growth = jnp.exp(cumulative)
    summary = INJECT * jnp.einsum("tbh,tbhp,tbn->bhpn", to_end, x_float, b_float, precision=EXACT)
    adjoint = jnp.einsum("tbh,tbhp,tbn->bhpn", growth, g_float, c_float, precision=EXACT)
    total_decay = jnp.exp(log_total)
    unit_decay = jnp.ones_like(total_decay)
    empty_state = jnp.zeros_like(summary)
    carried = carried_in(
        (total_decay, summary), "tm", forward_join, (unit_decay, empty_state), False
    )[1]
    incoming = carried_in(
        (total_decay, adjoint), "tm", backward_join, (unit_decay, empty_state), True
    )[1]
    grad_c = grad_c_local + jnp.einsum(
        "tbh,tbhp,bhpn->tbn", growth, g_float, carried, precision=EXACT
    )
    grad_scan_x = grad_x_local + INJECT * jnp.einsum(
        "tbh,bhpn,tbn->tbhp", to_end, incoming, b_float, precision=EXACT
    )
    grad_b = grad_b_local + INJECT * jnp.einsum(
        "tbh,tbhp,bhpn->tbn", to_end, x_float, incoming, precision=EXACT
    )
    bc_cot = jnp.concatenate([grad_b, grad_c], axis=2).astype(jnp.bfloat16)
    flat_cot = bc_cot.reshape(length * blocks, 2 * state_size)
    back_proj = lax.dot_general(
        flat_cot, bc_weight, (((1,), (1,)), ((), ())), preferred_element_type=jnp.float32
    )
    skip_term = g_float * skip_gain[:, None]
    grad_x = (grad_scan_x + skip_term).reshape(length * blocks, model_width) + back_proj
    grad_x = grad_x.astype(jnp.bfloat16).reshape(length, blocks, model_width)
    token_total = length * blocks * lax.axis_size("tm") * lax.axis_size("blk")
    grad_bc = lax.psum_scatter(
        lax.dot_general(
            flat_x, flat_cot, (((0,), (0,)), ((), ())), preferred_element_type=jnp.float32
        )
        / token_total,
        ("tm", "blk"),
        scatter_dimension=0,
        tiled=True,
    )
    time_index = lax.axis_index("tm")
    group_count = length // window
    q_heads = queries.reshape(shape_heads)
    k_heads = keys.reshape(shape_heads)
    v_heads = values.reshape(shape_heads)
    rim_keys, rim_values = from_behind((k_heads, v_heads), "tm", 1)
    part_shape = (group_count, window, blocks, head_count, head_size)
    q_parts = q_heads.reshape(part_shape)
    g_parts = g_heads.reshape(part_shape)
    g_part_float = g_float.reshape(part_shape)
    ext_keys = jnp.concatenate([rim_keys, k_heads], axis=0).reshape(
        (group_count + 1,) + part_shape[1:]
    )
    ext_values = jnp.concatenate([rim_values, v_heads], axis=0).reshape(
        (group_count + 1,) + part_shape[1:]
    )
    key_pairs = jnp.concatenate([ext_keys[:-1], ext_keys[1:]], axis=1)
    value_pairs = jnp.concatenate([ext_values[:-1], ext_values[1:]], axis=1)
    query_pos = jnp.arange(window)[:, None]
    key_pos = jnp.arange(2 * window)[None, :]
    in_window = (key_pos >= query_pos) & (key_pos <= query_pos + window)
    key_exists = (
        (jnp.arange(group_count) > 0)[:, None, None] | (time_index > 0) | (key_pos >= window)[None]
    )
    allowed = (in_window[None] & key_exists)[:, None, None]
    scores = (
        jnp.einsum("ktbhp,kjbhp->kbhtj", q_parts, key_pairs, preferred_element_type=jnp.float32)
        * SCALE
    )
    masked = jnp.where(allowed, scores, -jnp.inf)
    row_max = jnp.max(masked, axis=-1)
    log_norm = row_max + jnp.log(jnp.sum(jnp.exp(masked - row_max[..., None]), axis=-1))
    probability = jnp.where(allowed, jnp.exp(scores - log_norm[..., None]), 0.0)
    weights = probability.astype(jnp.bfloat16)
    attended = jnp.einsum(
        "kbhtj,kjbhp->ktbhp", weights, value_pairs, preferred_element_type=jnp.float32
    )
    delta_row = jnp.sum(g_part_float * attended, axis=-1)
    grad_v_pairs = jnp.einsum(
        "kbhtj,ktbhp->kjbhp", weights, g_parts, preferred_element_type=jnp.float32
    )
    value_inner = jnp.einsum(
        "ktbhp,kjbhp->kbhtj", g_parts, value_pairs, preferred_element_type=jnp.float32
    )
    score_cot = (
        probability * (value_inner - jnp.transpose(delta_row, (0, 2, 3, 1))[..., None]) * SCALE
    )
    score_cot = score_cot.astype(jnp.bfloat16)
    grad_q = jnp.einsum(
        "kbhtj,kjbhp->ktbhp", score_cot, key_pairs, preferred_element_type=jnp.float32
    )
    grad_k_pairs = jnp.einsum(
        "kbhtj,ktbhp->kjbhp", score_cot, q_parts, preferred_element_type=jnp.float32
    )
    back_keys, back_values = (
        from_behind(grad_k_pairs[0, :window].astype(jnp.bfloat16), "tm", -1).astype(jnp.float32),
        from_behind(grad_v_pairs[0, :window].astype(jnp.bfloat16), "tm", -1).astype(jnp.float32),
    )
    later_keys = jnp.concatenate([grad_k_pairs[1:, :window], back_keys[None]], axis=0)
    later_values = jnp.concatenate([grad_v_pairs[1:, :window], back_values[None]], axis=0)
    grad_k = (
        (grad_k_pairs[:, window:] + later_keys)
        .reshape(length, blocks, model_width)
        .astype(jnp.bfloat16)
    )
    grad_v = (
        (grad_v_pairs[:, window:] + later_values)
        .reshape(length, blocks, model_width)
        .astype(jnp.bfloat16)
    )
    grad_q = grad_q.reshape(length, blocks, model_width).astype(jnp.bfloat16)
    return (grad_x, grad_q, grad_k, grad_v, grad_bc)


def solution(mesh):
    placed = (
        P("tm", "blk", None),
        P(),
        P("tm", "blk", None),
        P(),
        P(),
        P("tm", "blk", None),
        P("tm", "blk", None),
        P("tm", "blk", None),
        P("tm", "blk", None),
    )
    return jax.shard_map(
        local,
        mesh=mesh,
        in_specs=placed,
        out_specs=(
            P("tm", "blk", None),
            P("tm", "blk", None),
            P("tm", "blk", None),
            P("tm", "blk", None),
            P(("tm", "blk"), None),
        ),
        check_vma=False,
    )
```

profile of v0, /device:TPU:2, one launch (start us, length us, event | category | flops | bytes accessed | tf_op | source)
XLA Modules:
  0.0 1766.5 jit_solution(13606138968896271660)
XLA Ops:
  10.1 3.5 fusion.23
  15.1 3.4 multiply_convert_fusion
  20.1 10.2 collective-permute-start
  31.6 2.3 collective-permute-start.1
  33.9 2.7 copy.97
  36.7 2.3 copy.118
  39.0 124.3 %all_gather.20 = bf16[8,2,32]{2,1,0:T(2,128)(2,1)S(1)} all-gather(bf16[1,2,32]{2,1,0:T(2,128)(2,1)S(1)} %get-tuple-element.307), channel_id=1, replica_groups=mesh['tm'=8,'blk'=32] {'tm'}, dimensions={0}, use_global_device_ids=true | all-gather | bytes 1152 | tf_op jit(solution)/shard_map/all_gather | solution.py:18
  163.5 4.8 fusion.19
  168.3 1.7 multiply_reduce_fusion
  170.0 102.6 %all-gather.5.cloned.1.call-done = bf16[16,32,64,128]{3,2,1,0:T(8,128)(2,1)} async-done(((bf16[2,32,64,128]{3,2,1,0:T(8,128)(2,1)}), bf16[16,32,64,128]{3,2,1,0:T(8,128)(2,1)}) %all-gather.5.cloned.1.call-update) | async-done | bytes 8388624 | tf_op jit(solution)/shard_map/all_gather | solution.py:18
  272.7 14.7 while.30
  272.7 1.8 fusion.107
  274.5 1.8 fusion.107
  276.3 1.8 fusion.107
  278.1 1.8 fusion.107
  279.9 1.8 fusion.107
  281.8 1.9 fusion.107
  283.7 1.8 fusion.107
  285.6 1.8 fusion.107
  287.4 156.0 %all-gather.7.cloned.1.call-done = bf16[16,32,64,128]{3,2,1,0:T(8,128)(2,1)} async-done(((bf16[2,32,64,128]{3,2,1,0:T(8,128)(2,1)}), bf16[16,32,64,128]{3,2,1,0:T(8,128)(2,1)}) %all-gather.7.cloned.1.call-update) | async-done | bytes 8388624 | tf_op jit(solution)/shard_map/all_gather | solution.py:18
  443.3 28.1 %while.31 = (s32[]{:T(128)}, f32[2,32,64,128]{3,2,1,0:T(8,128)}, s32[]{:T(128)}, bf16[8,2,32]{2,1,0:T(2,128)(2,1)S(1)}, bf16[8,2,32,64,128]{4,3,2,1,0:T(8,128)(2,1)}, /*index=5*/s32[]{:T(128)}, s32[]{:T(128)}) while((s32[]{:T(128)}, f32[2,32,64,128]{3,2,1,0:T(8,128)}, s32[]{:T(128)}, bf16[8,2,32]{2,1,0:T(2,128)(2,1)S(1)}, ...), condition=%wide.region_5.6_spmd.clone, body=%wide.region_4.5_spmd.clone.sunk | while | flops 2621508 | bytes 5243633 | solution.py:36
  443.4 3.0 fusion.108
  446.3 3.6 fusion.108
  449.9 3.6 fusion.108
  453.5 3.6 fusion.108
  457.1 3.6 fusion.108
  460.7 3.6 fusion.108
  464.3 3.6 fusion.108
  467.9 3.6 fusion.108
  471.5 4.9 fusion.25
  476.4 2.9 fusion.29
  479.7 1.8 fusion.3
  481.5 2.9 copy.112
  484.5 3.2 fusion.21
  489.3 2.9 fusion.10
  492.2 3.4 fusion.12
  499.4 1.6 convolution_bitcast_fusion.1
  503.7 3.3 convolution_convert_fusion
  506.9 2.3 copy.101
  509.2 21.2 %collective-permute-done.2 = bf16[64,2,32,64]{0,3,2,1:T(8,128)(2,1)} collective-permute-done((bf16[64,2,32,64]{0,3,2,1:T(8,128)(2,1)}, bf16[64,2,32,64]{0,3,2,1:T(8,128)(2,1)}, u32[]{:S(2)}, u32[]{:S(2)}) %collective-permute-start.2) | collective-permute-done | bytes 524320 | tf_op jit(solution)/shard_map/ppermute | solution.py:42
  530.4 3.5 fusion.9
  533.8 2.3 copy.102
  536.1 15.1 collective-permute-done.3
  551.2 3.5 fusion.8
  554.7 2.3 copy.103
  557.0 4.9 fusion.7
  564.8 1.7 fusion.6
  567.6 1192.4 %reduce-scatter.4.cloned.1.call-done = f32[8,256]{1,0:T(8,128)} async-done(((f32[2048,256]{1,0:T(8,128)}), f32[8,256]{1,0:T(8,128)}) %reduce-scatter.4.cloned.1.call-update) | async-done | bytes 8208
  (102 shorter events, 19.9 us)
Async XLA Ops:
  7.2 1.4 copy-start
  7.2 1.8 copy-start.18
  7.2 1.9 copy-start.16
  7.2 2.1 copy-start.13
  7.2 265.5 %all-gather.5.cloned.1.call-start = ((), (), s32[]{:S(2)}) async-start(), calls=%async_computation.1 | async-start | bytes 9437184 | tf_op jit(solution)/shard_map/all_gather | solution.py:18
  10.0 3.9 copy-start.1
  10.0 3.7 copy-start.8
  13.6 429.7 %all-gather.7.cloned.1.call-start = ((), (), s32[]{:S(2)}) async-start(), calls=%async_computation.2 | async-start | bytes 9437184 | tf_op jit(solution)/shard_map/all_gather | solution.py:18
  15.0 5.0 copy-start.10
  15.0 3.5 copy-start.14
  15.0 15.2 copy-start.15
  18.5 1741.5 %reduce-scatter.4.cloned.1.call-start = ((), (), s32[]{:S(2)}) async-start(), calls=%async_computation.3 | async-start | bytes 2105344
  20.1 464.4 %collective-permute-start = (bf16[64,2,32,64]{0,3,2,1:T(8,128)(2,1)}, bf16[64,2,32,64]{0,3,2,1:T(8,128)(2,1)}, u32[]{:S(2)}, u32[]{:S(2)}) collective-permute-start(bf16[64,2,32,64]{0,3,2,1:T(8,128)(2,1)} %bitcast.21), channel_id=1, source_target_pairs={{0,32},{32,64},{64,96},{96,128},{128,160},{160,192},{192,224},{1,3... | collective-permute-start | bytes 1572872 | tf_op jit(solution)/shard_map/ppermute | solution.py:42
  31.6 457.4 %collective-permute-start.1 = (bf16[64,2,32,64]{0,3,2,1:T(8,128)(2,1)}, bf16[64,2,32,64]{0,3,2,1:T(8,128)(2,1)}, u32[]{:S(2)}, u32[]{:S(2)}) collective-permute-start(bf16[64,2,32,64]{0,3,2,1:T(8,128)(2,1)} %bitcast.26), channel_id=1, source_target_pairs={{0,32},{32,64},{64,96},{96,128},{128,160},{160,192},{192,224},{1,3... | collective-permute-start | bytes 1572872 | tf_op jit(solution)/shard_map/ppermute | solution.py:42
  163.5 4.8 copy-start.2
  163.5 4.8 copy-start.11
  471.5 5.0 copy-start.12
  476.4 3.3 copy-start.9
  487.7 1.6 copy-start.7
  489.3 2.9 copy-start.3
  492.2 3.4 copy-start.6
  496.1 1.8 copy-start.5
  497.8 32.5 %collective-permute-start.2 = (bf16[64,2,32,64]{0,3,2,1:T(8,128)(2,1)}, bf16[64,2,32,64]{0,3,2,1:T(8,128)(2,1)}, u32[]{:S(2)}, u32[]{:S(2)}) collective-permute-start(bf16[64,2,32,64]{0,3,2,1:T(8,128)(2,1)} %fusion.32), channel_id=1, source_target_pairs={{32,0},{64,32},{96,64},{128,96},{160,128},{192,160},{224,192},{33,... | collective-permute-start | bytes 1572872 | tf_op jit(solution)/shard_map/ppermute | solution.py:42
  501.0 5.9 copy-start.4
  502.4 48.8 %collective-permute-start.3 = (bf16[64,2,32,64]{0,3,2,1:T(8,128)(2,1)}, bf16[64,2,32,64]{0,3,2,1:T(8,128)(2,1)}, u32[]{:S(2)}, u32[]{:S(2)}) collective-permute-start(bf16[64,2,32,64]{0,3,2,1:T(8,128)(2,1)} %fusion.33), channel_id=1, source_target_pairs={{32,0},{64,32},{96,64},{128,96},{160,128},{192,160},{224,192},{33,... | collective-permute-start | bytes 1572872 | tf_op jit(solution)/shard_map/ppermute | solution.py:42
  536.1 20.9 %copy-start.17 = (f32[32]{0:T(128)S(1)}, f32[32]{0:T(128)}, u32[]{:S(2)}) copy-start(f32[32]{0:T(128)} %param.17) | copy-start | bytes 388
Sparse Core Ops, SparseCore 0:
  13.7 258.8 all-gather.4
  275.3 168.0 all-gather.6
  484.6 1275.3 reduce-scatter.3
where the time goes:
time: 1770 us
  waiting for transfers between devices  1490 us (84%)
  blocking collectives  124 us (7%)
  other arithmetic  51.1 us (3%)
  matrix products  45.3 us (3%)
  local copies, waits for them, and re-layouts  28.7 us (2%)
    unnamed x4, waiting for transfers between devices  1190 us
    all_gather x2, waiting for transfers between devices, carried_in(): lax.all_gather(part.astype(kind), axis)  259 us
    all_gather x1, blocking collectives, carried_in(): lax.all_gather(part.astype(kind), axis)  124 us
    select_n x16, other arithmetic, hop(): return jax.tree.map(lambda a, b: jnp.where(reached, a, b), new, before)  42.5 us
    ppermute x4, waiting for transfers between devices, from_behind(): return lax.ppermute(shard, axis, pairs)  36.2 us
  transfers between devices with their start and end apart: 7, of which 5 were waited for; matrix products, arithmetic and copies ran while one was open for 7% of the time, Pallas kernels for 0%

commit v1 on v0

v1 whole, which is shorter than its diff:
```python
import functools

import jax
import jax.numpy as jnp
from jax import lax
from jax.experimental import pallas as pl
from jax.experimental.pallas import tpu as pltpu
from jax.sharding import Mesh, PartitionSpec as P

HEAD = 64
LANES = 128
INJECT = 0.015625
CODE_UNIT = 4096.0
SCALE = 0.125
LOW = -1e30
BF = jnp.bfloat16
F32 = jnp.float32
TM = ("y", "zh")
VM = pl.BlockSpec(memory_space=pltpu.VMEM)
SM = pl.BlockSpec(memory_space=pltpu.SMEM)


def call(body, outs, scalars, arrays, scratch=()):
    return pl.pallas_call(
        body,
        out_shape=[jax.ShapeDtypeStruct(s, d) for s, d in outs],
        in_specs=[SM] * len(scalars) + [VM] * len(arrays),
        out_specs=[VM] * len(outs),
        scratch_shapes=list(scratch),
        compiler_params=pltpu.CompilerParams(vmem_limit_bytes=48 * 1024 * 1024),
    )(*scalars, *arrays)


def nn(a, b):
    return lax.dot_general(a, b, (((1,), (0,)), ((), ())), preferred_element_type=F32)


def nt(a, b):
    return lax.dot_general(a, b, (((1,), (1,)), ((), ())), preferred_element_type=F32)


def tn(a, b):
    return lax.dot_general(a, b, (((0,), (0,)), ((), ())), preferred_element_type=F32)


def iota(shape, dim):
    return lax.broadcasted_iota(jnp.int32, shape, dim)


def one(cond):
    return jnp.where(cond, 1.0, 0.0).astype(BF)


def halves(value, scale=1.0):
    low = jnp.where(iota((1, LANES), 1) < HEAD, scale, 0.0).astype(BF)
    high = jnp.where(iota((1, LANES), 1) < HEAD, 0.0, scale).astype(BF)
    return jnp.concatenate([value * low, value * high], axis=0)


def side(value):
    n = value.shape[0] // 2
    return jnp.concatenate([value[:n], value[n:]], axis=1)


def pack_body(at, x, g, codes, own, out):
    z = at[0]
    rows, width = x.shape
    n = rows // 2
    row, col = iota((n, rows), 0), iota((n, rows), 1)
    keep, give = one(col == 2 * row + z), one(col == 2 * row + 1 - z)
    for pick, ref in ((keep, own), (give, out)):
        ref[:, :width] = nn(pick, x[...]).astype(BF)
        ref[:, width : 2 * width] = nn(pick, g[...]).astype(BF)
        ref[:, 2 * width :] = nn(pick, codes[...]).astype(BF)


def summary_body(
    at, own, got, w, rate, xs, gs, bc, sums, sums_t, scaled_x, scaled_g, leave, m1, m2, m3
):
    z, y = at[0], at[1]
    n = own.shape[0]
    rows = 2 * n
    width = xs.shape[1]
    mine = pl.multiple_of(z * n, n)
    other = pl.multiple_of((1 - z) * n, n)
    for src, start in ((own, mine), (got, other)):
        xs[pl.ds(start, n), :] = src[:, :width]
        gs[pl.ds(start, n), :] = src[:, width : 2 * width]
    first = jnp.where(z == 0, own[:, 2 * width :].astype(F32), got[:, 2 * width :].astype(F32))
    second = jnp.where(z == 0, got[:, 2 * width :].astype(F32), own[:, 2 * width :].astype(F32))
    codes = jnp.concatenate([first, second], axis=0).astype(BF)
    hi, lo = codes[:, :LANES], codes[:, LANES:]
    row, col = iota((rows, rows), 0), iota((rows, rows), 1)
    lower, upper = one(col <= row), one(row <= col)
    total = nn(lower, hi) * 256.0 + nn(lower, lo)
    sums[...] = total
    sums_t[...] = tn(hi, upper) * 256.0 + tn(lo, upper)
    whole = total.astype(jnp.int32)
    spread = one(iota((LANES, width), 1) // HEAD == iota((LANES, width), 0))
    wide = jnp.zeros((rows, width), F32)
    lasts = []
    for shift in (16, 8, 0):
        piece = ((whole >> shift) & 255).astype(F32).astype(BF)
        part = nn(piece, spread)
        lasts.append(part[rows - 1 :, :])
        wide = wide * 256.0 + part
    last = wide[rows - 1 :, :]
    slope = rate[...] * (-1.0 / CODE_UNIT)
    to_end = jnp.exp((last - wide) * slope)
    growth = jnp.exp(wide * slope)
    bc_rows = nn(xs[...], w[...]).astype(BF)
    bc[...] = bc_rows
    gone = xs[...].astype(F32) * to_end
    sx = gone.astype(BF)
    sg = (gs[...].astype(F32) * growth).astype(BF)
    scaled_x[...] = sx
    scaled_g[...] = sg
    leave[...] = to_end
    state = (tn(bc_rows[:, :LANES], sx) * INJECT).astype(BF)
    back = tn(bc_rows[:, LANES:], sg).astype(BF)
    tail = jnp.concatenate(lasts + [jnp.zeros((13, width), F32)], axis=0).astype(BF)
    for shift, ref in ((1, m1), (2, m2), (3, m3)):
        later = y + shift < 4

        @pl.when(later)
        def _():
            ref[:LANES, :] = state

        @pl.when(jnp.logical_not(later))
        def _():
            ref[:LANES, :] = back

        ref[LANES:, :] = tail


def inner_body(rate, xs, gs, bc, sums, sums_t, gx, gb, gc, x_t):
    rows, width = xs.shape
    row, col = iota((rows, rows), 0), iota((rows, rows), 1)
    ahead = row <= col
    b_rows, c_rows = bc[:, :LANES], bc[:, LANES:]
    kernel = nt(b_rows, c_rows) * INJECT
    mixing = jnp.zeros((rows, rows), F32)
    for p in range(width // LANES):
        at = slice(p * LANES, (p + 1) * LANES)
        x_pair, g_pair = xs[:, at], gs[:, at]
        both = nt(halves(x_pair), g_pair)
        parts = []
        for k in (0, 1):
            h = 2 * p + k
            gap = sums_t[h : h + 1, :] - sums[:, h : h + 1]
            decay = jnp.exp(jnp.where(ahead, gap * (rate[h] * (-1.0 / CODE_UNIT)), LOW))
            mixing = mixing + decay * both[k * rows : (k + 1) * rows]
            parts.append((decay * kernel).astype(BF))
        gx[:, at] = nn(jnp.concatenate(parts, axis=1), halves(g_pair))
        x_t[at, :] = x_pair.astype(F32).T.astype(BF)
    mixed = (mixing * INJECT).astype(BF)
    gb[...] = nn(mixed, c_rows)
    gc[...] = tn(mixed, b_rows)


def carry_body(
    at, order, m1, m2, m3, rate, gain, w, gs, bc, scaled_x, scaled_g, leave, gx, gb, gc, x_t,
    keep, give, partial,
):
    z, y = at[0], at[1]
    n = keep.shape[0]
    slope = rate[...] * (-1.0 / CODE_UNIT)

    def fade(ref):
        v = ref[LANES : LANES + 16, :].astype(F32)
        return ((v[0:1] * 256.0 + v[1:2]) * 256.0 + v[2:3]) * slope

    l1, l2, l3 = fade(m1), fade(m2), fade(m3)
    s1, s2, s3 = (m[:LANES, :].astype(F32) for m in (m1, m2, m3))

    def use(cond, log):
        return jnp.where(cond, jnp.exp(log), 0.0)

    zero = jnp.zeros_like(l1)
    state = use(y >= 1, zero) * s1 + use(y >= 2, l1) * s2 + use(y >= 3, l1 + l2) * s3
    back = use(y < 3, zero) * s3 + use(y < 2, l3) * s2 + use(y < 1, l3 + l2) * s1
    state, back = state.astype(BF), back.astype(BF)
    b_cot = gb[...] + nt(scaled_x[...], back) * INJECT
    c_cot = gc[...] + nt(scaled_g[...], state)
    cot = jnp.concatenate([b_cot, c_cot], axis=1).astype(BF)
    out = gx[...] + leave[...] * (nn(bc[:, :LANES], back) * INJECT)
    out = out + gs[...].astype(F32) * gain[...] + nt(cot, w[...])

    @pl.when(z == 0)
    def _():
        keep[...] = out[:n].astype(BF)
        give[...] = out[n:].astype(BF)

    @pl.when(z == 1)
    def _():
        keep[...] = out[n:].astype(BF)
        give[...] = out[:n].astype(BF)

    grad = nn(x_t[...], cot) * order
    for index in range(partial.shape[0]):
        partial[index] = grad[8 * index : 8 * index + 8]


def softened(k_pair, v_pair, q_pair, g_pair, seen):
    rows = q_pair.shape[0]
    score = nt(halves(k_pair, SCALE), q_pair)
    inner = nt(halves(v_pair), g_pair)
    result = []
    for k in (0, 1):
        s = jnp.where(seen, score[k * rows : (k + 1) * rows], LOW)
        result.append((s, inner[k * rows : (k + 1) * rows]))
    return result


def row_sums(s, d):
    top = jnp.max(s, axis=0, keepdims=True)
    e = jnp.exp(s - top)
    norm = jnp.sum(e, axis=0, keepdims=True)
    return e, top, norm, jnp.sum(e * d, axis=0, keepdims=True) / norm


def merged(log_a, delta_a, log_b, delta_b):
    top = jnp.maximum(log_a, log_b)
    a, b = jnp.exp(log_a - top), jnp.exp(log_b - top)
    norm = a + b
    return top + jnp.log(norm), (a * delta_a + b * delta_b) / norm


def seen_mask(rows, cross):
    key, query = iota((rows, rows), 0), iota((rows, rows), 1)
    order = key >= query if cross else key <= query
    return jnp.logical_and(order, (key & 1) == (query & 1))


def stats_body(q, k, v, g, stats):
    rows, width = q.shape
    heads = width // HEAD
    seen = seen_mask(rows, False)
    for p in range(width // LANES):
        at = slice(p * LANES, (p + 1) * LANES)
        for j, (s, d) in enumerate(softened(k[:, at], v[:, at], q[:, at], g[:, at], seen)):
            e, top, norm, delta = row_sums(s, d)
            stats[2 * p + j : 2 * p + j + 1, :] = top + jnp.log(norm)
            stats[heads + 2 * p + j : heads + 2 * p + j + 1, :] = delta


def products(ps, ds, q_pair, k_pair, g_pair):
    p_side = jnp.concatenate(ps, axis=1)
    d_side = jnp.concatenate(ds, axis=1)
    grad_v = nn(p_side, halves(g_pair))
    grad_k = nn(d_side, halves(q_pair, SCALE))
    grad_q = tn(jnp.concatenate(ds, axis=0), halves(k_pair, SCALE))
    return grad_q, grad_k, grad_v


def cross_body(q, g, theirs, k, v, stats, gq, gk, gv):
    rows, width = q.shape
    heads = width // HEAD
    seen = seen_mask(rows, True)
    for p in range(width // LANES):
        at = slice(p * LANES, (p + 1) * LANES)
        q_pair, k_pair, g_pair = q[:, at], k[:, at], g[:, at]
        ps, ds = [], []
        for j, (s, d) in enumerate(softened(k_pair, v[:, at], q_pair, g_pair, seen)):
            h = 2 * p + j
            e, top, norm, delta = row_sums(s, d)
            log_here = top + jnp.log(norm)
            stats[h : h + 1, :] = log_here
            stats[heads + h : heads + h + 1, :] = delta
            log_norm, delta = merged(
                log_here, delta, theirs[h : h + 1, :], theirs[heads + h : heads + h + 1, :]
            )
            prob = e * jnp.exp(top - log_norm)
            ps.append(prob.astype(BF))
            ds.append((prob * (d - delta)).astype(BF))
        a, b, c = products(ps, ds, q_pair, k_pair, g_pair)
        gq[:, at] = a.astype(BF)
        gk[:, at] = b
        gv[:, at] = c


def own_body(at_ref, q, k, v, g, ours, theirs, gk_far, gv_far, gq, gk, gv):
    rows, width = q.shape
    heads = width // HEAD
    seen = seen_mask(rows, False)
    begins = at_ref[2] == 0
    for p in range(width // LANES):
        at = slice(p * LANES, (p + 1) * LANES)
        q_pair, k_pair, g_pair = q[:, at], k[:, at], g[:, at]
        ps, ds = [], []
        for j, (s, d) in enumerate(softened(k_pair, v[:, at], q_pair, g_pair, seen)):
            h = 2 * p + j
            far = jnp.where(begins, LOW, theirs[h : h + 1, :])
            log_norm, delta = merged(
                ours[h : h + 1, :],
                ours[heads + h : heads + h + 1, :],
                far,
                theirs[heads + h : heads + h + 1, :],
            )
            prob = jnp.exp(s - log_norm)
            ps.append(prob.astype(BF))
            ds.append((prob * (d - delta)).astype(BF))
        a, b, c = products(ps, ds, q_pair, k_pair, g_pair)
        gq[:, at] = a
        gk[:, at] = (b + gk_far[:, at]).astype(BF)
        gv[:, at] = (c + gv_far[:, at]).astype(BF)


def after(value, *others):
    return lax.optimization_barrier((value,) + others)[0]


def local(
    frames_x, bc_weight, decay_codes, decay_rates, skip_gain, queries, keys, values, cotangent
):
    length, blocks, width = frames_x.shape
    rows = length * blocks
    heads = decay_rates.shape[0]
    tm = lax.axis_size(TM)
    ny, nx, nz = lax.axis_size("y"), lax.axis_size("x"), lax.axis_size(("zh", "zl"))
    y, z, core = lax.axis_index("y"), lax.axis_index("zh"), lax.axis_index("c")
    at = jnp.stack([z, y, 2 * y + z]).astype(jnp.int32)
    flip = [(0, 1), (1, 0)]
    to_prev = [(i, i - 1) for i in range(1, tm)]
    to_next = [(i - 1, i) for i in range(1, tm)]

    def flat(a):
        return a.reshape(rows, width)

    x2, g2, q2, k2, v2 = (flat(a) for a in (frames_x, cotangent, queries, keys, values))
    codes = decay_codes.reshape(rows, heads)
    pad = ((0, 0), (0, LANES - heads))
    codes = jnp.concatenate([jnp.pad(codes >> 8, pad), jnp.pad(codes & 255, pad)], axis=1)
    codes = codes.astype(BF)
    rate_wide = jnp.repeat(decay_rates, HEAD)[None]
    gain_wide = jnp.repeat(skip_gain, HEAD)[None]

    msg = (rows // 2, 2 * width + 2 * LANES)
    own, out = call(pack_body, [(msg, BF)] * 2, [at], [x2, g2, codes])
    got = lax.ppermute(out, "zh", flip)

    stats_own = call(stats_body, [((2 * heads, rows), F32)], [], [q2, k2, v2, g2])[0]
    stats_next = lax.ppermute(stats_own, TM, to_prev)
    q_next = lax.ppermute(after(q2, got), TM, to_prev)
    g_next = lax.ppermute(after(g2, got), TM, to_prev)

    wide = (rows, width)
    state = (LANES + 16, width)
    square = (rows, LANES)
    xs, gs, bc, sums, sums_t, scaled_x, scaled_g, leave, m1, m2, m3 = call(
        summary_body,
        [(wide, BF), (wide, BF), ((rows, 2 * LANES), BF), (square, F32), (square, F32)]
        + [(wide, BF), (wide, BF), (wide, F32)]
        + [(state, BF)] * 3,
        [at],
        [own, got, bc_weight, rate_wide],
    )
    m1, m2, m3 = (
        lax.ppermute(m, "y", [(i, (i + s) % ny) for i in range(ny)])
        for s, m in ((1, m1), (2, m2), (3, m3))
    )
    gx, gb, gc, x_t = call(
        inner_body,
        [(wide, F32), (square, F32), (square, F32), ((width, rows), BF)],
        [decay_rates],
        [xs, gs, bc, sums, sums_t],
    )
    order = 1.0 / (rows * tm * lax.axis_size(("zl", "x", "c")))
    keep, give, partial = call(
        lambda at_ref, *refs: carry_body(at_ref, order, *refs),
        [((rows // 2, width), BF)] * 2 + [((width // 8, 8, 2 * LANES), F32)],
        [at],
        [m1, m2, m3, rate_wide, gain_wide, bc_weight, gs, bc, scaled_x, scaled_g, leave, gx, gb, gc, x_t],
    )
    gx_far = lax.ppermute(give, "zh", flip)

    partial = partial.reshape(ny, nz, nx, 2, 8, 2 * LANES)
    mine = lax.dynamic_index_in_dim(partial, core, 3, False)
    yours = lax.dynamic_index_in_dim(partial, 1 - core, 3, False)
    chip = mine + lax.ppermute(yours, "c", flip)
    chip = jnp.swapaxes(chip, 1, 2).reshape(ny * nx, nz * 8, 2 * LANES).astype(BF)
    spread = lax.all_to_all(chip, ("y", "x"), 0, 0, tiled=True)
    plane = jnp.sum(spread.astype(F32), axis=0).astype(BF).reshape(nz, 8, 2 * LANES)
    spread = lax.all_to_all(plane, ("zh", "zl"), 0, 0, tiled=True)
    grad_bc = jnp.sum(spread.astype(F32), axis=0)

    stats_far, gq_out, gk_far, gv_far = call(
        cross_body,
        [((2 * heads, rows), F32), (wide, BF), (wide, F32), (wide, F32)],
        [],
        [q_next, g_next, stats_next, k2, v2],
    )
    stats_prev = lax.ppermute(stats_far, TM, to_next)
    gq_prev = lax.ppermute(gq_out, TM, to_next)
    gq, gk, gv = call(
        own_body,
        [(wide, F32), (wide, BF), (wide, BF)],
        [at],
        [q2, k2, v2, g2, stats_own, stats_prev, gk_far, gv_far],
    )
    gq = (gq + gq_prev.astype(F32)).astype(BF)
    shape = (length, blocks, width)
    grad_x = jnp.stack(
        [jnp.where(z == 0, keep, gx_far), jnp.where(z == 0, gx_far, keep)], axis=1
    )
    return grad_x, gq.reshape(shape), gk.reshape(shape), gv.reshape(shape), grad_bc


def solution(mesh):
    tm, blk = mesh.devices.shape
    fine = Mesh(
        mesh.devices.reshape(tm // 2, 2, blk // 8, 4, 2), TM + ("zl", "x", "c")
    )
    tokens = P(TM, ("zl", "x", "c"), None)
    return jax.shard_map(
        local,
        mesh=fine,
        in_specs=(tokens, P(), tokens, P(), P(), tokens, tokens, tokens, tokens),
        out_specs=(tokens,) * 4 + (P(TM + ("zl", "x", "c"), None),),
        check_vma=False,
    )
```

time: 1770 us -> 214 us (0.12)
  waiting for transfers between devices: 1490 us -> 73.2 us
  blocking collectives: 124 us -> 0 us
  starting transfers between devices: 15.4 us -> 77 us
  other arithmetic: 51.1 us -> 5.53 us
  matrix products: 45.3 us -> 0 us
  Pallas kernels: 0 us -> 24.8 us
    unnamed x4 -> x0, waiting for transfers between devices: 1190 us -> none
    all_gather x2 -> x0, waiting for transfers between devices: 259 us -> none  [carried_in(): lax.all_gather(part.astype(kind), axis)]
    all_gather x1 -> x0, blocking collectives: 124 us -> none  [carried_in(): lax.all_gather(part.astype(kind), axis)]
    dot_general x19 -> x0, matrix products: 45.3 us -> none  [the longest x1 4.93 us: local(): jnp.einsum('tbh,tbhp,bhpn->tbn', growth, g_float, carried, precision=EXACT)]
    select_n x16 -> x0, other arithmetic: 42.5 us -> none  [hop(): return jax.tree.map(lambda a, b: jnp.where(reached, a, b), new, before)]
    ppermute x4 -> x11, starting transfers between devices: 15.2 us -> 56.9 us  [the longest x1 31.4 us: local(): stats_prev = lax.ppermute(stats_far, TM, to_next)]
    ppermute x4 -> x11, waiting for transfers between devices: 36.2 us -> 62.7 us  [the longest x1 25.5 us: local(): stats_next = lax.ppermute(stats_own, TM, to_prev)]
    pallas_call x0 -> x7, Pallas kernels: none -> 24.8 us  [call(): pl.pallas_call(body, out_shape=[jax.ShapeDtypeStruct(s, d) for s, d in ou...]
  transfers between devices with their start and end apart: 7 -> 13, of which waited for: 5 -> 7; matrix products, arithmetic and copies ran while one was open for 7% -> 6% of each run, Pallas kernels for 0% -> 6%
where the time goes in v1:
time: 214 us; the launch traced here: 212 us
  starting transfers between devices  77 us (36%)
  waiting for transfers between devices  73.2 us (34%)
  local copies, waits for them, and re-layouts  30.2 us (14%)
  Pallas kernels  24.8 us (12%)
  other arithmetic  5.53 us (3%)
    ppermute x1, starting transfers between devices, local(): stats_prev = lax.ppermute(stats_far, TM, to_next)  31.4 us
    ppermute x1, waiting for transfers between devices, local(): stats_next = lax.ppermute(stats_own, TM, to_prev)  25.5 us
    pallas_call x7, Pallas kernels, call(): pl.pallas_call(body, out_shape=[jax.ShapeDtypeStruct(s, d) for s, d in ou...  24.8 us
    ppermute x3, waiting for transfers between devices, local(): lax.ppermute(m, 'y', [(i, (i + s) % ny) for i in range(ny)])  19.7 us
    unnamed x55, local copies, waits for them, and re-layouts  15.9 us
    ppermute x1, waiting for transfers between devices, local(): got = lax.ppermute(out, 'zh', flip)  14.9 us
    all_to_all x1, starting transfers between devices, local(): spread = lax.all_to_all(plane, ('zh', 'zl'), 0, 0, tiled=True)  13.4 us
    ppermute x1, starting transfers between devices, local(): got = lax.ppermute(out, 'zh', flip)  7.19 us
  transfers between devices with their start and end apart: 13, of which 7 were waited for; matrix products, arithmetic and copies ran while one was open for 6% of the time, Pallas kernels for 6%

profile of v1, /device:TPU:2, one launch (start us, length us, event | category | flops | bytes accessed | tf_op | source)
XLA Modules:
  0.0 211.5 jit_solution(16792903928872295607)
XLA Ops:
  0.6 1.2 reshape.50.g
  2.9 1.2 reshape.49.x
  4.2 1.8 shard_map.128
  6.0 7.2 %collective-permute-start = (bf16[64,4352]{1,0:T(8,128)(2,1)}, bf16[64,4352]{1,0:T(8,128)(2,1)S(1)}, u32[]{:S(2)}, u32[]{:S(2)}) collective-permute-start(bf16[64,4352]{1,0:T(8,128)(2,1)} %get-tuple-element.35), channel_id=1, source_target_pairs={{0,32},{32,0},{1,33},{33,1},{2,34},{34,2},{3,35},{35,3},{4,36},{36... | collective-permute-start | bytes 1671176 | tf_op jit(solution)/shard_map/ppermute | solution.py:340
  13.4 14.9 %collective-permute-done.got = bf16[64,4352]{1,0:T(8,128)(2,1)S(1)} collective-permute-done((bf16[64,4352]{1,0:T(8,128)(2,1)}, bf16[64,4352]{1,0:T(8,128)(2,1)S(1)}, u32[]{:S(2)}, u32[]{:S(2)}) %collective-permute-start) | collective-permute-done | bytes 557088 | tf_op jit(solution)/shard_map/ppermute | solution.py:340
  28.3 4.7 %shard_map.129 = (bf16[128,2048]{1,0:T(8,128)(2,1)S(1)}, bf16[128,2048]{1,0:T(8,128)(2,1)S(1)}, bf16[128,256]{1,0:T(8,128)(2,1)S(1)}, f32[128,128]{1,0:T(8,128)S...) custom-call(s32[3]{0:T(128)S(1)} %pad_add_fusion.at.at_ref, ...), custom_call_target="tpu_custom_call" | custom-call | tf_op jit(solution)/shard_map/pallas_call | solution.py:24
  33.0 0.8 copy-done.5
  35.4 1.5 collective-permute-start.1
  37.0 2.9 %collective-permute-start.2 = (bf16[144,2048]{1,0:T(8,128)(2,1)}, bf16[144,2048]{1,0:T(8,128)(2,1)S(1)}, u32[]{:S(2)}, u32[]{:S(2)}) collective-permute-start(bf16[144,2048]{1,0:T(8,128)(2,1)} %get-tuple-element.37), channel_id=1, source_target_pairs={{0,128},{64,192},{128,0},{192,64},{1,129},{65,193},{129,1},{193,65... | collective-permute-start | bytes 1769480 | tf_op jit(solution)/shard_map/ppermute | solution.py:359
  39.9 1.4 collective-permute-start.3
  41.4 1.0 copy-done.10
  42.4 1.9 shard_map.130
  44.4 1.0 copy-done.1
  45.3 6.6 %collective-permute-done.1.refs_0_ = bf16[144,2048]{1,0:T(8,128)(2,1)S(1)} collective-permute-done((bf16[144,2048]{1,0:T(8,128)(2,1)}, bf16[144,2048]{1,0:T(8,128)(2,1)S(1)}, u32[]{:S(2)}, u32[]{:S(2)}) %collective-permute-start.1) | collective-permute-done | bytes 589856 | tf_op jit(solution)/shard_map/ppermute | solution.py:359
  51.9 13.1 %collective-permute-done.2.refs_1_ = bf16[144,2048]{1,0:T(8,128)(2,1)S(1)} collective-permute-done((bf16[144,2048]{1,0:T(8,128)(2,1)}, bf16[144,2048]{1,0:T(8,128)(2,1)S(1)}, u32[]{:S(2)}, u32[]{:S(2)}) %collective-permute-start.2) | collective-permute-done | bytes 589856 | tf_op jit(solution)/shard_map/ppermute | solution.py:359
  65.1 1.0 copy-done.6
  66.1 1.0 copy-done.8
  67.2 4.9 %shard_map.131 = (bf16[64,2048]{1,0:T(8,128)(2,1)S(1)}, bf16[64,2048]{1,0:T(8,128)(2,1)S(1)}, f32[256,8,256]{2,1,0:T(8,128)}) custom-call(s32[3]{0:T(128)S(1)} %pad_add_fusion.at.at_ref, bf16[144,2048]{1,0:T(8,128)(2,1)S(1)} %collective-permute-done.1.refs_0_, bf16[144,2048]{1,0:T(8,128)(2,1)S(1)} %collective-permute-done.2.refs_1_, ...), custom_call_target="tpu_custom_call" | custom-call | tf_op jit(solution)/shard_map/pallas_call | solution.py:24
  72.0 3.0 %constant_dynamic-slice_fusion.1 = (f32[4,8,4,1,8,256]{5,4,3,2,1,0:T(8,128)}, f32[4,8,4,1,8,256]{5,4,3,2,1,0:T(8,128)S(1)}) fusion(f32[4,8,4,2,8,256]{5,4,3,2,1,0:T(8,128)} %bitcast.21, s32[]{:T(128)S(6)} %select_n.22, s32[]{:T(128)S(6)} %select_n.23), kind=kLoop, calls=%fused_computation.17 | loop fusion | bytes 4194312 | tf_op jit(solution)/shard_map/jit(dynamic_index_in_dim)/dynamic_slice | solution.py:378
  75.0 1.1 copy.29
  76.3 1.3 collective-permute-start.6
  77.6 1.3 collective-permute-start.5
  79.1 1.2 reshape.53.v
  80.4 1.2 shard_map.132.ours
  81.6 1.5 collective-permute-start.7
  83.0 25.5 %collective-permute-done.7.theirs = f32[64,128]{1,0:T(8,128)S(1)} collective-permute-done((f32[64,128]{1,0:T(8,128)S(1)}, f32[64,128]{1,0:T(8,128)S(1)}, u32[]{:S(2)}, u32[]{:S(2)}) %collective-permute-start.7) | collective-permute-done | bytes 32800 | tf_op jit(solution)/shard_map/ppermute | solution.py:343
  108.5 0.8 copy-done.13
  109.3 0.8 copy-done.15
  110.1 1.0 copy-done.14
  111.1 1.0 copy-done.16
  112.2 4.7 %shard_map.133 = (f32[64,128]{1,0:T(8,128)S(1)}, bf16[128,2048]{1,0:T(8,128)(2,1)S(1)}, f32[128,2048]{1,0:T(8,128)S(1)}, f32[128,2048]{1,0:T(8,128)S(1)}) custom-call(bf16[128,2048]{1,0:T(8,128)(2,1)S(1)} %copy-done.16, bf16[128,2048]{1,0:T(8,128)(2,1)S(1)} %copy-done.14, f32[64,128]{1,0:T(8,128)S(1)} %collective-permute-done.7.theirs, ...), custom_call_target="tpu_custom_call" | custom-call | tf_op jit(solution)/shard_map/pallas_call | solution.py:24
  116.9 1.0 copy-done.2
  118.7 31.4 %collective-permute-start.8 = (f32[64,128]{1,0:T(8,128)S(1)}, f32[64,128]{1,0:T(8,128)S(1)}, u32[]{:S(2)}, u32[]{:S(2)}) collective-permute-start(f32[64,128]{1,0:T(8,128)S(1)} %get-tuple-element.55), channel_id=1, source_target_pairs={{0,32},{32,64},{64,96},{96,128},{128,160},{160,192},{192,224},{1,3... | collective-permute-start | bytes 98312 | tf_op jit(solution)/shard_map/ppermute | solution.py:393
  150.2 2.7 %collective-permute-start.9 = (bf16[128,2048]{1,0:T(8,128)(2,1)}, bf16[128,2048]{1,0:T(8,128)(2,1)}, u32[]{:S(2)}, u32[]{:S(2)}) collective-permute-start(bf16[128,2048]{1,0:T(8,128)(2,1)} %copy-done.20), channel_id=1, source_target_pairs={{0,32},{32,64},{64,96},{96,128},{128,160},{160,192},{192,224},{1,3... | collective-permute-start | bytes 1572872 | tf_op jit(solution)/shard_map/ppermute | solution.py:394
  152.9 5.6 %shard_map.134 = (f32[128,2048]{1,0:T(8,128)S(1)}, bf16[128,2048]{1,0:T(8,128)(2,1)S(1)}, bf16[128,2048]{1,0:T(8,128)(2,1)S(1)}) custom-call(s32[3]{0:T(128)S(1)} %pad_add_fusion.at.at_ref, bf16[128,2048]{1,0:T(8,128)(2,1)S(1)} %reshape.51.q, bf16[128,2048]{1,0:T(8,128)(2,1)S(1)} %reshape.52.k, bf16[128,2048]{1,0:T(8,128)(2,1)S(1)} %reshape.53.v, ...), custom_call_target="tpu_custom_call" | custom-call | tf_op jit(solution)/shard_map/pallas_call | solution.py:24
  158.5 1.0 copy-done.3
  161.1 2.3 %reshape.55 = bf16[64,2,2048]{2,1,0:T(2,128)(2,1)} reshape(bf16[128,2048]{1,0:T(8,128)(2,1)} %copy-done.12) | data formatting | bytes 1048576 | tf_op jit(solution)/shard_map/reshape | solution.py:406
  163.4 2.2 %reshape.56 = bf16[64,2,2048]{2,1,0:T(2,128)(2,1)} reshape(bf16[128,2048]{1,0:T(8,128)(2,1)} %copy-done.11) | data formatting | bytes 1048576 | tf_op jit(solution)/shard_map/reshape | solution.py:406
  165.6 5.7 %collective-permute-start.4 = (bf16[64,2048]{1,0:T(8,128)(2,1)S(1)}, bf16[64,2048]{1,0:T(8,128)(2,1)S(1)}, u32[]{:S(2)}, u32[]{:S(2)}) collective-permute-start(bf16[64,2048]{1,0:T(8,128)(2,1)S(1)} %copy-done.22), channel_id=1, source_target_pairs={{0,32},{32,0},{1,33},{33,1},{2,34},{34,2},{3,35},{35,3},{4,36},{36... | collective-permute-start | bytes 786440 | tf_op jit(solution)/shard_map/ppermute | solution.py:375
  171.3 2.1 %fusion = bf16[4,8,4,8,256]{4,3,1,2,0:T(8,128)(2,1)} fusion(f32[4,8,4,8,256]{4,3,1,2,0:T(8,128)} %collective-permute-done.10, f32[4,8,4,1,8,256]{5,4,3,2,1,0:T(8,128)S(1)} %copy-done.23), kind=kLoop, calls=%fused_computation.1 | loop fusion | flops 524288 | bytes 2621440 | tf_op jit(solution)/shard_map/convert_element_type | solution.py:381
  173.4 6.7 %all-to-all-start = ((bf16[16,64,256]{2,1,0:T(8,128)(2,1)}), bf16[16,64,256]{2,1,0:T(8,128)(2,1)S(1)}, u32[]{:S(2)}, u32[]{:S(2)}) async-start(bf16[16,64,256]{2,1,0:T(8,128)(2,1)} %bitcast.11), calls=%async_computation | async-start | bytes 1048576 | tf_op jit(solution)/shard_map/all_to_all | solution.py:382
  180.1 2.6 %collective-permute-done.4 = bf16[64,2048]{1,0:T(8,128)(2,1)S(1)} collective-permute-done((bf16[64,2048]{1,0:T(8,128)(2,1)S(1)}, bf16[64,2048]{1,0:T(8,128)(2,1)S(1)}, u32[]{:S(2)}, u32[]{:S(2)}) %collective-permute-start.4) | collective-permute-done | bytes 262176 | tf_op jit(solution)/shard_map/ppermute | solution.py:375
  182.8 1.3 copy.26
  184.1 4.7 %all-to-all-done = bf16[16,64,256]{2,1,0:T(8,128)(2,1)S(1)} async-done(((bf16[16,64,256]{2,1,0:T(8,128)(2,1)}), bf16[16,64,256]{2,1,0:T(8,128)(2,1)S(1)}, u32[]{:S(2)}, u32[]{:S(2)}) %all-to-all-start) | async-done | bytes 524320 | tf_op jit(solution)/shard_map/all_to_all | solution.py:382
  189.5 13.4 %all-to-all-start.1 = ((bf16[8,8,256]{2,1,0:T(8,128)(2,1)}), bf16[8,8,256]{2,1,0:T(8,128)(2,1)S(1)}, u32[]{:S(2)}, u32[]{:S(2)}) async-start(bf16[8,8,256]{2,1,0:T(8,128)(2,1)} %bitcast.12), calls=%async_computation.1 | async-start | bytes 65536 | tf_op jit(solution)/shard_map/all_to_all | solution.py:384
  202.9 1.1 add_convert_fusion
  204.1 1.1 reshape.54
  205.2 5.7 %all-to-all-done.1 = bf16[8,8,256]{2,1,0:T(8,128)(2,1)S(1)} async-done(((bf16[8,8,256]{2,1,0:T(8,128)(2,1)}), bf16[8,8,256]{2,1,0:T(8,128)(2,1)S(1)}, u32[]{:S(2)}, u32[]{:S(2)}) %all-to-all-start.1) | async-done | bytes 32800 | tf_op jit(solution)/shard_map/all_to_all | solution.py:384
  (65 shorter events, 7.2 us)
Async XLA Ops:
  0.6 12.6 %copy-start.19 = (f32[32]{0:T(128)S(1)}, f32[32]{0:T(128)}, u32[]{:S(2)}) copy-start(f32[32]{0:T(128)} %rate.1) | copy-start | bytes 388
  2.9 38.3 %copy-start.26 = (f32[32]{0:T(128)S(1)}, f32[32]{0:T(128)}, u32[]{:S(2)}) copy-start(f32[32]{0:T(128)} %param.13) | copy-start | bytes 388
  4.2 60.8 %copy-start = (bf16[2048,256]{1,0:T(8,128)(2,1)S(1)}, bf16[2048,256]{1,0:T(8,128)(2,1)}, u32[]{:S(2)}) copy-start(bf16[2048,256]{1,0:T(8,128)(2,1)} %refs_5_.1) | copy-start | bytes 3145732
  6.0 22.3 %collective-permute-start = (bf16[64,4352]{1,0:T(8,128)(2,1)}, bf16[64,4352]{1,0:T(8,128)(2,1)S(1)}, u32[]{:S(2)}, u32[]{:S(2)}) collective-permute-start(bf16[64,4352]{1,0:T(8,128)(2,1)} %get-tuple-element.35), channel_id=1, source_target_pairs={{0,32},{32,0},{1,33},{33,1},{2,34},{34,2},{3,35},{35,3},{4,36},{36... | collective-permute-start | bytes 1671176 | tf_op jit(solution)/shard_map/ppermute | solution.py:340
  33.0 0.8 copy-start.5
  33.8 0.8 copy-start.7
  34.6 0.8 copy-start.9
  35.4 16.5 %collective-permute-start.1 = (bf16[144,2048]{1,0:T(8,128)(2,1)}, bf16[144,2048]{1,0:T(8,128)(2,1)S(1)}, u32[]{:S(2)}, u32[]{:S(2)}) collective-permute-start(bf16[144,2048]{1,0:T(8,128)(2,1)} %get-tuple-element.36), channel_id=1, source_target_pairs={{0,64},{64,128},{128,192},{192,0},{1,65},{65,129},{129,193},{193,1... | collective-permute-start | bytes 1769480 | tf_op jit(solution)/shard_map/ppermute | solution.py:359
  37.0 28.1 %collective-permute-start.2 = (bf16[144,2048]{1,0:T(8,128)(2,1)}, bf16[144,2048]{1,0:T(8,128)(2,1)S(1)}, u32[]{:S(2)}, u32[]{:S(2)}) collective-permute-start(bf16[144,2048]{1,0:T(8,128)(2,1)} %get-tuple-element.37), channel_id=1, source_target_pairs={{0,128},{64,192},{128,0},{192,64},{1,129},{65,193},{129,1},{193,65... | collective-permute-start | bytes 1769480 | tf_op jit(solution)/shard_map/ppermute | solution.py:359
  39.9 25.2 %collective-permute-start.3 = (bf16[144,2048]{1,0:T(8,128)(2,1)}, bf16[144,2048]{1,0:T(8,128)(2,1)}, u32[]{:S(2)}, u32[]{:S(2)}) collective-permute-start(bf16[144,2048]{1,0:T(8,128)(2,1)} %get-tuple-element.38), channel_id=1, source_target_pairs={{0,192},{64,0},{128,64},{192,128},{1,193},{65,1},{129,65},{193,129... | collective-permute-start | bytes 1769480 | tf_op jit(solution)/shard_map/ppermute | solution.py:359
  41.4 1.0 copy-start.10
  44.4 1.0 copy-start.1
  65.1 1.0 copy-start.6
  66.1 1.0 copy-start.8
  72.0 3.0 %copy-start.17 = (bf16[64,2048]{1,0:T(8,128)(2,1)}, bf16[64,2048]{1,0:T(8,128)(2,1)S(1)}, u32[]{:S(2)}) copy-start(bf16[64,2048]{1,0:T(8,128)(2,1)S(1)} %get-tuple-element.51) | copy-start | bytes 786436
  72.0 3.0 %copy-start.21 = (bf16[64,2048]{1,0:T(8,128)(2,1)}, bf16[64,2048]{1,0:T(8,128)(2,1)S(1)}, u32[]{:S(2)}) copy-start(bf16[64,2048]{1,0:T(8,128)(2,1)S(1)} %get-tuple-element.52) | copy-start | bytes 786436
  75.0 1.1 copy-start.24
  75.0 3.9 %copy-start.25 = (bf16[64,2,2048]{2,1,0:T(2,128)(2,1)S(1)}, bf16[64,2,2048]{2,1,0:T(2,128)(2,1)}, u32[]{:S(2)}) copy-start(bf16[64,2,2048]{2,1,0:T(2,128)(2,1)} %param.15) | copy-start | bytes 1572868
  76.1 95.1 %collective-permute-start.10 = (f32[4,8,4,8,256]{4,3,1,2,0:T(8,128)}, f32[4,8,4,8,256]{4,3,1,2,0:T(8,128)}, u32[]{:S(2)}, u32[]{:S(2)}) collective-permute-start(f32[4,8,4,8,256]{4,3,1,2,0:T(8,128)} %bitcast.20), channel_id=1, source_target_pairs={{0,1},{1,0},{2,3},{3,2},{4,5},{5,4},{6,7},{7,6},{8,9},{9,8},{10,11... | collective-permute-start | bytes 3145736 | tf_op jit(solution)/shard_map/ppermute | solution.py:380
  76.3 32.2 %collective-permute-start.6 = (bf16[128,2048]{1,0:T(8,128)(2,1)S(1)}, bf16[128,2048]{1,0:T(8,128)(2,1)S(1)}, u32[]{:S(2)}, u32[]{:S(2)}) collective-permute-start(bf16[128,2048]{1,0:T(8,128)(2,1)S(1)} %reshape.50.g), channel_id=1, source_target_pairs={{32,0},{64,32},{96,64},{128,96},{160,128},{192,160},{224,192},{33,... | collective-permute-start | bytes 1572872 | tf_op jit(solution)/shard_map/ppermute | solution.py:345
  77.6 31.7 %collective-permute-start.5 = (bf16[128,2048]{1,0:T(8,128)(2,1)S(1)}, bf16[128,2048]{1,0:T(8,128)(2,1)S(1)}, u32[]{:S(2)}, u32[]{:S(2)}) collective-permute-start(bf16[128,2048]{1,0:T(8,128)(2,1)S(1)} %reshape.51.q), channel_id=1, source_target_pairs={{32,0},{64,32},{96,64},{128,96},{160,128},{192,160},{224,192},{33,... | collective-permute-start | bytes 1572872 | tf_op jit(solution)/shard_map/ppermute | solution.py:344
  81.6 26.9 %collective-permute-start.7 = (f32[64,128]{1,0:T(8,128)S(1)}, f32[64,128]{1,0:T(8,128)S(1)}, u32[]{:S(2)}, u32[]{:S(2)}) collective-permute-start(f32[64,128]{1,0:T(8,128)S(1)} %shard_map.132.ours), channel_id=1, source_target_pairs={{32,0},{64,32},{96,64},{128,96},{160,128},{192,160},{224,192},{33,... | collective-permute-start | bytes 98312 | tf_op jit(solution)/shard_map/ppermute | solution.py:343
  108.5 0.8 copy-start.13
  109.3 0.8 copy-start.15
  110.1 1.0 copy-start.14
  111.1 1.0 copy-start.16
  116.9 1.0 copy-start.2
  117.9 0.8 copy-start.20
  118.7 34.2 %collective-permute-start.8 = (f32[64,128]{1,0:T(8,128)S(1)}, f32[64,128]{1,0:T(8,128)S(1)}, u32[]{:S(2)}, u32[]{:S(2)}) collective-permute-start(f32[64,128]{1,0:T(8,128)S(1)} %get-tuple-element.55), channel_id=1, source_target_pairs={{0,32},{32,64},{64,96},{96,128},{128,160},{160,192},{192,224},{1,3... | collective-permute-start | bytes 98312 | tf_op jit(solution)/shard_map/ppermute | solution.py:393
  150.2 52.7 %collective-permute-start.9 = (bf16[128,2048]{1,0:T(8,128)(2,1)}, bf16[128,2048]{1,0:T(8,128)(2,1)}, u32[]{:S(2)}, u32[]{:S(2)}) collective-permute-start(bf16[128,2048]{1,0:T(8,128)(2,1)} %copy-done.20), channel_id=1, source_target_pairs={{0,32},{32,64},{64,96},{96,128},{128,160},{160,192},{192,224},{1,3... | collective-permute-start | bytes 1572872 | tf_op jit(solution)/shard_map/ppermute | solution.py:394
  158.5 1.0 copy-start.3
  159.5 0.8 copy-start.11
  160.3 0.8 copy-start.12
  161.1 4.5 %copy-start.22 = (bf16[64,2048]{1,0:T(8,128)(2,1)S(1)}, bf16[64,2048]{1,0:T(8,128)(2,1)}, u32[]{:S(2)}) copy-start(bf16[64,2048]{1,0:T(8,128)(2,1)} %copy-done.21) | copy-start | bytes 786436
  161.1 10.1 %copy-start.23 = (f32[4,8,4,1,8,256]{5,4,3,2,1,0:T(8,128)S(1)}, f32[4,8,4,1,8,256]{5,4,3,2,1,0:T(8,128)}, u32[]{:S(2)}) copy-start(f32[4,8,4,1,8,256]{5,4,3,2,1,0:T(8,128)} %get-tuple-element.78) | copy-start | bytes 3145732
  165.6 17.1 %copy-start.18 = (bf16[64,2048]{1,0:T(8,128)(2,1)S(1)}, bf16[64,2048]{1,0:T(8,128)(2,1)}, u32[]{:S(2)}) copy-start(bf16[64,2048]{1,0:T(8,128)(2,1)} %copy-done.17) | copy-start | bytes 786436
  165.6 17.1 %collective-permute-start.4 = (bf16[64,2048]{1,0:T(8,128)(2,1)S(1)}, bf16[64,2048]{1,0:T(8,128)(2,1)S(1)}, u32[]{:S(2)}, u32[]{:S(2)}) collective-permute-start(bf16[64,2048]{1,0:T(8,128)(2,1)S(1)} %copy-done.22), channel_id=1, source_target_pairs={{0,32},{32,0},{1,33},{33,1},{2,34},{34,2},{3,35},{35,3},{4,36},{36... | collective-permute-start | bytes 786440 | tf_op jit(solution)/shard_map/ppermute | solution.py:375
  173.4 15.4 %all-to-all-start = ((bf16[16,64,256]{2,1,0:T(8,128)(2,1)}), bf16[16,64,256]{2,1,0:T(8,128)(2,1)S(1)}, u32[]{:S(2)}, u32[]{:S(2)}) async-start(bf16[16,64,256]{2,1,0:T(8,128)(2,1)} %bitcast.11), calls=%async_computation | async-start | bytes 1048576 | tf_op jit(solution)/shard_map/all_to_all | solution.py:382
  180.1 22.8 %copy-start.4 = (f32[128,2048]{1,0:T(8,128)S(1)}, f32[128,2048]{1,0:T(8,128)}, u32[]{:S(2)}) copy-start(f32[128,2048]{1,0:T(8,128)} %copy-done.3) | copy-start | bytes 3145732
  189.5 21.4 %all-to-all-start.1 = ((bf16[8,8,256]{2,1,0:T(8,128)(2,1)}), bf16[8,8,256]{2,1,0:T(8,128)(2,1)S(1)}, u32[]{:S(2)}, u32[]{:S(2)}) async-start(bf16[8,8,256]{2,1,0:T(8,128)(2,1)} %bitcast.12), calls=%async_computation.1 | async-start | bytes 65536 | tf_op jit(solution)/shard_map/all_to_all | solution.py:384

commit v2 on v1

--- a/solution.py
+++ b/solution.py
@@ -12,6 +12,7 @@
 INJECT = 0.015625
 CODE_UNIT = 4096.0
 SCALE = 0.125
+VMEM_BYTES = 60 * 1024 * 1024
 LOW = -1e30
 BF = jnp.bfloat16
 F32 = jnp.float32
@@ -20,15 +21,22 @@
 SM = pl.BlockSpec(memory_space=pltpu.SMEM)
 
 
-def call(body, outs, scalars, arrays, scratch=()):
+def call(body, outs, scalars, arrays, first=()):
+    used = len(scalars) + len(arrays)
+
+    def run(*refs):
+        body(*refs[:used], *refs[used + len(first) :])
+
     return pl.pallas_call(
-        body,
+        run,
         out_shape=[jax.ShapeDtypeStruct(s, d) for s, d in outs],
-        in_specs=[SM] * len(scalars) + [VM] * len(arrays),
-        out_specs=[VM] * len(outs),
-        scratch_shapes=list(scratch),
-        compiler_params=pltpu.CompilerParams(vmem_limit_bytes=48 * 1024 * 1024),
-    )(*scalars, *arrays)
+        in_specs=[SM] * len(scalars) + [pl.BlockSpec(a.shape, lambda *_, n=a.ndim: (0,) * n) for a in arrays]
+        + [pl.BlockSpec(memory_space=pl.ANY)] * len(first),
+        out_specs=[pl.BlockSpec(s, lambda *_, n=len(s): (0,) * n) for s, d in outs],
+        grid=(1,),
+        cost_estimate=pl.CostEstimate(flops=1, bytes_accessed=1, transcendentals=0),
+        compiler_params=pltpu.CompilerParams(vmem_limit_bytes=VMEM_BYTES),
+    )(*scalars, *arrays, *first)
 
 
 def nn(a, b):
@@ -60,6 +68,30 @@
 def side(value):
     n = value.shape[0] // 2
     return jnp.concatenate([value[:n], value[n:]], axis=1)
+
+
+def join_body(q, g, stats, out):
+    rows = q.shape[0]
+    out[:rows, :] = q[...]
+    out[rows : 2 * rows, :] = g[...]
+    out[2 * rows :, :] = jnp.zeros((16, q.shape[1]), BF)
+    rest = stats[...]
+    groups = stats.shape[0] // 16
+    for piece in range(3):
+        part = rest.astype(BF)
+        rest = rest - part.astype(F32)
+        for k in range(groups):
+            lane = (piece * groups + k) * LANES
+            out[2 * rows :, lane : lane + LANES] = part[16 * k : 16 * k + 16]
+
+
+def joined_stats(qg, rows, groups):
+    found = []
+    for k in range(groups):
+        lanes = [(piece * groups + k) * LANES for piece in range(3)]
+        a, b, c = (qg[2 * rows :, lane : lane + LANES].astype(F32) for lane in lanes)
+        found.append(a + (b + c))
+    return jnp.concatenate(found, axis=0)
 
 
 def pack_body(at, x, g, codes, own, out):
@@ -68,10 +100,15 @@
     n = rows // 2
     row, col = iota((n, rows), 0), iota((n, rows), 1)
     keep, give = one(col == 2 * row + z), one(col == 2 * row + 1 - z)
-    for pick, ref in ((keep, own), (give, out)):
+    here = z == 0
+    for pick, code, ref in (
+        (keep, jnp.where(here, codes[0], codes[1]), own),
+        (give, jnp.where(here, codes[1], codes[0]), out),
+    ):
         ref[:, :width] = nn(pick, x[...]).astype(BF)
         ref[:, width : 2 * width] = nn(pick, g[...]).astype(BF)
-        ref[:, 2 * width :] = nn(pick, codes[...]).astype(BF)
+        both = jnp.concatenate([code >> 8, code & 255], axis=0).astype(F32)
+        ref[:, 2 * width :] = jnp.concatenate([both, jnp.zeros_like(both)], axis=1).astype(BF)
 
 
 def summary_body(
@@ -86,15 +123,19 @@
     for src, start in ((own, mine), (got, other)):
         xs[pl.ds(start, n), :] = src[:, :width]
         gs[pl.ds(start, n), :] = src[:, width : 2 * width]
-    first = jnp.where(z == 0, own[:, 2 * width :].astype(F32), got[:, 2 * width :].astype(F32))
-    second = jnp.where(z == 0, got[:, 2 * width :].astype(F32), own[:, 2 * width :].astype(F32))
-    codes = jnp.concatenate([first, second], axis=0).astype(BF)
-    hi, lo = codes[:, :LANES], codes[:, LANES:]
+    mine_codes, other_codes = own[:, 2 * width :].astype(F32), got[:, 2 * width :].astype(F32)
+    early = jnp.where(z == 0, mine_codes, other_codes)
+    late = jnp.where(z == 0, other_codes, mine_codes)
+    codes = jnp.concatenate([early[:, :n], late[:, :n]], axis=1)
+    heads = codes.shape[0] // 2
+    blank = jnp.zeros((LANES - heads, rows), F32)
+    hi = jnp.concatenate([codes[:heads], blank], axis=0).astype(BF)
+    lo = jnp.concatenate([codes[heads:], blank], axis=0).astype(BF)
     row, col = iota((rows, rows), 0), iota((rows, rows), 1)
     lower, upper = one(col <= row), one(row <= col)
-    total = nn(lower, hi) * 256.0 + nn(lower, lo)
+    total = nt(lower, hi) * 256.0 + nt(lower, lo)
     sums[...] = total
-    sums_t[...] = tn(hi, upper) * 256.0 + tn(lo, upper)
+    sums_t[...] = nn(hi, upper) * 256.0 + nn(lo, upper)
     whole = total.astype(jnp.int32)
     spread = one(iota((LANES, width), 1) // HEAD == iota((LANES, width), 0))
     wide = jnp.zeros((rows, width), F32)
@@ -160,9 +201,9 @@
 
 def carry_body(
     at, order, m1, m2, m3, rate, gain, w, gs, bc, scaled_x, scaled_g, leave, gx, gb, gc, x_t,
-    keep, give, partial,
+    keep, give, mine, yours,
 ):
-    z, y = at[0], at[1]
+    z, y, core = at[0], at[1], at[3]
     n = keep.shape[0]
     slope = rate[...] * (-1.0 / CODE_UNIT)
 
@@ -197,8 +238,16 @@
         give[...] = out[:n].astype(BF)
 
     grad = nn(x_t[...], cot) * order
-    for index in range(partial.shape[0]):
-        partial[index] = grad[8 * index : 8 * index + 8]
+    for side in (0, 1):
+
+        @pl.when(core == side)
+        def _():
+            for index in range(mine.shape[0]):
+                xy, nz = index // 8, index % 8
+                block = (((xy // 4) * 8 + nz) * 4 + xy % 4) * 2
+                for ref, c in ((mine, side), (yours, 1 - side)):
+                    start = 8 * (block + c)
+                    ref[index] = grad[start : start + 8]
 
 
 def softened(k_pair, v_pair, q_pair, g_pair, seen):
@@ -253,13 +302,14 @@
     return grad_q, grad_k, grad_v
 
 
-def cross_body(q, g, theirs, k, v, stats, gq, gk, gv):
-    rows, width = q.shape
+def cross_body(qg, k, v, stats, gq, gk, gv):
+    rows, width = k.shape
     heads = width // HEAD
+    theirs = joined_stats(qg, rows, stats.shape[0] // 16)
     seen = seen_mask(rows, True)
     for p in range(width // LANES):
         at = slice(p * LANES, (p + 1) * LANES)
-        q_pair, k_pair, g_pair = q[:, at], k[:, at], g[:, at]
+        q_pair, k_pair, g_pair = qg[:rows, at], k[:, at], qg[rows : 2 * rows, at]
         ps, ds = [], []
         for j, (s, d) in enumerate(softened(k_pair, v[:, at], q_pair, g_pair, seen)):
             h = 2 * p + j
@@ -306,10 +356,6 @@
         gv[:, at] = (c + gv_far[:, at]).astype(BF)
 
 
-def after(value, *others):
-    return lax.optimization_barrier((value,) + others)[0]
-
-
 def local(
     frames_x, bc_weight, decay_codes, decay_rates, skip_gain, queries, keys, values, cotangent
 ):
@@ -319,7 +365,7 @@
     tm = lax.axis_size(TM)
     ny, nx, nz = lax.axis_size("y"), lax.axis_size("x"), lax.axis_size(("zh", "zl"))
     y, z, core = lax.axis_index("y"), lax.axis_index("zh"), lax.axis_index("c")
-    at = jnp.stack([z, y, 2 * y + z]).astype(jnp.int32)
+    at = jnp.stack([z, y, 2 * y + z, core]).astype(jnp.int32)
     flip = [(0, 1), (1, 0)]
     to_prev = [(i, i - 1) for i in range(1, tm)]
     to_next = [(i - 1, i) for i in range(1, tm)]
@@ -328,21 +374,17 @@
         return a.reshape(rows, width)
 
     x2, g2, q2, k2, v2 = (flat(a) for a in (frames_x, cotangent, queries, keys, values))
-    codes = decay_codes.reshape(rows, heads)
-    pad = ((0, 0), (0, LANES - heads))
-    codes = jnp.concatenate([jnp.pad(codes >> 8, pad), jnp.pad(codes & 255, pad)], axis=1)
-    codes = codes.astype(BF)
+    codes = jnp.transpose(decay_codes, (1, 2, 0))
     rate_wide = jnp.repeat(decay_rates, HEAD)[None]
     gain_wide = jnp.repeat(skip_gain, HEAD)[None]
 
-    msg = (rows // 2, 2 * width + 2 * LANES)
+    msg = (rows // 2, 2 * width + LANES)
     own, out = call(pack_body, [(msg, BF)] * 2, [at], [x2, g2, codes])
     got = lax.ppermute(out, "zh", flip)
 
     stats_own = call(stats_body, [((2 * heads, rows), F32)], [], [q2, k2, v2, g2])[0]
-    stats_next = lax.ppermute(stats_own, TM, to_prev)
-    q_next = lax.ppermute(after(q2, got), TM, to_prev)
-    g_next = lax.ppermute(after(g2, got), TM, to_prev)
+    qg = call(join_body, [((2 * rows + 16, width), BF)], [], [q2, g2, stats_own], [got])[0]
+    qg_next = lax.ppermute(qg, TM, to_prev)
 
     wide = (rows, width)
     state = (LANES + 16, width)
@@ -354,6 +396,7 @@
         + [(state, BF)] * 3,
         [at],
         [own, got, bc_weight, rate_wide],
+        [qg],
     )
     m1, m2, m3 = (
         lax.ppermute(m, "y", [(i, (i + s) % ny) for i in range(ny)])
@@ -366,19 +409,17 @@
         [xs, gs, bc, sums, sums_t],
     )
     order = 1.0 / (rows * tm * lax.axis_size(("zl", "x", "c")))
-    keep, give, partial = call(
+    keep, give, mine, yours = call(
         lambda at_ref, *refs: carry_body(at_ref, order, *refs),
-        [((rows // 2, width), BF)] * 2 + [((width // 8, 8, 2 * LANES), F32)],
+        [((rows // 2, width), BF)] * 2 + [((width // 16, 8, 2 * LANES), F32)] * 2,
         [at],
         [m1, m2, m3, rate_wide, gain_wide, bc_weight, gs, bc, scaled_x, scaled_g, leave, gx, gb, gc, x_t],
+        [qg_next],
     )
     gx_far = lax.ppermute(give, "zh", flip)
 
-    partial = partial.reshape(ny, nz, nx, 2, 8, 2 * LANES)
-    mine = lax.dynamic_index_in_dim(partial, core, 3, False)
-    yours = lax.dynamic_index_in_dim(partial, 1 - core, 3, False)
-    chip = mine + lax.ppermute(yours, "c", flip)
-    chip = jnp.swapaxes(chip, 1, 2).reshape(ny * nx, nz * 8, 2 * LANES).astype(BF)
+    chip = (mine + lax.ppermute(yours, "c", flip)).astype(BF)
+    chip = chip.reshape(ny * nx, nz * 8, 2 * LANES)
     spread = lax.all_to_all(chip, ("y", "x"), 0, 0, tiled=True)
     plane = jnp.sum(spread.astype(F32), axis=0).astype(BF).reshape(nz, 8, 2 * LANES)
     spread = lax.all_to_all(plane, ("zh", "zl"), 0, 0, tiled=True)
@@ -388,7 +429,8 @@
         cross_body,
         [((2 * heads, rows), F32), (wide, BF), (wide, F32), (wide, F32)],
         [],
-        [q_next, g_next, stats_next, k2, v2],
+        [qg_next, k2, v2],
+        [chip],
     )
     stats_prev = lax.ppermute(stats_far, TM, to_next)
     gq_prev = lax.ppermute(gq_out, TM, to_next)

time: 214 us -> 185 us (0.86)
  waiting for transfers between devices: 73.2 us -> 30.1 us
  starting transfers between devices: 77 us -> 93.1 us
  Pallas kernels: 24.8 us -> 39.6 us
  local copies, waits for them, and re-layouts: 30.2 us -> 16.3 us
    ppermute x4 -> x2, waiting for transfers between devices: 25.5 us -> 0.01 us  [the longest x1 0.01 us: local(): qg_next = lax.ppermute(qg, TM, to_prev)]
    ppermute x1, starting transfers between devices: 31.4 us -> 6.13 us  [local(): stats_prev = lax.ppermute(stats_far, TM, to_next)]
    ppermute x3, starting transfers between devices: 5.79 us -> 20.7 us  [local(): lax.ppermute(m, 'y', [(i, (i + s) % ny) for i in range(ny)])]
    pallas_call x7 -> x8, Pallas kernels: 24.8 us -> 39.6 us  [call(): pl.pallas_call(run, out_shape=[jax.ShapeDtypeStruct(s, d) for s, d in out...]
    ppermute x1, starting transfers between devices: 5.68 us -> 19.7 us  [local(): gx_far = lax.ppermute(give, 'zh', flip)]
    all_to_all x1, starting transfers between devices: 13.4 us -> 26 us  [local(): spread = lax.all_to_all(plane, ('zh', 'zl'), 0, 0, tiled=True)]
    unnamed x55 -> x31, local copies, waits for them, and re-layouts: 15.9 us -> 4.2 us
    ppermute x3, waiting for transfers between devices: 19.7 us -> 10.5 us  [local(): lax.ppermute(m, 'y', [(i, (i + s) % ny) for i in range(ny)])]
  transfers between devices with their start and end apart: 13 -> 11, of which waited for: 7 -> 5; matrix products, arithmetic and copies ran while one was open for 6% -> 7% of each run, Pallas kernels for 6% -> 15%
where the time goes in v2:
time: 185 us; the launch traced here: 184 us
  starting transfers between devices  93.1 us (50%)
  Pallas kernels  39.6 us (21%)
  waiting for transfers between devices  30.1 us (16%)
  local copies, waits for them, and re-layouts  16.3 us (9%)
  other arithmetic  4.23 us (2%)
    pallas_call x8, Pallas kernels, call(): pl.pallas_call(run, out_shape=[jax.ShapeDtypeStruct(s, d) for s, d in out...  39.6 us
    all_to_all x1, starting transfers between devices, local(): spread = lax.all_to_all(plane, ('zh', 'zl'), 0, 0, tiled=True)  26 us
    ppermute x3, starting transfers between devices, local(): lax.ppermute(m, 'y', [(i, (i + s) % ny) for i in range(ny)])  20.7 us
    ppermute x1, starting transfers between devices, local(): gx_far = lax.ppermute(give, 'zh', flip)  19.7 us
    ppermute x3, waiting for transfers between devices, local(): lax.ppermute(m, 'y', [(i, (i + s) % ny) for i in range(ny)])  10.5 us
    ppermute x1, waiting for transfers between devices, local(): got = lax.ppermute(out, 'zh', flip)  8.52 us
    all_to_all x1, starting transfers between devices, local(): spread = lax.all_to_all(chip, ('y', 'x'), 0, 0, tiled=True)  7.52 us
    ppermute x1, starting transfers between devices, local(): got = lax.ppermute(out, 'zh', flip)  7.19 us
  transfers between devices with their start and end apart: 11, of which 5 were waited for; matrix products, arithmetic and copies ran while one was open for 7% of the time, Pallas kernels for 15%

profile of v2, /device:TPU:2, one launch (start us, length us, event | category | flops | bytes accessed | tf_op | source)
XLA Modules:
  0.0 184.1 jit_solution(13256795799185891266)
XLA Ops:
  0.6 2.1 %reshape.41.refs_2_.refs_3_.refs_1_.refs_4_ = bf16[128,2048]{1,0:T(8,128)(2,1)} reshape(bf16[64,2,2048]{2,1,0:T(2,128)(2,1)} %param.17) | data formatting | bytes 1048576 | tf_op jit(solution)/shard_map/reshape | solution.py:374
  2.7 1.0 reshape.40.refs_1_
  3.7 0.6 pad_add_fusion.refs_0_
  4.3 2.5 %shard_map.128 = (bf16[64,4224]{1,0:T(8,128)(2,1)}, bf16[64,4224]{1,0:T(8,128)(2,1)}) custom-call(s32[4]{0:T(128)} %pad_add_fusion.refs_0_, bf16[128,2048]{1,0:T(8,128)(2,1)} %reshape.40.refs_1_, bf16[128,2048]{1,0:T(8,128)(2,1)} %reshape.41.refs_2_.refs_3_.refs_1_.refs_4_, s32[2,32,64]{2,1,0:T(8,128)} %bitcast.11), custom_call_target="tpu_custom_call" | custom-call | flops 1 | bytes 1 | tf_op jit(solution)/shard_map/pallas_call | solution.py:30
  6.9 7.2 %collective-permute-start = (bf16[64,4224]{1,0:T(8,128)(2,1)}, bf16[64,4224]{1,0:T(8,128)(2,1)S(1)}, u32[]{:S(2)}, u32[]{:S(2)}) collective-permute-start(bf16[64,4224]{1,0:T(8,128)(2,1)} %get-tuple-element.34), channel_id=1, source_target_pairs={{0,32},{32,0},{1,33},{33,1},{2,34},{34,2},{3,35},{35,3},{4,36},{36... | collective-permute-start | bytes 1622024 | tf_op jit(solution)/shard_map/ppermute | solution.py:383
  14.0 1.0 reshape.42.refs_0_.refs_1_
  15.0 1.0 reshape.43.refs_1_.refs_2_
  16.0 1.0 reshape.44.refs_2_.refs_3_
  17.0 3.2 %shard_map.129.refs_2_.refs_5_ = f32[64,128]{1,0:T(8,128)} custom-call(bf16[128,2048]{1,0:T(8,128)(2,1)} %reshape.42.refs_0_.refs_1_, bf16[128,2048]{1,0:T(8,128)(2,1)} %reshape.43.refs_1_.refs_2_, bf16[128,2048]{1,0:T(8,128)(2,1)} %reshape.44.refs_2_.refs_3_, bf16[128,2048]{1,0:T(8,128)(2,1)} %reshape.41.refs_2_.refs_3_.refs_1_.refs_4_), custom_call_target="tpu_custom_call" | custom-call | flops 1 | bytes 1 | tf_op jit(solution)/shard_map/pallas_call | solution.py:30
  20.2 8.5 %collective-permute-done.refs_3_.refs_2_ = bf16[64,4224]{1,0:T(8,128)(2,1)S(1)} collective-permute-done((bf16[64,4224]{1,0:T(8,128)(2,1)}, bf16[64,4224]{1,0:T(8,128)(2,1)S(1)}, u32[]{:S(2)}, u32[]{:S(2)}) %collective-permute-start) | collective-permute-done | bytes 540704 | tf_op jit(solution)/shard_map/ppermute | solution.py:383
  28.8 0.8 copy-done.1
  29.6 2.3 %shard_map.130.refs_5_ = bf16[272,2048]{1,0:T(8,128)(2,1)} custom-call(bf16[128,2048]{1,0:T(8,128)(2,1)} %reshape.42.refs_0_.refs_1_, bf16[128,2048]{1,0:T(8,128)(2,1)} %reshape.41.refs_2_.refs_3_.refs_1_.refs_4_, f32[64,128]{1,0:T(8,128)} %shard_map.129.refs_2_.refs_5_, bf16[64,4224]{1,0:T(8,128)(2,1)} %copy-done.1), custom_call_target="tpu_custom_call" | custom-call | flops 1 | bytes 1 | tf_op jit(solution)/shard_map/pallas_call | solution.py:30
  31.9 1.3 collective-permute-start.4
  33.2 0.1 broadcast_in_dim.6
  33.2 0.7 broadcast_in_dim_reshape.6.refs_4_
  33.9 5.9 %shard_map.131 = (bf16[128,2048]{1,0:T(8,128)(2,1)}, bf16[128,2048]{1,0:T(8,128)(2,1)}, bf16[128,256]{1,0:T(8,128)(2,1)}, f32[128,128]{1,0:T(8,128)}, f32[128,12...) custom-call(s32[4]{0:T(128)} %pad_add_fusion.refs_0_, ...), custom_call_target="tpu_custom_call" | custom-call | flops 1 | bytes 1 | tf_op jit(solution)/shard_map/pallas_call | solution.py:30
  39.8 16.5 %collective-permute-start.1 = (bf16[144,2048]{1,0:T(8,128)(2,1)}, bf16[144,2048]{1,0:T(8,128)(2,1)S(1)}, u32[]{:S(2)}, u32[]{:S(2)}) collective-permute-start(bf16[144,2048]{1,0:T(8,128)(2,1)} %get-tuple-element.35), channel_id=1, source_target_pairs={{0,64},{64,128},{128,192},{192,0},{1,65},{65,129},{129,193},{193,1... | collective-permute-start | bytes 1769480 | tf_op jit(solution)/shard_map/ppermute | solution.py:402
  56.3 3.2 %collective-permute-start.2 = (bf16[144,2048]{1,0:T(8,128)(2,1)}, bf16[144,2048]{1,0:T(8,128)(2,1)S(1)}, u32[]{:S(2)}, u32[]{:S(2)}) collective-permute-start(bf16[144,2048]{1,0:T(8,128)(2,1)} %get-tuple-element.36), channel_id=1, source_target_pairs={{0,128},{64,192},{128,0},{192,64},{1,129},{65,193},{129,1},{193,65... | collective-permute-start | bytes 1769480 | tf_op jit(solution)/shard_map/ppermute | solution.py:402
  59.5 1.1 collective-permute-start.3
  60.5 0.1 broadcast_in_dim.7
  60.6 0.7 broadcast_in_dim_reshape.7.refs_5_
  61.3 3.7 %shard_map.132 = (f32[128,2048]{1,0:T(8,128)}, f32[128,128]{1,0:T(8,128)}, f32[128,128]{1,0:T(8,128)}, bf16[2048,128]{1,0:T(8,128)(2,1)}) custom-call(f32[32]{0:T(128)} %refs_0_.1, bf16[128,2048]{1,0:T(8,128)(2,1)} %get-tuple-element.43.refs_1_, bf16[128,2048]{1,0:T(8,128)(2,1)} %get-tuple-element.38.refs_2_.refs_7_, ...), custom_call_target="tpu_custom_call" | custom-call | flops 1 | bytes 1 | tf_op jit(solution)/shard_map/pallas_call | solution.py:30
  65.0 4.2 %collective-permute-done.1.refs_1_ = bf16[144,2048]{1,0:T(8,128)(2,1)S(1)} collective-permute-done((bf16[144,2048]{1,0:T(8,128)(2,1)}, bf16[144,2048]{1,0:T(8,128)(2,1)S(1)}, u32[]{:S(2)}, u32[]{:S(2)}) %collective-permute-start.1) | collective-permute-done | bytes 589856 | tf_op jit(solution)/shard_map/ppermute | solution.py:402
  69.2 6.3 %collective-permute-done.2.refs_2_ = bf16[144,2048]{1,0:T(8,128)(2,1)S(1)} collective-permute-done((bf16[144,2048]{1,0:T(8,128)(2,1)}, bf16[144,2048]{1,0:T(8,128)(2,1)S(1)}, u32[]{:S(2)}, u32[]{:S(2)}) %collective-permute-start.2) | collective-permute-done | bytes 589856 | tf_op jit(solution)/shard_map/ppermute | solution.py:402
  75.5 0.0 collective-permute-done.4.refs_16_.refs_0_
  75.5 0.8 copy-done.4
  76.3 0.2 copy-done.5
  76.5 0.4 copy-done
  76.9 6.5 %shard_map.133 = (bf16[64,2048]{1,0:T(8,128)(2,1)}, bf16[64,2048]{1,0:T(8,128)(2,1)}, f32[128,8,256]{2,1,0:T(8,128)}, f32[128,8,256]{2,1,0:T(8,128)}) custom-call(s32[4]{0:T(128)} %pad_add_fusion.refs_0_, bf16[144,2048]{1,0:T(8,128)(2,1)} %copy-done.3, bf16[144,2048]{1,0:T(8,128)(2,1)} %copy-done.4, bf16[144,2048]{1,0:T(8,128)(2,1)} %copy-done.5, ...), custom_call_target="tpu_custom_call" | custom-call | flops 1 | bytes 1 | tf_op jit(solution)/shard_map/pallas_call | solution.py:30
  83.4 19.7 %collective-permute-start.5 = (bf16[64,2048]{1,0:T(8,128)(2,1)}, bf16[64,2048]{1,0:T(8,128)(2,1)S(1)}, u32[]{:S(2)}, u32[]{:S(2)}) collective-permute-start(bf16[64,2048]{1,0:T(8,128)(2,1)} %get-tuple-element.51), channel_id=1, source_target_pairs={{0,32},{32,0},{1,33},{33,1},{2,34},{34,2},{3,35},{35,3},{4,36},{36... | collective-permute-start | bytes 786440 | tf_op jit(solution)/shard_map/ppermute | solution.py:419
  103.1 2.1 %add_convert_fusion.1 = bf16[128,8,256]{2,1,0:T(8,128)(2,1)} fusion(f32[128,8,256]{2,1,0:T(8,128)} %get-tuple-element.52, f32[128,8,256]{2,1,0:T(8,128)S(1)} %collective-permute-done.6), kind=kLoop, calls=%fused_computation.1 | loop fusion | flops 524288 | bytes 2621440 | tf_op jit(solution)/shard_map/convert_element_type | solution.py:421
  105.3 7.5 %all-to-all-start = ((bf16[16,64,256]{2,1,0:T(8,128)(2,1)}), bf16[16,64,256]{2,1,0:T(8,128)(2,1)S(1)}, u32[]{:S(2)}, u32[]{:S(2)}) async-start(bf16[16,64,256]{2,1,0:T(8,128)(2,1)} %bitcast.7.refs_3_), calls=%async_computation | async-start | bytes 1048576 | tf_op jit(solution)/shard_map/all_to_all | solution.py:423
  112.8 7.7 %shard_map.134 = (f32[64,128]{1,0:T(8,128)}, bf16[128,2048]{1,0:T(8,128)(2,1)}, f32[128,2048]{1,0:T(8,128)}, f32[128,2048]{1,0:T(8,128)}) custom-call(bf16[272,2048]{1,0:T(8,128)(2,1)} %copy-done, bf16[128,2048]{1,0:T(8,128)(2,1)} %reshape.43.refs_1_.refs_2_, bf16[128,2048]{1,0:T(8,128)(2,1)} %reshape.44.refs_2_.refs_3_, bf16[16,64,256]{2,1,0:T(8,128)(2,1)} %bitcast.7.refs_3_), custom_call_target="tpu_custom_call" | custom-call | flops 1 | bytes 1 | tf_op jit(solution)/shard_map/pallas_call | solution.py:30
  120.5 4.5 %collective-permute-start.8 = (bf16[128,2048]{1,0:T(8,128)(2,1)}, bf16[128,2048]{1,0:T(8,128)(2,1)S(1)}, u32[]{:S(2)}, u32[]{:S(2)}) collective-permute-start(bf16[128,2048]{1,0:T(8,128)(2,1)} %get-tuple-element.58), channel_id=1, source_target_pairs={{0,32},{32,64},{64,96},{96,128},{128,160},{160,192},{192,224},{1,3... | collective-permute-start | bytes 1572872 | tf_op jit(solution)/shard_map/ppermute | solution.py:436
  125.1 6.1 %collective-permute-start.7 = (f32[64,128]{1,0:T(8,128)}, f32[64,128]{1,0:T(8,128)S(1)}, u32[]{:S(2)}, u32[]{:S(2)}) collective-permute-start(f32[64,128]{1,0:T(8,128)} %get-tuple-element.54), channel_id=1, source_target_pairs={{0,32},{32,64},{64,96},{96,128},{128,160},{160,192},{192,224},{1,3... | collective-permute-start | bytes 98312 | tf_op jit(solution)/shard_map/ppermute | solution.py:435
  131.3 0.1 pad_maximum_fusion
  131.3 1.3 copy.15
  132.7 4.3 %collective-permute-done.7.refs_6_ = f32[64,128]{1,0:T(8,128)S(1)} collective-permute-done((f32[64,128]{1,0:T(8,128)}, f32[64,128]{1,0:T(8,128)S(1)}, u32[]{:S(2)}, u32[]{:S(2)}) %collective-permute-start.7) | collective-permute-done | bytes 32800 | tf_op jit(solution)/shard_map/ppermute | solution.py:435
  137.0 0.6 copy-done.12
  137.6 7.8 %shard_map.135 = (f32[128,2048]{1,0:T(8,128)}, bf16[128,2048]{1,0:T(8,128)(2,1)}, bf16[128,2048]{1,0:T(8,128)(2,1)}) custom-call(s32[4]{0:T(128)} %pad_add_fusion.refs_0_, bf16[128,2048]{1,0:T(8,128)(2,1)} %reshape.42.refs_0_.refs_1_, bf16[128,2048]{1,0:T(8,128)(2,1)} %reshape.43.refs_1_.refs_2_, bf16[128,2048]{1,0:T(8,128)(2,1)} %reshape.44.refs_2_.refs_3_, ...), custom_call_target="tpu_custom_call" | custom-call | flops 1 | bytes 1 | tf_op jit(solution)/shard_map/pallas_call | solution.py:30
  145.4 2.3 %reshape.47 = bf16[64,2,2048]{2,1,0:T(2,128)(2,1)} reshape(bf16[128,2048]{1,0:T(8,128)(2,1)} %get-tuple-element.59) | data formatting | bytes 1048576 | tf_op jit(solution)/shard_map/reshape | solution.py:448
  147.6 1.1 reshape.48
  148.8 0.7 reduce_sum.21
  149.5 26.0 %all-to-all-start.1 = ((bf16[8,8,256]{2,1,0:T(8,128)(2,1)}), bf16[8,8,256]{2,1,0:T(8,128)(2,1)S(1)}, u32[]{:S(2)}, u32[]{:S(2)}) async-start(bf16[8,8,256]{2,1,0:T(8,128)(2,1)} %bitcast.8), calls=%async_computation.1 | async-start | bytes 65536 | tf_op jit(solution)/shard_map/all_to_all | solution.py:425
  175.5 0.1 add_convert_fusion
  175.6 1.1 reshape.46
  176.7 6.8 %all-to-all-done.1 = bf16[8,8,256]{2,1,0:T(8,128)(2,1)S(1)} async-done(((bf16[8,8,256]{2,1,0:T(8,128)(2,1)}), bf16[8,8,256]{2,1,0:T(8,128)(2,1)S(1)}, u32[]{:S(2)}, u32[]{:S(2)}) %all-to-all-start.1) | async-done | bytes 32800 | tf_op jit(solution)/shard_map/all_to_all | solution.py:425
  183.5 0.6 convert_reduce_fusion
  (32 shorter events, 0.1 us)
Async XLA Ops:
  0.6 2.1 %copy-start.6 = (bf16[64,2,2048]{2,1,0:T(2,128)(2,1)S(1)}, bf16[64,2,2048]{2,1,0:T(2,128)(2,1)}, u32[]{:S(2)}) copy-start(bf16[64,2,2048]{2,1,0:T(2,128)(2,1)} %param.9) | copy-start | bytes 1572868
  2.7 11.3 %copy-start.7 = (bf16[64,2,2048]{2,1,0:T(2,128)(2,1)S(1)}, bf16[64,2,2048]{2,1,0:T(2,128)(2,1)}, u32[]{:S(2)}) copy-start(bf16[64,2,2048]{2,1,0:T(2,128)(2,1)} %param.14) | copy-start | bytes 1572868
  3.7 11.3 %copy-start.8 = (bf16[64,2,2048]{2,1,0:T(2,128)(2,1)S(1)}, bf16[64,2,2048]{2,1,0:T(2,128)(2,1)}, u32[]{:S(2)}) copy-start(bf16[64,2,2048]{2,1,0:T(2,128)(2,1)} %param.15) | copy-start | bytes 1572868
  6.9 9.2 %copy-start.9 = (bf16[64,2,2048]{2,1,0:T(2,128)(2,1)S(1)}, bf16[64,2,2048]{2,1,0:T(2,128)(2,1)}, u32[]{:S(2)}) copy-start(bf16[64,2,2048]{2,1,0:T(2,128)(2,1)} %param.16) | copy-start | bytes 1572868
  6.9 21.9 %collective-permute-start = (bf16[64,4224]{1,0:T(8,128)(2,1)}, bf16[64,4224]{1,0:T(8,128)(2,1)S(1)}, u32[]{:S(2)}, u32[]{:S(2)}) collective-permute-start(bf16[64,4224]{1,0:T(8,128)(2,1)} %get-tuple-element.34), channel_id=1, source_target_pairs={{0,32},{32,0},{1,33},{33,1},{2,34},{34,2},{3,35},{35,3},{4,36},{36... | collective-permute-start | bytes 1622024 | tf_op jit(solution)/shard_map/ppermute | solution.py:383
  20.2 12.9 %copy-start.13 = (f32[32]{0:T(128)S(1)}, f32[32]{0:T(128)}, u32[]{:S(2)}) copy-start(f32[32]{0:T(128)} %refs_0_.1) | copy-start | bytes 388
  28.8 0.8 copy-start.1
  31.9 43.6 %collective-permute-start.4 = (bf16[272,2048]{1,0:T(8,128)(2,1)}, bf16[272,2048]{1,0:T(8,128)(2,1)S(1)}, u32[]{:S(2)}, u32[]{:S(2)}) collective-permute-start(bf16[272,2048]{1,0:T(8,128)(2,1)} %shard_map.130.refs_5_), channel_id=1, source_target_pairs={{32,0},{64,32},{96,64},{128,96},{160,128},{192,160},{224,192},{33,... | collective-permute-start | bytes 3342344 | tf_op jit(solution)/shard_map/ppermute | solution.py:387
  33.9 26.6 %copy-start.14 = (f32[32]{0:T(128)S(1)}, f32[32]{0:T(128)}, u32[]{:S(2)}) copy-start(f32[32]{0:T(128)} %param.13) | copy-start | bytes 388
  39.8 29.4 %collective-permute-start.1 = (bf16[144,2048]{1,0:T(8,128)(2,1)}, bf16[144,2048]{1,0:T(8,128)(2,1)S(1)}, u32[]{:S(2)}, u32[]{:S(2)}) collective-permute-start(bf16[144,2048]{1,0:T(8,128)(2,1)} %get-tuple-element.35), channel_id=1, source_target_pairs={{0,64},{64,128},{128,192},{192,0},{1,65},{65,129},{129,193},{193,1... | collective-permute-start | bytes 1769480 | tf_op jit(solution)/shard_map/ppermute | solution.py:402
  56.3 19.2 %collective-permute-start.2 = (bf16[144,2048]{1,0:T(8,128)(2,1)}, bf16[144,2048]{1,0:T(8,128)(2,1)S(1)}, u32[]{:S(2)}, u32[]{:S(2)}) collective-permute-start(bf16[144,2048]{1,0:T(8,128)(2,1)} %get-tuple-element.36), channel_id=1, source_target_pairs={{0,128},{64,192},{128,0},{192,64},{1,129},{65,193},{129,1},{193,65... | collective-permute-start | bytes 1769480 | tf_op jit(solution)/shard_map/ppermute | solution.py:402
  59.5 16.0 %collective-permute-start.3 = (bf16[144,2048]{1,0:T(8,128)(2,1)}, bf16[144,2048]{1,0:T(8,128)(2,1)S(1)}, u32[]{:S(2)}, u32[]{:S(2)}) collective-permute-start(bf16[144,2048]{1,0:T(8,128)(2,1)} %get-tuple-element.37), channel_id=1, source_target_pairs={{0,192},{64,0},{128,64},{192,128},{1,193},{65,1},{129,65},{193,129... | collective-permute-start | bytes 1769480 | tf_op jit(solution)/shard_map/ppermute | solution.py:402
  69.2 6.4 %copy-start.3 = (bf16[144,2048]{1,0:T(8,128)(2,1)}, bf16[144,2048]{1,0:T(8,128)(2,1)S(1)}, u32[]{:S(2)}) copy-start(bf16[144,2048]{1,0:T(8,128)(2,1)S(1)} %collective-permute-done.1.refs_1_) | copy-start | bytes 1769476
  75.5 0.8 copy-start.4
  75.5 1.0 copy-start.5
  75.5 1.4 copy-start
  83.4 19.7 %collective-permute-start.6 = (f32[128,8,256]{2,1,0:T(8,128)}, f32[128,8,256]{2,1,0:T(8,128)S(1)}, u32[]{:S(2)}, u32[]{:S(2)}) collective-permute-start(f32[128,8,256]{2,1,0:T(8,128)} %get-tuple-element.53), channel_id=1, source_target_pairs={{0,1},{1,0},{2,3},{3,2},{4,5},{5,4},{6,7},{7,6},{8,9},{9,8},{10,11... | collective-permute-start | bytes 3145736 | tf_op jit(solution)/shard_map/ppermute | solution.py:421
  83.4 41.7 %collective-permute-start.5 = (bf16[64,2048]{1,0:T(8,128)(2,1)}, bf16[64,2048]{1,0:T(8,128)(2,1)S(1)}, u32[]{:S(2)}, u32[]{:S(2)}) collective-permute-start(bf16[64,2048]{1,0:T(8,128)(2,1)} %get-tuple-element.51), channel_id=1, source_target_pairs={{0,32},{32,0},{1,33},{33,1},{2,34},{34,2},{3,35},{35,3},{4,36},{36... | collective-permute-start | bytes 786440 | tf_op jit(solution)/shard_map/ppermute | solution.py:419
  105.3 43.5 %all-to-all-start = ((bf16[16,64,256]{2,1,0:T(8,128)(2,1)}), bf16[16,64,256]{2,1,0:T(8,128)(2,1)S(1)}, u32[]{:S(2)}, u32[]{:S(2)}) async-start(bf16[16,64,256]{2,1,0:T(8,128)(2,1)} %bitcast.7.refs_3_), calls=%async_computation | async-start | bytes 1048576 | tf_op jit(solution)/shard_map/all_to_all | solution.py:423
  112.8 12.3 %copy-start.11 = (bf16[64,2048]{1,0:T(8,128)(2,1)S(1)}, bf16[64,2048]{1,0:T(8,128)(2,1)}, u32[]{:S(2)}) copy-start(bf16[64,2048]{1,0:T(8,128)(2,1)} %get-tuple-element.50) | copy-start | bytes 786436
  120.5 54.9 %collective-permute-start.8 = (bf16[128,2048]{1,0:T(8,128)(2,1)}, bf16[128,2048]{1,0:T(8,128)(2,1)S(1)}, u32[]{:S(2)}, u32[]{:S(2)}) collective-permute-start(bf16[128,2048]{1,0:T(8,128)(2,1)} %get-tuple-element.58), channel_id=1, source_target_pairs={{0,32},{32,64},{64,96},{96,128},{128,160},{160,192},{192,224},{1,3... | collective-permute-start | bytes 1572872 | tf_op jit(solution)/shard_map/ppermute | solution.py:436
  125.1 11.8 %collective-permute-start.7 = (f32[64,128]{1,0:T(8,128)}, f32[64,128]{1,0:T(8,128)S(1)}, u32[]{:S(2)}, u32[]{:S(2)}) collective-permute-start(f32[64,128]{1,0:T(8,128)} %get-tuple-element.54), channel_id=1, source_target_pairs={{0,32},{32,64},{64,96},{96,128},{128,160},{160,192},{192,224},{1,3... | collective-permute-start | bytes 98312 | tf_op jit(solution)/shard_map/ppermute | solution.py:435
  136.9 0.6 copy-start.12
  145.3 2.3 %copy-start.10 = (bf16[128,2048]{1,0:T(8,128)(2,1)S(1)}, bf16[128,2048]{1,0:T(8,128)(2,1)}, u32[]{:S(2)}) copy-start(bf16[128,2048]{1,0:T(8,128)(2,1)} %get-tuple-element.60) | copy-start | bytes 1572868
  145.3 30.1 %copy-start.2 = (f32[128,2048]{1,0:T(8,128)S(1)}, f32[128,2048]{1,0:T(8,128)}, u32[]{:S(2)}) copy-start(f32[128,2048]{1,0:T(8,128)} %get-tuple-element.57) | copy-start | bytes 3145732
  149.5 34.0 %all-to-all-start.1 = ((bf16[8,8,256]{2,1,0:T(8,128)(2,1)}), bf16[8,8,256]{2,1,0:T(8,128)(2,1)S(1)}, u32[]{:S(2)}, u32[]{:S(2)}) async-start(bf16[8,8,256]{2,1,0:T(8,128)(2,1)} %bitcast.8), calls=%async_computation.1 | async-start | bytes 65536 | tf_op jit(solution)/shard_map/all_to_all | solution.py:425

commit v3 on v2

--- a/solution.py
+++ b/solution.py
@@ -17,26 +17,48 @@
 BF = jnp.bfloat16
 F32 = jnp.float32
 TM = ("y", "zh")
-VM = pl.BlockSpec(memory_space=pltpu.VMEM)
 SM = pl.BlockSpec(memory_space=pltpu.SMEM)
 
 
-def call(body, outs, scalars, arrays, first=()):
+GROUP = 512
+
+
+def call(body, outs, scalars, arrays, first=(), steps=1):
     used = len(scalars) + len(arrays)
 
     def run(*refs):
         body(*refs[:used], *refs[used + len(first) :])
+
+    def spec(shape):
+        if steps == 1:
+            return pl.BlockSpec(shape, lambda i: (0,) * len(shape))
+        if len(shape) == 3:
+            return pl.BlockSpec((1,) + tuple(shape[1:]), lambda i: (i, 0, 0))
+        return pl.BlockSpec((shape[0], shape[1] // steps), lambda i: (0, i))
 
     return pl.pallas_call(
         run,
         out_shape=[jax.ShapeDtypeStruct(s, d) for s, d in outs],
-        in_specs=[SM] * len(scalars) + [pl.BlockSpec(a.shape, lambda *_, n=a.ndim: (0,) * n) for a in arrays]
+        in_specs=[SM] * len(scalars)
+        + [spec(a.shape) for a in arrays]
         + [pl.BlockSpec(memory_space=pl.ANY)] * len(first),
-        out_specs=[pl.BlockSpec(s, lambda *_, n=len(s): (0,) * n) for s, d in outs],
-        grid=(1,),
+        out_specs=[spec(s) for s, d in outs],
+        grid=(steps,),
         cost_estimate=pl.CostEstimate(flops=1, bytes_accessed=1, transcendentals=0),
         compiler_params=pltpu.CompilerParams(vmem_limit_bytes=VMEM_BYTES),
     )(*scalars, *arrays, *first)
+
+
+def held_until(value, event):
+    anywhere = pl.BlockSpec(memory_space=pl.ANY)
+    return pl.pallas_call(
+        lambda *refs: None,
+        out_shape=jax.ShapeDtypeStruct(value.shape, value.dtype),
+        in_specs=[anywhere, anywhere],
+        out_specs=anywhere,
+        input_output_aliases={0: 0},
+        cost_estimate=pl.CostEstimate(flops=1, bytes_accessed=1, transcendentals=0),
+    )(value, event)
 
 
 def nn(a, b):
@@ -74,24 +96,19 @@
     rows = q.shape[0]
     out[:rows, :] = q[...]
     out[rows : 2 * rows, :] = g[...]
-    out[2 * rows :, :] = jnp.zeros((16, q.shape[1]), BF)
-    rest = stats[...]
-    groups = stats.shape[0] // 16
+    rest = stats[0]
     for piece in range(3):
         part = rest.astype(BF)
         rest = rest - part.astype(F32)
-        for k in range(groups):
-            lane = (piece * groups + k) * LANES
-            out[2 * rows :, lane : lane + LANES] = part[16 * k : 16 * k + 16]
-
-
-def joined_stats(qg, rows, groups):
-    found = []
-    for k in range(groups):
-        lanes = [(piece * groups + k) * LANES for piece in range(3)]
-        a, b, c = (qg[2 * rows :, lane : lane + LANES].astype(F32) for lane in lanes)
-        found.append(a + (b + c))
-    return jnp.concatenate(found, axis=0)
+        out[2 * rows :, piece * LANES : (piece + 1) * LANES] = part
+    out[2 * rows :, 3 * LANES :] = jnp.zeros((16, GROUP - 3 * LANES), BF)
+
+
+def joined_stats(qg, rows):
+    a, b, c = (
+        qg[2 * rows :, piece * LANES : (piece + 1) * LANES].astype(F32) for piece in range(3)
+    )
+    return a + (b + c)
 
 
 def pack_body(at, x, g, codes, own, out):
@@ -238,16 +255,14 @@
         give[...] = out[:n].astype(BF)
 
     grad = nn(x_t[...], cot) * order
+    grad = grad.reshape(4, 8, 4, 2, 8, 2 * LANES)
     for side in (0, 1):
 
         @pl.when(core == side)
         def _():
-            for index in range(mine.shape[0]):
-                xy, nz = index // 8, index % 8
-                block = (((xy // 4) * 8 + nz) * 4 + xy % 4) * 2
-                for ref, c in ((mine, side), (yours, 1 - side)):
-                    start = 8 * (block + c)
-                    ref[index] = grad[start : start + 8]
+            for x in range(4):
+                mine[:, x] = grad[:, :, x, side]
+                yours[:, x] = grad[:, :, x, 1 - side]
 
 
 def softened(k_pair, v_pair, q_pair, g_pair, seen):
@@ -283,14 +298,15 @@
 
 def stats_body(q, k, v, g, stats):
     rows, width = q.shape
-    heads = width // HEAD
     seen = seen_mask(rows, False)
+    logs, deltas = [], []
     for p in range(width // LANES):
         at = slice(p * LANES, (p + 1) * LANES)
-        for j, (s, d) in enumerate(softened(k[:, at], v[:, at], q[:, at], g[:, at], seen)):
+        for s, d in softened(k[:, at], v[:, at], q[:, at], g[:, at], seen):
             e, top, norm, delta = row_sums(s, d)
-            stats[2 * p + j : 2 * p + j + 1, :] = top + jnp.log(norm)
-            stats[heads + 2 * p + j : heads + 2 * p + j + 1, :] = delta
+            logs.append(top + jnp.log(norm))
+            deltas.append(delta)
+    stats[0] = jnp.concatenate(logs + deltas, axis=0)
 
 
 def products(ps, ds, q_pair, k_pair, g_pair):
@@ -305,8 +321,9 @@
 def cross_body(qg, k, v, stats, gq, gk, gv):
     rows, width = k.shape
     heads = width // HEAD
-    theirs = joined_stats(qg, rows, stats.shape[0] // 16)
+    theirs = joined_stats(qg, rows)
     seen = seen_mask(rows, True)
+    logs, deltas = [], []
     for p in range(width // LANES):
         at = slice(p * LANES, (p + 1) * LANES)
         q_pair, k_pair, g_pair = qg[:rows, at], k[:, at], qg[rows : 2 * rows, at]
@@ -315,8 +332,8 @@
             h = 2 * p + j
             e, top, norm, delta = row_sums(s, d)
             log_here = top + jnp.log(norm)
-            stats[h : h + 1, :] = log_here
-            stats[heads + h : heads + h + 1, :] = delta
+            logs.append(log_here)
+            deltas.append(delta)
             log_norm, delta = merged(
                 log_here, delta, theirs[h : h + 1, :], theirs[heads + h : heads + h + 1, :]
             )
@@ -327,6 +344,7 @@
         gq[:, at] = a.astype(BF)
         gk[:, at] = b
         gv[:, at] = c
+    stats[0] = jnp.concatenate(logs + deltas, axis=0)
 
 
 def own_body(at_ref, q, k, v, g, ours, theirs, gk_far, gv_far, gq, gk, gv):
@@ -334,18 +352,19 @@
     heads = width // HEAD
     seen = seen_mask(rows, False)
     begins = at_ref[2] == 0
+    near, away = ours[0], theirs[0]
     for p in range(width // LANES):
         at = slice(p * LANES, (p + 1) * LANES)
         q_pair, k_pair, g_pair = q[:, at], k[:, at], g[:, at]
         ps, ds = [], []
         for j, (s, d) in enumerate(softened(k_pair, v[:, at], q_pair, g_pair, seen)):
             h = 2 * p + j
-            far = jnp.where(begins, LOW, theirs[h : h + 1, :])
+            far = jnp.where(begins, LOW, away[h : h + 1])
             log_norm, delta = merged(
-                ours[h : h + 1, :],
-                ours[heads + h : heads + h + 1, :],
+                near[h : h + 1],
+                near[heads + h : heads + h + 1],
                 far,
-                theirs[heads + h : heads + h + 1, :],
+                away[heads + h : heads + h + 1],
             )
             prob = jnp.exp(s - log_norm)
             ps.append(prob.astype(BF))
@@ -382,8 +401,11 @@
     own, out = call(pack_body, [(msg, BF)] * 2, [at], [x2, g2, codes])
     got = lax.ppermute(out, "zh", flip)
 
-    stats_own = call(stats_body, [((2 * heads, rows), F32)], [], [q2, k2, v2, g2])[0]
-    qg = call(join_body, [((2 * rows + 16, width), BF)], [], [q2, g2, stats_own], [got])[0]
+    steps = width // GROUP
+    stats = ((steps, 2 * GROUP // HEAD, rows), F32)
+    stats_own = call(stats_body, [stats], [], [q2, k2, v2, g2], steps=steps)[0]
+    qg = call(join_body, [((2 * rows + 16, width), BF)], [], [q2, g2, stats_own], steps=steps)[0]
+    qg = held_until(qg, got)
     qg_next = lax.ppermute(qg, TM, to_prev)
 
     wide = (rows, width)
@@ -411,7 +433,7 @@
     order = 1.0 / (rows * tm * lax.axis_size(("zl", "x", "c")))
     keep, give, mine, yours = call(
         lambda at_ref, *refs: carry_body(at_ref, order, *refs),
-        [((rows // 2, width), BF)] * 2 + [((width // 16, 8, 2 * LANES), F32)] * 2,
+        [((rows // 2, width), BF)] * 2 + [((ny, nx, nz, 8, 2 * LANES), F32)] * 2,
         [at],
         [m1, m2, m3, rate_wide, gain_wide, bc_weight, gs, bc, scaled_x, scaled_g, leave, gx, gb, gc, x_t],
         [qg_next],
@@ -427,10 +449,10 @@
 
     stats_far, gq_out, gk_far, gv_far = call(
         cross_body,
-        [((2 * heads, rows), F32), (wide, BF), (wide, F32), (wide, F32)],
+        [stats, (wide, BF), (wide, F32), (wide, F32)],
         [],
         [qg_next, k2, v2],
-        [chip],
+        steps=steps,
     )
     stats_prev = lax.ppermute(stats_far, TM, to_next)
     gq_prev = lax.ppermute(gq_out, TM, to_next)
@@ -439,6 +461,8 @@
         [(wide, F32), (wide, BF), (wide, BF)],
         [at],
         [q2, k2, v2, g2, stats_own, stats_prev, gk_far, gv_far],
+        [chip],
+        steps=steps,
     )
     gq = (gq + gq_prev.astype(F32)).astype(BF)
     shape = (length, blocks, width)

time: 185 us -> 185 us (level)
  starting transfers between devices: 93.1 us -> 75.3 us
  waiting for transfers between devices: 30.1 us -> 47.5 us
    ppermute x1, waiting for transfers between devices: 0.01 us -> 29.8 us  [local(): gx_far = lax.ppermute(give, 'zh', flip)]
    all_to_all x1, starting transfers between devices: 26 us -> 9.27 us  [local(): spread = lax.all_to_all(plane, ('zh', 'zl'), 0, 0, tiled=True)]
    ppermute x1, starting transfers between devices: 6.13 us -> 21.9 us  [local(): stats_prev = lax.ppermute(stats_far, TM, to_next)]
    ppermute x1, starting transfers between devices: 19.7 us -> 7.17 us  [local(): gx_far = lax.ppermute(give, 'zh', flip)]
    ppermute x1, waiting for transfers between devices: 8.52 us -> 4.14 us  [local(): got = lax.ppermute(out, 'zh', flip)]
    ppermute x1, waiting for transfers between devices: 4.29 us -> 0.01 us  [local(): stats_prev = lax.ppermute(stats_far, TM, to_next)]
    all_to_all x1, waiting for transfers between devices: 6.76 us -> 3.2 us  [local(): spread = lax.all_to_all(plane, ('zh', 'zl'), 0, 0, tiled=True)]
    ppermute x1, starting transfers between devices: 4.51 us -> 1.95 us  [local(): gq_prev = lax.ppermute(gq_out, TM, to_next)]
  transfers between devices with their start and end apart: 11 -> 11, of which waited for: 5 -> 5; matrix products, arithmetic and copies ran while one was open for 7% -> 7% of each run, Pallas kernels for 15% -> 17%
where the time goes in v3:
time: 185 us; the launch traced here: 184 us
  starting transfers between devices  75.3 us (41%)
  waiting for transfers between devices  47.5 us (26%)
  Pallas kernels  40.9 us (22%)
  local copies, waits for them, and re-layouts  15.2 us (8%)
  other arithmetic  4.28 us (2%)
    pallas_call x8, Pallas kernels, call(): pl.pallas_call(run, out_shape=[jax.ShapeDtypeStruct(s, d) for s, d in out...  40.9 us
    ppermute x1, waiting for transfers between devices, local(): gx_far = lax.ppermute(give, 'zh', flip)  29.8 us
    ppermute x1, starting transfers between devices, local(): stats_prev = lax.ppermute(stats_far, TM, to_next)  21.9 us
    ppermute x3, starting transfers between devices, local(): lax.ppermute(m, 'y', [(i, (i + s) % ny) for i in range(ny)])  20.8 us
    ppermute x3, waiting for transfers between devices, local(): lax.ppermute(m, 'y', [(i, (i + s) % ny) for i in range(ny)])  10.4 us
    all_to_all x1, starting transfers between devices, local(): spread = lax.all_to_all(plane, ('zh', 'zl'), 0, 0, tiled=True)  9.27 us
    ppermute x1, starting transfers between devices, local(): got = lax.ppermute(out, 'zh', flip)  7.2 us
    ppermute x1, starting transfers between devices, local(): gx_far = lax.ppermute(give, 'zh', flip)  7.17 us
  transfers between devices with their start and end apart: 11, of which 5 were waited for; matrix products, arithmetic and copies ran while one was open for 7% of the time, Pallas kernels for 17%

profile of v3, /device:TPU:2, one launch (start us, length us, event | category | flops | bytes accessed | tf_op | source)
XLA Modules:
  0.0 184.0 jit_solution(16638407702264126024)
XLA Ops:
  0.6 2.1 %reshape.41.refs_2_.refs_3_.refs_1_.refs_4_ = bf16[128,2048]{1,0:T(8,128)(2,1)} reshape(bf16[64,2,2048]{2,1,0:T(2,128)(2,1)} %param.17) | data formatting | bytes 1048576 | tf_op jit(solution)/shard_map/reshape | solution.py:393
  2.7 1.0 reshape.40.refs_1_
  3.7 0.6 pad_add_fusion.refs_0_
  4.3 2.5 %shard_map.128 = (bf16[64,4224]{1,0:T(8,128)(2,1)}, bf16[64,4224]{1,0:T(8,128)(2,1)}) custom-call(s32[4]{0:T(128)} %pad_add_fusion.refs_0_, bf16[128,2048]{1,0:T(8,128)(2,1)} %reshape.40.refs_1_, bf16[128,2048]{1,0:T(8,128)(2,1)} %reshape.41.refs_2_.refs_3_.refs_1_.refs_4_, s32[2,32,64]{2,1,0:T(8,128)} %bitcast.11), custom_call_target="tpu_custom_call" | custom-call | flops 1 | bytes 1 | tf_op jit(solution)/shard_map/pallas_call | solution.py:39
  6.8 7.2 %collective-permute-start = (bf16[64,4224]{1,0:T(8,128)(2,1)}, bf16[64,4224]{1,0:T(8,128)(2,1)S(1)}, u32[]{:S(2)}, u32[]{:S(2)}) collective-permute-start(bf16[64,4224]{1,0:T(8,128)(2,1)} %get-tuple-element.34), channel_id=1, source_target_pairs={{0,32},{32,0},{1,33},{33,1},{2,34},{34,2},{3,35},{35,3},{4,36},{36... | collective-permute-start | bytes 1622024 | tf_op jit(solution)/shard_map/ppermute | solution.py:402
  14.0 1.0 reshape.42.refs_0_.refs_1_
  15.0 1.0 reshape.43.refs_1_.refs_2_
  16.0 1.0 reshape.44.refs_2_.refs_3_
  17.0 4.1 %shard_map.129.refs_2_.refs_5_ = f32[4,16,128]{2,1,0:T(8,128)} custom-call(bf16[128,2048]{1,0:T(8,128)(2,1)} %reshape.42.refs_0_.refs_1_, bf16[128,2048]{1,0:T(8,128)(2,1)} %reshape.43.refs_1_.refs_2_, bf16[128,2048]{1,0:T(8,128)(2,1)} %reshape.44.refs_2_.refs_3_, bf16[128,2048]{1,0:T(8,128)(2,1)} %reshape.41.refs_2_.refs_3_.refs_1_.refs_4_), custom_call_target="tpu_custom_call" | custom-call | flops 1 | bytes 1 | tf_op jit(solution)/shard_map/pallas_call | solution.py:39
  21.1 3.5 %shard_map.130.refs_0_ = bf16[272,2048]{1,0:T(8,128)(2,1)} custom-call(bf16[128,2048]{1,0:T(8,128)(2,1)} %reshape.42.refs_0_.refs_1_, bf16[128,2048]{1,0:T(8,128)(2,1)} %reshape.41.refs_2_.refs_3_.refs_1_.refs_4_, f32[4,16,128]{2,1,0:T(8,128)} %shard_map.129.refs_2_.refs_5_), custom_call_target="tpu_custom_call" | custom-call | flops 1 | bytes 1 | tf_op jit(solution)/shard_map/pallas_call | solution.py:39
  24.6 4.1 %collective-permute-done.refs_1_.refs_2_ = bf16[64,4224]{1,0:T(8,128)(2,1)S(1)} collective-permute-done((bf16[64,4224]{1,0:T(8,128)(2,1)}, bf16[64,4224]{1,0:T(8,128)(2,1)S(1)}, u32[]{:S(2)}, u32[]{:S(2)}) %collective-permute-start) | collective-permute-done | bytes 540704 | tf_op jit(solution)/shard_map/ppermute | solution.py:402
  28.7 0.8 copy-done.1
  29.6 1.3 collective-permute-start.4
  30.8 0.1 broadcast_in_dim.6
  30.9 0.7 broadcast_in_dim_reshape.6.refs_4_
  31.6 5.9 %shard_map.132 = (bf16[128,2048]{1,0:T(8,128)(2,1)}, bf16[128,2048]{1,0:T(8,128)(2,1)}, bf16[128,256]{1,0:T(8,128)(2,1)}, f32[128,128]{1,0:T(8,128)}, f32[128,12...) custom-call(s32[4]{0:T(128)} %pad_add_fusion.refs_0_, ...), custom_call_target="tpu_custom_call" | custom-call | flops 1 | bytes 1 | tf_op jit(solution)/shard_map/pallas_call | solution.py:39
  37.5 16.5 %collective-permute-start.1 = (bf16[144,2048]{1,0:T(8,128)(2,1)}, bf16[144,2048]{1,0:T(8,128)(2,1)S(1)}, u32[]{:S(2)}, u32[]{:S(2)}) collective-permute-start(bf16[144,2048]{1,0:T(8,128)(2,1)} %get-tuple-element.35), channel_id=1, source_target_pairs={{0,64},{64,128},{128,192},{192,0},{1,65},{65,129},{129,193},{193,1... | collective-permute-start | bytes 1769480 | tf_op jit(solution)/shard_map/ppermute | solution.py:424
  54.0 3.3 %collective-permute-start.2 = (bf16[144,2048]{1,0:T(8,128)(2,1)}, bf16[144,2048]{1,0:T(8,128)(2,1)S(1)}, u32[]{:S(2)}, u32[]{:S(2)}) collective-permute-start(bf16[144,2048]{1,0:T(8,128)(2,1)} %get-tuple-element.36), channel_id=1, source_target_pairs={{0,128},{64,192},{128,0},{192,64},{1,129},{65,193},{129,1},{193,65... | collective-permute-start | bytes 1769480 | tf_op jit(solution)/shard_map/ppermute | solution.py:424
  57.2 1.1 collective-permute-start.3
  58.3 0.1 broadcast_in_dim.7
  58.4 0.7 broadcast_in_dim_reshape.7.refs_5_
  59.1 3.7 %shard_map.133 = (f32[128,2048]{1,0:T(8,128)}, f32[128,128]{1,0:T(8,128)}, f32[128,128]{1,0:T(8,128)}, bf16[2048,128]{1,0:T(8,128)(2,1)}) custom-call(f32[32]{0:T(128)} %refs_0_.1, bf16[128,2048]{1,0:T(8,128)(2,1)} %get-tuple-element.43.refs_1_, bf16[128,2048]{1,0:T(8,128)(2,1)} %get-tuple-element.38.refs_2_.refs_7_, ...), custom_call_target="tpu_custom_call" | custom-call | flops 1 | bytes 1 | tf_op jit(solution)/shard_map/pallas_call | solution.py:39
  62.8 4.0 %collective-permute-done.1.refs_1_ = bf16[144,2048]{1,0:T(8,128)(2,1)S(1)} collective-permute-done((bf16[144,2048]{1,0:T(8,128)(2,1)}, bf16[144,2048]{1,0:T(8,128)(2,1)S(1)}, u32[]{:S(2)}, u32[]{:S(2)}) %collective-permute-start.1) | collective-permute-done | bytes 589856 | tf_op jit(solution)/shard_map/ppermute | solution.py:424
  66.8 6.3 %collective-permute-done.2.refs_2_ = bf16[144,2048]{1,0:T(8,128)(2,1)S(1)} collective-permute-done((bf16[144,2048]{1,0:T(8,128)(2,1)}, bf16[144,2048]{1,0:T(8,128)(2,1)S(1)}, u32[]{:S(2)}, u32[]{:S(2)}) %collective-permute-start.2) | collective-permute-done | bytes 589856 | tf_op jit(solution)/shard_map/ppermute | solution.py:424
  73.2 0.8 copy-done.4
  74.0 0.2 copy-done.5
  74.2 0.4 copy-done
  74.6 6.5 %shard_map.134 = (bf16[64,2048]{1,0:T(8,128)(2,1)}, bf16[64,2048]{1,0:T(8,128)(2,1)}, f32[4,4,8,8,256]{4,3,2,1,0:T(8,128)}, f32[4,4,8,8,256]{4,3,2,1,0:T(8,128)}) custom-call(s32[4]{0:T(128)} %pad_add_fusion.refs_0_, bf16[144,2048]{1,0:T(8,128)(2,1)} %copy-done.3, bf16[144,2048]{1,0:T(8,128)(2,1)} %copy-done.4, bf16[144,2048]{1,0:T(8,128)(2,1)} %copy-done.5, ...), custom_call_target="tpu_custom_call" | custom-call | flops 1 | bytes 1 | tf_op jit(solution)/shard_map/pallas_call | solution.py:39
  81.1 0.1 collective-permute-start.7
  81.2 7.4 %shard_map.135 = (f32[4,16,128]{2,1,0:T(8,128)}, bf16[128,2048]{1,0:T(8,128)(2,1)}, f32[128,2048]{1,0:T(8,128)}, f32[128,2048]{1,0:T(8,128)}) custom-call(bf16[272,2048]{1,0:T(8,128)(2,1)} %copy-done, bf16[128,2048]{1,0:T(8,128)(2,1)} %reshape.43.refs_1_.refs_2_, bf16[128,2048]{1,0:T(8,128)(2,1)} %reshape.44.refs_2_.refs_3_), custom_call_target="tpu_custom_call" | custom-call | flops 1 | bytes 1 | tf_op jit(solution)/shard_map/pallas_call | solution.py:39
  88.6 21.9 %collective-permute-start.6 = (f32[4,16,128]{2,1,0:T(8,128)}, f32[4,16,128]{2,1,0:T(8,128)S(1)}, u32[]{:S(2)}, u32[]{:S(2)}) collective-permute-start(f32[4,16,128]{2,1,0:T(8,128)} %get-tuple-element.52), channel_id=1, source_target_pairs={{0,32},{32,64},{64,96},{96,128},{128,160},{160,192},{192,224},{1,3... | collective-permute-start | bytes 98312 | tf_op jit(solution)/shard_map/ppermute | solution.py:457
  110.5 2.0 %collective-permute-start.8 = (bf16[128,2048]{1,0:T(8,128)(2,1)}, bf16[128,2048]{1,0:T(8,128)(2,1)S(1)}, u32[]{:S(2)}, u32[]{:S(2)}) collective-permute-start(bf16[128,2048]{1,0:T(8,128)(2,1)} %get-tuple-element.58), channel_id=1, source_target_pairs={{0,32},{32,64},{64,96},{96,128},{128,160},{160,192},{192,224},{1,3... | collective-permute-start | bytes 1572872 | tf_op jit(solution)/shard_map/ppermute | solution.py:458
  112.5 7.2 %collective-permute-start.5 = (bf16[64,2048]{1,0:T(8,128)(2,1)}, bf16[64,2048]{1,0:T(8,128)(2,1)S(1)}, u32[]{:S(2)}, u32[]{:S(2)}) collective-permute-start(bf16[64,2048]{1,0:T(8,128)(2,1)} %get-tuple-element.51), channel_id=1, source_target_pairs={{0,32},{32,0},{1,33},{33,1},{2,34},{34,2},{3,35},{35,3},{4,36},{36... | collective-permute-start | bytes 786440 | tf_op jit(solution)/shard_map/ppermute | solution.py:441
  119.6 0.9 add_convert_fusion.1
  120.6 5.7 %all-to-all-start = ((bf16[16,64,256]{2,1,0:T(8,128)(2,1)}), bf16[16,64,256]{2,1,0:T(8,128)(2,1)S(1)}, u32[]{:S(2)}, u32[]{:S(2)}) async-start(bf16[16,64,256]{2,1,0:T(8,128)(2,1)} %bitcast.7.refs_9_), calls=%async_computation | async-start | bytes 1048576 | tf_op jit(solution)/shard_map/all_to_all | solution.py:445
  126.3 29.8 %collective-permute-done.5 = bf16[64,2048]{1,0:T(8,128)(2,1)S(1)} collective-permute-done((bf16[64,2048]{1,0:T(8,128)(2,1)}, bf16[64,2048]{1,0:T(8,128)(2,1)S(1)}, u32[]{:S(2)}, u32[]{:S(2)}) %collective-permute-start.5) | collective-permute-done | bytes 262176 | tf_op jit(solution)/shard_map/ppermute | solution.py:441
  156.1 0.1 pad_maximum_fusion
  156.2 1.3 copy.16
  157.5 0.6 copy-done.13
  158.1 7.3 %shard_map.136 = (f32[128,2048]{1,0:T(8,128)}, bf16[128,2048]{1,0:T(8,128)(2,1)}, bf16[128,2048]{1,0:T(8,128)(2,1)}) custom-call(s32[4]{0:T(128)} %pad_add_fusion.refs_0_, bf16[128,2048]{1,0:T(8,128)(2,1)} %reshape.42.refs_0_.refs_1_, bf16[128,2048]{1,0:T(8,128)(2,1)} %reshape.43.refs_1_.refs_2_, bf16[128,2048]{1,0:T(8,128)(2,1)} %reshape.44.refs_2_.refs_3_, ...), custom_call_target="tpu_custom_call" | custom-call | flops 1 | bytes 1 | tf_op jit(solution)/shard_map/pallas_call | solution.py:39
  165.4 0.7 reduce_sum.21
  166.1 9.3 %all-to-all-start.1 = ((bf16[8,8,256]{2,1,0:T(8,128)(2,1)}), bf16[8,8,256]{2,1,0:T(8,128)(2,1)S(1)}, u32[]{:S(2)}, u32[]{:S(2)}) async-start(bf16[8,8,256]{2,1,0:T(8,128)(2,1)} %bitcast.8), calls=%async_computation.1 | async-start | bytes 65536 | tf_op jit(solution)/shard_map/all_to_all | solution.py:447
  175.4 1.4 add_convert_fusion
  176.8 1.1 reshape.46
  177.9 1.1 reshape.47
  179.1 1.1 reshape.48
  180.2 3.2 %all-to-all-done.1 = bf16[8,8,256]{2,1,0:T(8,128)(2,1)S(1)} async-done(((bf16[8,8,256]{2,1,0:T(8,128)(2,1)}), bf16[8,8,256]{2,1,0:T(8,128)(2,1)S(1)}, u32[]{:S(2)}, u32[]{:S(2)}) %all-to-all-start.1) | async-done | bytes 32800 | tf_op jit(solution)/shard_map/all_to_all | solution.py:447
  183.4 0.6 convert_reduce_fusion
  (35 shorter events, 0.1 us)
Async XLA Ops:
  0.6 2.1 %copy-start.6 = (bf16[64,2,2048]{2,1,0:T(2,128)(2,1)S(1)}, bf16[64,2,2048]{2,1,0:T(2,128)(2,1)}, u32[]{:S(2)}) copy-start(bf16[64,2,2048]{2,1,0:T(2,128)(2,1)} %param.9) | copy-start | bytes 1572868
  2.7 11.3 %copy-start.7 = (bf16[64,2,2048]{2,1,0:T(2,128)(2,1)S(1)}, bf16[64,2,2048]{2,1,0:T(2,128)(2,1)}, u32[]{:S(2)}) copy-start(bf16[64,2,2048]{2,1,0:T(2,128)(2,1)} %param.14) | copy-start | bytes 1572868
  3.7 11.3 %copy-start.8 = (bf16[64,2,2048]{2,1,0:T(2,128)(2,1)S(1)}, bf16[64,2,2048]{2,1,0:T(2,128)(2,1)}, u32[]{:S(2)}) copy-start(bf16[64,2,2048]{2,1,0:T(2,128)(2,1)} %param.15) | copy-start | bytes 1572868
  6.8 9.2 %copy-start.9 = (bf16[64,2,2048]{2,1,0:T(2,128)(2,1)S(1)}, bf16[64,2,2048]{2,1,0:T(2,128)(2,1)}, u32[]{:S(2)}) copy-start(bf16[64,2,2048]{2,1,0:T(2,128)(2,1)} %param.16) | copy-start | bytes 1572868
  6.8 21.9 %collective-permute-start = (bf16[64,4224]{1,0:T(8,128)(2,1)}, bf16[64,4224]{1,0:T(8,128)(2,1)S(1)}, u32[]{:S(2)}, u32[]{:S(2)}) collective-permute-start(bf16[64,4224]{1,0:T(8,128)(2,1)} %get-tuple-element.34), channel_id=1, source_target_pairs={{0,32},{32,0},{1,33},{33,1},{2,34},{34,2},{3,35},{35,3},{4,36},{36... | collective-permute-start | bytes 1622024 | tf_op jit(solution)/shard_map/ppermute | solution.py:402
  24.6 6.3 %copy-start.14 = (f32[32]{0:T(128)S(1)}, f32[32]{0:T(128)}, u32[]{:S(2)}) copy-start(f32[32]{0:T(128)} %refs_0_.1) | copy-start | bytes 388
  28.7 0.8 copy-start.1
  29.6 43.6 %collective-permute-start.4 = (bf16[272,2048]{1,0:T(8,128)(2,1)}, bf16[272,2048]{1,0:T(8,128)(2,1)S(1)}, u32[]{:S(2)}, u32[]{:S(2)}) collective-permute-start(bf16[272,2048]{1,0:T(8,128)(2,1)} %shard_map.131.refs_5_), channel_id=1, source_target_pairs={{32,0},{64,32},{96,64},{128,96},{160,128},{192,160},{224,192},{33,... | collective-permute-start | bytes 3342344 | tf_op jit(solution)/shard_map/ppermute | solution.py:409
  31.6 26.7 %copy-start.15 = (f32[32]{0:T(128)S(1)}, f32[32]{0:T(128)}, u32[]{:S(2)}) copy-start(f32[32]{0:T(128)} %param.13) | copy-start | bytes 388
  37.5 29.3 %collective-permute-start.1 = (bf16[144,2048]{1,0:T(8,128)(2,1)}, bf16[144,2048]{1,0:T(8,128)(2,1)S(1)}, u32[]{:S(2)}, u32[]{:S(2)}) collective-permute-start(bf16[144,2048]{1,0:T(8,128)(2,1)} %get-tuple-element.35), channel_id=1, source_target_pairs={{0,64},{64,128},{128,192},{192,0},{1,65},{65,129},{129,193},{193,1... | collective-permute-start | bytes 1769480 | tf_op jit(solution)/shard_map/ppermute | solution.py:424
  54.0 19.2 %collective-permute-start.2 = (bf16[144,2048]{1,0:T(8,128)(2,1)}, bf16[144,2048]{1,0:T(8,128)(2,1)S(1)}, u32[]{:S(2)}, u32[]{:S(2)}) collective-permute-start(bf16[144,2048]{1,0:T(8,128)(2,1)} %get-tuple-element.36), channel_id=1, source_target_pairs={{0,128},{64,192},{128,0},{192,64},{1,129},{65,193},{129,1},{193,65... | collective-permute-start | bytes 1769480 | tf_op jit(solution)/shard_map/ppermute | solution.py:424
  57.2 15.9 %collective-permute-start.3 = (bf16[144,2048]{1,0:T(8,128)(2,1)}, bf16[144,2048]{1,0:T(8,128)(2,1)S(1)}, u32[]{:S(2)}, u32[]{:S(2)}) collective-permute-start(bf16[144,2048]{1,0:T(8,128)(2,1)} %get-tuple-element.37), channel_id=1, source_target_pairs={{0,192},{64,0},{128,64},{192,128},{1,193},{65,1},{129,65},{193,129... | collective-permute-start | bytes 1769480 | tf_op jit(solution)/shard_map/ppermute | solution.py:424
  66.8 6.4 %copy-start.3 = (bf16[144,2048]{1,0:T(8,128)(2,1)}, bf16[144,2048]{1,0:T(8,128)(2,1)S(1)}, u32[]{:S(2)}) copy-start(bf16[144,2048]{1,0:T(8,128)(2,1)S(1)} %collective-permute-done.1.refs_1_) | copy-start | bytes 1769476
  73.1 0.8 copy-start.4
  73.2 1.1 copy-start.5
  73.2 1.4 copy-start
  81.1 38.5 %copy-start.2 = (f32[4,4,8,8,256]{4,3,2,1,0:T(8,128)S(1)}, f32[4,4,8,8,256]{4,3,2,1,0:T(8,128)}, u32[]{:S(2)}) copy-start(f32[4,4,8,8,256]{4,3,2,1,0:T(8,128)} %get-tuple-element.55) | copy-start | bytes 3145732
  81.1 38.5 %collective-permute-start.7 = (f32[4,4,8,8,256]{4,3,2,1,0:T(8,128)}, f32[4,4,8,8,256]{4,3,2,1,0:T(8,128)S(1)}, u32[]{:S(2)}, u32[]{:S(2)}) collective-permute-start(f32[4,4,8,8,256]{4,3,2,1,0:T(8,128)} %get-tuple-element.56), channel_id=1, source_target_pairs={{0,1},{1,0},{2,3},{3,2},{4,5},{5,4},{6,7},{7,6},{8,9},{9,8},{10,11... | collective-permute-start | bytes 3145736 | tf_op jit(solution)/shard_map/ppermute | solution.py:443
  88.6 68.9 %collective-permute-start.6 = (f32[4,16,128]{2,1,0:T(8,128)}, f32[4,16,128]{2,1,0:T(8,128)S(1)}, u32[]{:S(2)}, u32[]{:S(2)}) collective-permute-start(f32[4,16,128]{2,1,0:T(8,128)} %get-tuple-element.52), channel_id=1, source_target_pairs={{0,32},{32,64},{64,96},{96,128},{128,160},{160,192},{192,224},{1,3... | collective-permute-start | bytes 98312 | tf_op jit(solution)/shard_map/ppermute | solution.py:457
  110.5 64.9 %collective-permute-start.8 = (bf16[128,2048]{1,0:T(8,128)(2,1)}, bf16[128,2048]{1,0:T(8,128)(2,1)S(1)}, u32[]{:S(2)}, u32[]{:S(2)}) collective-permute-start(bf16[128,2048]{1,0:T(8,128)(2,1)} %get-tuple-element.58), channel_id=1, source_target_pairs={{0,32},{32,64},{64,96},{96,128},{128,160},{160,192},{192,224},{1,3... | collective-permute-start | bytes 1572872 | tf_op jit(solution)/shard_map/ppermute | solution.py:458
  112.5 43.6 %collective-permute-start.5 = (bf16[64,2048]{1,0:T(8,128)(2,1)}, bf16[64,2048]{1,0:T(8,128)(2,1)S(1)}, u32[]{:S(2)}, u32[]{:S(2)}) collective-permute-start(bf16[64,2048]{1,0:T(8,128)(2,1)} %get-tuple-element.51), channel_id=1, source_target_pairs={{0,32},{32,0},{1,33},{33,1},{2,34},{34,2},{3,35},{35,3},{4,36},{36... | collective-permute-start | bytes 786440 | tf_op jit(solution)/shard_map/ppermute | solution.py:441
  120.6 35.5 %copy-start.12 = (bf16[64,2048]{1,0:T(8,128)(2,1)S(1)}, bf16[64,2048]{1,0:T(8,128)(2,1)}, u32[]{:S(2)}) copy-start(bf16[64,2048]{1,0:T(8,128)(2,1)} %get-tuple-element.50) | copy-start | bytes 786436
  120.6 44.8 %all-to-all-start = ((bf16[16,64,256]{2,1,0:T(8,128)(2,1)}), bf16[16,64,256]{2,1,0:T(8,128)(2,1)S(1)}, u32[]{:S(2)}, u32[]{:S(2)}) async-start(bf16[16,64,256]{2,1,0:T(8,128)(2,1)} %bitcast.7.refs_9_), calls=%async_computation | async-start | bytes 1048576 | tf_op jit(solution)/shard_map/all_to_all | solution.py:445
  157.5 0.6 copy-start.13
  166.1 17.3 %all-to-all-start.1 = ((bf16[8,8,256]{2,1,0:T(8,128)(2,1)}), bf16[8,8,256]{2,1,0:T(8,128)(2,1)S(1)}, u32[]{:S(2)}, u32[]{:S(2)}) async-start(bf16[8,8,256]{2,1,0:T(8,128)(2,1)} %bitcast.8), calls=%async_computation.1 | async-start | bytes 65536 | tf_op jit(solution)/shard_map/all_to_all | solution.py:447
  175.4 2.6 %copy-start.11 = (bf16[128,2048]{1,0:T(8,128)(2,1)S(1)}, bf16[128,2048]{1,0:T(8,128)(2,1)}, u32[]{:S(2)}) copy-start(bf16[128,2048]{1,0:T(8,128)(2,1)} %get-tuple-element.59) | copy-start | bytes 1572868
  176.8 2.3 %copy-start.10 = (bf16[128,2048]{1,0:T(8,128)(2,1)S(1)}, bf16[128,2048]{1,0:T(8,128)(2,1)}, u32[]{:S(2)}) copy-start(bf16[128,2048]{1,0:T(8,128)(2,1)} %get-tuple-element.60) | copy-start | bytes 1572868

commit v4 on v3

--- a/solution.py
+++ b/solution.py
@@ -49,18 +49,6 @@
     )(*scalars, *arrays, *first)
 
 
-def held_until(value, event):
-    anywhere = pl.BlockSpec(memory_space=pl.ANY)
-    return pl.pallas_call(
-        lambda *refs: None,
-        out_shape=jax.ShapeDtypeStruct(value.shape, value.dtype),
-        in_specs=[anywhere, anywhere],
-        out_specs=anywhere,
-        input_output_aliases={0: 0},
-        cost_estimate=pl.CostEstimate(flops=1, bytes_accessed=1, transcendentals=0),
-    )(value, event)
-
-
 def nn(a, b):
     return lax.dot_general(a, b, (((1,), (0,)), ((), ())), preferred_element_type=F32)
 
@@ -92,23 +80,10 @@
     return jnp.concatenate([value[:n], value[n:]], axis=1)
 
 
-def join_body(q, g, stats, out):
+def join_body(q, g, out):
     rows = q.shape[0]
     out[:rows, :] = q[...]
-    out[rows : 2 * rows, :] = g[...]
-    rest = stats[0]
-    for piece in range(3):
-        part = rest.astype(BF)
-        rest = rest - part.astype(F32)
-        out[2 * rows :, piece * LANES : (piece + 1) * LANES] = part
-    out[2 * rows :, 3 * LANES :] = jnp.zeros((16, GROUP - 3 * LANES), BF)
-
-
-def joined_stats(qg, rows):
-    a, b, c = (
-        qg[2 * rows :, piece * LANES : (piece + 1) * LANES].astype(F32) for piece in range(3)
-    )
-    return a + (b + c)
+    out[rows:, :] = g[...]
 
 
 def pack_body(at, x, g, codes, own, out):
@@ -265,6 +240,14 @@
                 yours[:, x] = grad[:, :, x, 1 - side]
 
 
+def unpack_body(at, keep, far, out):
+    z = at[0]
+    n = keep.shape[0]
+    row, col = iota((2 * n, n), 0), iota((2 * n, n), 1)
+    ours, theirs = one(row == 2 * col + z), one(row == 2 * col + 1 - z)
+    out[...] = (nn(ours, keep[...]) + nn(theirs, far[...])).astype(BF)
+
+
 def softened(k_pair, v_pair, q_pair, g_pair, seen):
     rows = q_pair.shape[0]
     score = nt(halves(k_pair, SCALE), q_pair)
@@ -318,15 +301,15 @@
     return grad_q, grad_k, grad_v
 
 
-def cross_body(qg, k, v, stats, gq, gk, gv):
+def cross_body(qg, before, k, v, gq, gk, gv):
     rows, width = k.shape
     heads = width // HEAD
-    theirs = joined_stats(qg, rows)
+    theirs = before[0]
     seen = seen_mask(rows, True)
     logs, deltas = [], []
     for p in range(width // LANES):
         at = slice(p * LANES, (p + 1) * LANES)
-        q_pair, k_pair, g_pair = qg[:rows, at], k[:, at], qg[rows : 2 * rows, at]
+        q_pair, k_pair, g_pair = qg[:rows, at], k[:, at], qg[rows:, at]
         ps, ds = [], []
         for j, (s, d) in enumerate(softened(k_pair, v[:, at], q_pair, g_pair, seen)):
             h = 2 * p + j
@@ -341,18 +324,25 @@
             ps.append(prob.astype(BF))
             ds.append((prob * (d - delta)).astype(BF))
         a, b, c = products(ps, ds, q_pair, k_pair, g_pair)
-        gq[:, at] = a.astype(BF)
+        gq[:rows, at] = a.astype(BF)
         gk[:, at] = b
         gv[:, at] = c
-    stats[0] = jnp.concatenate(logs + deltas, axis=0)
-
-
-def own_body(at_ref, q, k, v, g, ours, theirs, gk_far, gv_far, gq, gk, gv):
+    rest = jnp.concatenate(logs + deltas, axis=0)
+    for piece in range(3):
+        part = rest.astype(BF)
+        rest = rest - part.astype(F32)
+        gq[rows:, piece * LANES : (piece + 1) * LANES] = part
+    gq[rows:, 3 * LANES :] = jnp.zeros((16, GROUP - 3 * LANES), BF)
+
+
+def own_body(at_ref, q, k, v, g, ours, gq_far, gk_far, gv_far, gq, gk, gv):
     rows, width = q.shape
     heads = width // HEAD
     seen = seen_mask(rows, False)
     begins = at_ref[2] == 0
-    near, away = ours[0], theirs[0]
+    near = ours[0]
+    pieces = (gq_far[rows:, i * LANES : (i + 1) * LANES].astype(F32) for i in range(3))
+    away = functools.reduce(lambda a, b: a + b, pieces)
     for p in range(width // LANES):
         at = slice(p * LANES, (p + 1) * LANES)
         q_pair, k_pair, g_pair = q[:, at], k[:, at], g[:, at]
@@ -370,7 +360,7 @@
             ps.append(prob.astype(BF))
             ds.append((prob * (d - delta)).astype(BF))
         a, b, c = products(ps, ds, q_pair, k_pair, g_pair)
-        gq[:, at] = a
+        gq[:, at] = (a + gq_far[:rows, at].astype(F32)).astype(BF)
         gk[:, at] = (b + gk_far[:, at]).astype(BF)
         gv[:, at] = (c + gv_far[:, at]).astype(BF)
 
@@ -404,8 +394,8 @@
     steps = width // GROUP
     stats = ((steps, 2 * GROUP // HEAD, rows), F32)
     stats_own = call(stats_body, [stats], [], [q2, k2, v2, g2], steps=steps)[0]
-    qg = call(join_body, [((2 * rows + 16, width), BF)], [], [q2, g2, stats_own], steps=steps)[0]
-    qg = held_until(qg, got)
+    stats_next = lax.ppermute(stats_own, TM, to_prev)
+    qg = call(join_body, [((2 * rows, width), BF)], [], [q2, g2])[0]
     qg_next = lax.ppermute(qg, TM, to_prev)
 
     wide = (rows, width)
@@ -418,7 +408,7 @@
         + [(state, BF)] * 3,
         [at],
         [own, got, bc_weight, rate_wide],
-        [qg],
+        [stats_own],
     )
     m1, m2, m3 = (
         lax.ppermute(m, "y", [(i, (i + s) % ny) for i in range(ny)])
@@ -429,6 +419,7 @@
         [(wide, F32), (square, F32), (square, F32), ((width, rows), BF)],
         [decay_rates],
         [xs, gs, bc, sums, sums_t],
+        [stats_next],
     )
     order = 1.0 / (rows * tm * lax.axis_size(("zl", "x", "c")))
     keep, give, mine, yours = call(
@@ -447,29 +438,25 @@
     spread = lax.all_to_all(plane, ("zh", "zl"), 0, 0, tiled=True)
     grad_bc = jnp.sum(spread.astype(F32), axis=0)
 
-    stats_far, gq_out, gk_far, gv_far = call(
+    gq_out, gk_far, gv_far = call(
         cross_body,
-        [stats, (wide, BF), (wide, F32), (wide, F32)],
+        [((rows + 16, width), BF), (wide, F32), (wide, F32)],
         [],
-        [qg_next, k2, v2],
+        [qg_next, stats_next, k2, v2],
         steps=steps,
     )
-    stats_prev = lax.ppermute(stats_far, TM, to_next)
-    gq_prev = lax.ppermute(gq_out, TM, to_next)
+    gq_far = lax.ppermute(gq_out, TM, to_next)
     gq, gk, gv = call(
         own_body,
-        [(wide, F32), (wide, BF), (wide, BF)],
+        [(wide, BF)] * 3,
         [at],
-        [q2, k2, v2, g2, stats_own, stats_prev, gk_far, gv_far],
+        [q2, k2, v2, g2, stats_own, gq_far, gk_far, gv_far],
         [chip],
         steps=steps,
     )
-    gq = (gq + gq_prev.astype(F32)).astype(BF)
     shape = (length, blocks, width)
-    grad_x = jnp.stack(
-        [jnp.where(z == 0, keep, gx_far), jnp.where(z == 0, gx_far, keep)], axis=1
-    )
-    return grad_x, gq.reshape(shape), gk.reshape(shape), gv.reshape(shape), grad_bc
+    grad_x = call(unpack_body, [(wide, BF)], [at], [keep, gx_far], [gk])[0]
+    return grad_x.reshape(shape), gq.reshape(shape), gk.reshape(shape), gv.reshape(shape), grad_bc
 
 
 def solution(mesh):

time: 185 us -> 177 us (0.957)
  waiting for transfers between devices: 47.5 us -> 34.8 us
  starting transfers between devices: 75.3 us -> 78.1 us
    ppermute x1, waiting for transfers between devices: 29.8 us -> 0.01 us  [local(): gx_far = lax.ppermute(give, 'zh', flip)]
    ppermute x2, waiting for transfers between devices: 0.01 us -> 17.4 us  [the longest x1 17.4 us: local(): stats_next = lax.ppermute(stats_own, TM, to_prev)]
    ppermute x3, starting transfers between devices: 20.8 us -> 5.83 us  [local(): lax.ppermute(m, 'y', [(i, (i + s) % ny) for i in range(ny)])]
    all_to_all x1, starting transfers between devices: 9.27 us -> 23.6 us  [local(): spread = lax.all_to_all(plane, ('zh', 'zl'), 0, 0, tiled=True)]
    all_to_all x1, waiting for transfers between devices: 0.01 us -> 13.5 us  [local(): spread = lax.all_to_all(chip, ('y', 'x'), 0, 0, tiled=True)]
    ppermute x3, waiting for transfers between devices: 10.4 us -> 0.01 us  [local(): lax.ppermute(m, 'y', [(i, (i + s) % ny) for i in range(ny)])]
    ppermute x2, starting transfers between devices: 23.8 us -> 32.6 us  [the longest x1 31.3 us: local(): gq_far = lax.ppermute(gq_out, TM, to_next)]
    ppermute x1, starting transfers between devices: 7.17 us -> 0.1 us  [local(): gx_far = lax.ppermute(give, 'zh', flip)]
  transfers between devices with their start and end apart: 11 -> 11, of which waited for: 5 -> 3; matrix products, arithmetic and copies ran while one was open for 7% -> 6% of each run, Pallas kernels for 17% -> 19%
where the time goes in v4:
time: 177 us; the launch traced here: 175 us
  starting transfers between devices  78.1 us (44%)
  Pallas kernels  42.1 us (24%)
  waiting for transfers between devices  34.8 us (20%)
  local copies, waits for them, and re-layouts  16.6 us (9%)
  other arithmetic  2.87 us (2%)
    pallas_call x9, Pallas kernels, call(): pl.pallas_call(run, out_shape=[jax.ShapeDtypeStruct(s, d) for s, d in out...  42.1 us
    ppermute x1, starting transfers between devices, local(): gq_far = lax.ppermute(gq_out, TM, to_next)  31.3 us
    all_to_all x1, starting transfers between devices, local(): spread = lax.all_to_all(plane, ('zh', 'zl'), 0, 0, tiled=True)  23.6 us
    ppermute x1, waiting for transfers between devices, local(): stats_next = lax.ppermute(stats_own, TM, to_prev)  17.4 us
    all_to_all x1, waiting for transfers between devices, local(): spread = lax.all_to_all(chip, ('y', 'x'), 0, 0, tiled=True)  13.5 us
    all_to_all x1, starting transfers between devices, local(): spread = lax.all_to_all(chip, ('y', 'x'), 0, 0, tiled=True)  7.27 us
    ppermute x1, starting transfers between devices, local(): got = lax.ppermute(out, 'zh', flip)  7.18 us
    reshape x5, local copies, waits for them, and re-layouts, flat(): return a.reshape(rows, width)  6.05 us
  transfers between devices with their start and end apart: 11, of which 3 were waited for; matrix products, arithmetic and copies ran while one was open for 6% of the time, Pallas kernels for 19%

profile of v4, /device:TPU:2, one launch (start us, length us, event | category | flops | bytes accessed | tf_op | source)
XLA Modules:
  0.0 175.3 jit_solution(1679255200835702511)
XLA Ops:
  0.6 2.1 %reshape.44.refs_2_.refs_3_.refs_1_.refs_4_ = bf16[128,2048]{1,0:T(8,128)(2,1)} reshape(bf16[64,2,2048]{2,1,0:T(2,128)(2,1)} %param.17) | data formatting | bytes 1048576 | tf_op jit(solution)/shard_map/reshape | solution.py:383
  2.7 1.0 reshape.43.refs_1_
  3.7 0.6 pad_add_fusion.refs_0_
  4.4 2.6 %shard_map.128 = (bf16[64,4224]{1,0:T(8,128)(2,1)}, bf16[64,4224]{1,0:T(8,128)(2,1)}) custom-call(s32[4]{0:T(128)} %pad_add_fusion.refs_0_, bf16[128,2048]{1,0:T(8,128)(2,1)} %reshape.43.refs_1_, bf16[128,2048]{1,0:T(8,128)(2,1)} %reshape.44.refs_2_.refs_3_.refs_1_.refs_4_, s32[2,32,64]{2,1,0:T(8,128)} %bitcast.7), custom_call_target="tpu_custom_call" | custom-call | flops 1 | bytes 1 | tf_op jit(solution)/shard_map/pallas_call | solution.py:39
  7.0 7.2 %collective-permute-start = (bf16[64,4224]{1,0:T(8,128)(2,1)}, bf16[64,4224]{1,0:T(8,128)(2,1)S(1)}, u32[]{:S(2)}, u32[]{:S(2)}) collective-permute-start(bf16[64,4224]{1,0:T(8,128)(2,1)} %get-tuple-element.33), channel_id=1, source_target_pairs={{0,32},{32,0},{1,33},{33,1},{2,34},{34,2},{3,35},{35,3},{4,36},{36... | collective-permute-start | bytes 1622024 | tf_op jit(solution)/shard_map/ppermute | solution.py:392
  14.1 1.0 reshape.45.refs_0_.refs_1_
  15.1 2.3 %shard_map.132 = bf16[256,2048]{1,0:T(8,128)(2,1)} custom-call(bf16[128,2048]{1,0:T(8,128)(2,1)} %reshape.45.refs_0_.refs_1_, bf16[128,2048]{1,0:T(8,128)(2,1)} %reshape.44.refs_2_.refs_3_.refs_1_.refs_4_), custom_call_target="tpu_custom_call" | custom-call | flops 1 | bytes 1 | tf_op jit(solution)/shard_map/pallas_call | solution.py:39
  17.4 1.4 collective-permute-start.5
  18.9 1.0 reshape.46.refs_1_.refs_2_
  19.9 1.0 reshape.47.refs_2_.refs_3_
  20.9 4.1 %shard_map.129.refs_5_ = f32[4,16,128]{2,1,0:T(8,128)} custom-call(bf16[128,2048]{1,0:T(8,128)(2,1)} %reshape.45.refs_0_.refs_1_, bf16[128,2048]{1,0:T(8,128)(2,1)} %reshape.46.refs_1_.refs_2_, bf16[128,2048]{1,0:T(8,128)(2,1)} %reshape.47.refs_2_.refs_3_, bf16[128,2048]{1,0:T(8,128)(2,1)} %reshape.44.refs_2_.refs_3_.refs_1_.refs_4_), custom_call_target="tpu_custom_call" | custom-call | flops 1 | bytes 1 | tf_op jit(solution)/shard_map/pallas_call | solution.py:39
  25.0 0.1 broadcast_in_dim.6
  25.1 0.7 broadcast_in_dim_reshape.6.refs_4_
  25.7 4.0 %collective-permute-done.refs_2_ = bf16[64,4224]{1,0:T(8,128)(2,1)S(1)} collective-permute-done((bf16[64,4224]{1,0:T(8,128)(2,1)}, bf16[64,4224]{1,0:T(8,128)(2,1)S(1)}, u32[]{:S(2)}, u32[]{:S(2)}) %collective-permute-start) | collective-permute-done | bytes 540704 | tf_op jit(solution)/shard_map/ppermute | solution.py:392
  29.7 0.8 copy-done.8
  30.5 5.9 %shard_map.130 = (bf16[128,2048]{1,0:T(8,128)(2,1)}, bf16[128,2048]{1,0:T(8,128)(2,1)}, bf16[128,256]{1,0:T(8,128)(2,1)}, f32[128,128]{1,0:T(8,128)}, f32[128,12...) custom-call(s32[4]{0:T(128)} %pad_add_fusion.refs_0_, ...), custom_call_target="tpu_custom_call" | custom-call | flops 1 | bytes 1 | tf_op jit(solution)/shard_map/pallas_call | solution.py:39
  36.4 1.6 collective-permute-start.1
  38.0 2.9 %collective-permute-start.2 = (bf16[144,2048]{1,0:T(8,128)(2,1)}, bf16[144,2048]{1,0:T(8,128)(2,1)S(1)}, u32[]{:S(2)}, u32[]{:S(2)}) collective-permute-start(bf16[144,2048]{1,0:T(8,128)(2,1)} %get-tuple-element.35), channel_id=1, source_target_pairs={{0,128},{64,192},{128,0},{192,64},{1,129},{65,193},{129,1},{193,65... | collective-permute-start | bytes 1769480 | tf_op jit(solution)/shard_map/ppermute | solution.py:414
  40.9 1.4 collective-permute-start.3
  42.3 1.3 collective-permute-start.4
  43.6 0.1 broadcast_in_dim.7
  43.6 0.7 broadcast_in_dim_reshape.7.refs_5_
  44.3 17.4 %collective-permute-done.4.refs_6_.refs_1_ = f32[4,16,128]{2,1,0:T(8,128)S(1)} collective-permute-done((f32[4,16,128]{2,1,0:T(8,128)S(1)}, f32[4,16,128]{2,1,0:T(8,128)S(1)}, u32[]{:S(2)}, u32[]{:S(2)}) %collective-permute-start.4) | collective-permute-done | bytes 32800 | tf_op jit(solution)/shard_map/ppermute | solution.py:397
  61.7 0.6 copy-done.17
  62.3 3.8 %shard_map.131 = (f32[128,2048]{1,0:T(8,128)}, f32[128,128]{1,0:T(8,128)}, f32[128,128]{1,0:T(8,128)}, bf16[2048,128]{1,0:T(8,128)(2,1)}) custom-call(f32[32]{0:T(128)} %refs_0_.1, bf16[128,2048]{1,0:T(8,128)(2,1)} %get-tuple-element.42.refs_1_, bf16[128,2048]{1,0:T(8,128)(2,1)} %get-tuple-element.37.refs_2_.refs_7_, ...), custom_call_target="tpu_custom_call" | custom-call | flops 1 | bytes 1 | tf_op jit(solution)/shard_map/pallas_call | solution.py:39
  66.1 0.9 copy-done
  67.0 0.2 copy-done.4
  67.2 0.2 copy-done.5
  67.4 0.2 copy-done.6
  67.6 6.5 %shard_map.133 = (bf16[64,2048]{1,0:T(8,128)(2,1)}, bf16[64,2048]{1,0:T(8,128)(2,1)}, f32[4,4,8,8,256]{4,3,2,1,0:T(8,128)}, f32[4,4,8,8,256]{4,3,2,1,0:T(8,128)}) custom-call(s32[4]{0:T(128)} %pad_add_fusion.refs_0_, bf16[144,2048]{1,0:T(8,128)(2,1)} %copy-done.4, bf16[144,2048]{1,0:T(8,128)(2,1)} %copy-done.5, bf16[144,2048]{1,0:T(8,128)(2,1)} %copy-done.6, ...), custom_call_target="tpu_custom_call" | custom-call | flops 1 | bytes 1 | tf_op jit(solution)/shard_map/pallas_call | solution.py:39
  74.1 0.1 collective-permute-start.8
  74.2 7.5 %shard_map.134 = (bf16[144,2048]{1,0:T(8,128)(2,1)}, f32[128,2048]{1,0:T(8,128)}, f32[128,2048]{1,0:T(8,128)}) custom-call(bf16[256,2048]{1,0:T(8,128)(2,1)} %copy-done, f32[4,16,128]{2,1,0:T(8,128)} %copy-done.17, bf16[128,2048]{1,0:T(8,128)(2,1)} %reshape.46.refs_1_.refs_2_, bf16[128,2048]{1,0:T(8,128)(2,1)} %reshape.47.refs_2_.refs_3_), custom_call_target="tpu_custom_call" | custom-call | flops 1 | bytes 1 | tf_op jit(solution)/shard_map/pallas_call | solution.py:39
  81.6 31.3 %collective-permute-start.7 = (bf16[144,2048]{1,0:T(8,128)(2,1)}, bf16[144,2048]{1,0:T(8,128)(2,1)S(1)}, u32[]{:S(2)}, u32[]{:S(2)}) collective-permute-start(bf16[144,2048]{1,0:T(8,128)(2,1)} %get-tuple-element.51), channel_id=1, source_target_pairs={{0,32},{32,64},{64,96},{96,128},{128,160},{160,192},{192,224},{1,3... | collective-permute-start | bytes 1769480 | tf_op jit(solution)/shard_map/ppermute | solution.py:448
  113.0 0.9 add_convert_fusion
  113.9 7.3 %all-to-all-start = ((bf16[16,64,256]{2,1,0:T(8,128)(2,1)}), bf16[16,64,256]{2,1,0:T(8,128)(2,1)S(1)}, u32[]{:S(2)}, u32[]{:S(2)}) async-start(bf16[16,64,256]{2,1,0:T(8,128)(2,1)} %bitcast.5.refs_9_), calls=%async_computation | async-start | bytes 1048576 | tf_op jit(solution)/shard_map/all_to_all | solution.py:436
  121.2 0.1 collective-permute-start.6
  121.3 13.5 %all-to-all-done = bf16[16,64,256]{2,1,0:T(8,128)(2,1)S(1)} async-done(((bf16[16,64,256]{2,1,0:T(8,128)(2,1)}), bf16[16,64,256]{2,1,0:T(8,128)(2,1)S(1)}, u32[]{:S(2)}, u32[]{:S(2)}) %all-to-all-start) | async-done | bytes 524320 | tf_op jit(solution)/shard_map/all_to_all | solution.py:436
  134.8 0.7 reduce_sum.21
  135.5 23.6 %all-to-all-start.1 = ((bf16[8,8,256]{2,1,0:T(8,128)(2,1)}), bf16[8,8,256]{2,1,0:T(8,128)(2,1)S(1)}, u32[]{:S(2)}, u32[]{:S(2)}) async-start(bf16[8,8,256]{2,1,0:T(8,128)(2,1)} %bitcast.6), calls=%async_computation.1 | async-start | bytes 65536 | tf_op jit(solution)/shard_map/all_to_all | solution.py:438
  159.1 0.8 copy-done.7
  159.9 7.2 %shard_map.135 = (bf16[128,2048]{1,0:T(8,128)(2,1)}, bf16[128,2048]{1,0:T(8,128)(2,1)}, bf16[128,2048]{1,0:T(8,128)(2,1)}) custom-call(s32[4]{0:T(128)} %pad_add_fusion.refs_0_, bf16[128,2048]{1,0:T(8,128)(2,1)} %reshape.45.refs_0_.refs_1_, bf16[128,2048]{1,0:T(8,128)(2,1)} %reshape.46.refs_1_.refs_2_, bf16[128,2048]{1,0:T(8,128)(2,1)} %reshape.47.refs_2_.refs_3_, ...), custom_call_target="tpu_custom_call" | custom-call | flops 1 | bytes 1 | tf_op jit(solution)/shard_map/pallas_call | solution.py:39
  167.2 0.7 copy-done.16
  167.9 2.3 %shard_map.136 = bf16[128,2048]{1,0:T(8,128)(2,1)} custom-call(s32[4]{0:T(128)} %pad_add_fusion.refs_0_, bf16[64,2048]{1,0:T(8,128)(2,1)} %get-tuple-element.49.refs_1_, bf16[64,2048]{1,0:T(8,128)(2,1)} %copy-done.16, bf16[128,2048]{1,0:T(8,128)(2,1)} %get-tuple-element.56.refs_3_), custom_call_target="tpu_custom_call" | custom-call | flops 1 | bytes 1 | tf_op jit(solution)/shard_map/pallas_call | solution.py:39
  170.2 1.1 reshape.51
  171.3 1.1 reshape.49
  172.5 1.1 reshape.50
  173.6 1.1 reshape.52
  174.7 0.6 convert_reduce_fusion
  (42 shorter events, 0.1 us)
Async XLA Ops:
  0.6 2.1 %copy-start.9 = (bf16[64,2,2048]{2,1,0:T(2,128)(2,1)S(1)}, bf16[64,2,2048]{2,1,0:T(2,128)(2,1)}, u32[]{:S(2)}) copy-start(bf16[64,2,2048]{2,1,0:T(2,128)(2,1)} %param.9) | copy-start | bytes 1572868
  4.4 9.8 %copy-start.10 = (bf16[64,2,2048]{2,1,0:T(2,128)(2,1)S(1)}, bf16[64,2,2048]{2,1,0:T(2,128)(2,1)}, u32[]{:S(2)}) copy-start(bf16[64,2,2048]{2,1,0:T(2,128)(2,1)} %param.14) | copy-start | bytes 1572868
  7.0 22.7 %collective-permute-start = (bf16[64,4224]{1,0:T(8,128)(2,1)}, bf16[64,4224]{1,0:T(8,128)(2,1)S(1)}, u32[]{:S(2)}, u32[]{:S(2)}) collective-permute-start(bf16[64,4224]{1,0:T(8,128)(2,1)} %get-tuple-element.33), channel_id=1, source_target_pairs={{0,32},{32,0},{1,33},{33,1},{2,34},{34,2},{3,35},{35,3},{4,36},{36... | collective-permute-start | bytes 1622024 | tf_op jit(solution)/shard_map/ppermute | solution.py:392
  15.1 3.7 %copy-start.11 = (bf16[64,2,2048]{2,1,0:T(2,128)(2,1)S(1)}, bf16[64,2,2048]{2,1,0:T(2,128)(2,1)}, u32[]{:S(2)}) copy-start(bf16[64,2,2048]{2,1,0:T(2,128)(2,1)} %param.15) | copy-start | bytes 1572868
  17.4 2.4 %copy-start.12 = (bf16[64,2,2048]{2,1,0:T(2,128)(2,1)S(1)}, bf16[64,2,2048]{2,1,0:T(2,128)(2,1)}, u32[]{:S(2)}) copy-start(bf16[64,2,2048]{2,1,0:T(2,128)(2,1)} %param.16) | copy-start | bytes 1572868
  17.4 48.6 %collective-permute-start.5 = (bf16[256,2048]{1,0:T(8,128)(2,1)}, bf16[256,2048]{1,0:T(8,128)(2,1)S(1)}, u32[]{:S(2)}, u32[]{:S(2)}) collective-permute-start(bf16[256,2048]{1,0:T(8,128)(2,1)} %shard_map.132), channel_id=1, source_target_pairs={{32,0},{64,32},{96,64},{128,96},{160,128},{192,160},{224,192},{33,... | collective-permute-start | bytes 3145736 | tf_op jit(solution)/shard_map/ppermute | solution.py:399
  20.8 4.1 %copy-start.18 = (f32[32]{0:T(128)S(1)}, f32[32]{0:T(128)}, u32[]{:S(2)}) copy-start(f32[32]{0:T(128)} %refs_0_.1) | copy-start | bytes 388
  29.7 0.8 copy-start.8
  30.5 11.7 %copy-start.15 = (f32[4,16,128]{2,1,0:T(8,128)S(1)}, f32[4,16,128]{2,1,0:T(8,128)}, u32[]{:S(2)}) copy-start(f32[4,16,128]{2,1,0:T(8,128)} %shard_map.129.refs_5_) | copy-start | bytes 98308
  36.4 29.6 %collective-permute-start.1 = (bf16[144,2048]{1,0:T(8,128)(2,1)}, bf16[144,2048]{1,0:T(8,128)(2,1)S(1)}, u32[]{:S(2)}, u32[]{:S(2)}) collective-permute-start(bf16[144,2048]{1,0:T(8,128)(2,1)} %get-tuple-element.34), channel_id=1, source_target_pairs={{0,64},{64,128},{128,192},{192,0},{1,65},{65,129},{129,193},{193,1... | collective-permute-start | bytes 1769480 | tf_op jit(solution)/shard_map/ppermute | solution.py:414
  38.0 5.5 %copy-start.19 = (f32[32]{0:T(128)S(1)}, f32[32]{0:T(128)}, u32[]{:S(2)}) copy-start(f32[32]{0:T(128)} %param.13) | copy-start | bytes 388
  38.0 28.0 %collective-permute-start.2 = (bf16[144,2048]{1,0:T(8,128)(2,1)}, bf16[144,2048]{1,0:T(8,128)(2,1)S(1)}, u32[]{:S(2)}, u32[]{:S(2)}) collective-permute-start(bf16[144,2048]{1,0:T(8,128)(2,1)} %get-tuple-element.35), channel_id=1, source_target_pairs={{0,128},{64,192},{128,0},{192,64},{1,129},{65,193},{129,1},{193,65... | collective-permute-start | bytes 1769480 | tf_op jit(solution)/shard_map/ppermute | solution.py:414
  40.9 25.2 %collective-permute-start.3 = (bf16[144,2048]{1,0:T(8,128)(2,1)}, bf16[144,2048]{1,0:T(8,128)(2,1)S(1)}, u32[]{:S(2)}, u32[]{:S(2)}) collective-permute-start(bf16[144,2048]{1,0:T(8,128)(2,1)} %get-tuple-element.36), channel_id=1, source_target_pairs={{0,192},{64,0},{128,64},{192,128},{1,193},{65,1},{129,65},{193,129... | collective-permute-start | bytes 1769480 | tf_op jit(solution)/shard_map/ppermute | solution.py:414
  42.3 19.4 %collective-permute-start.4 = (f32[4,16,128]{2,1,0:T(8,128)S(1)}, f32[4,16,128]{2,1,0:T(8,128)S(1)}, u32[]{:S(2)}, u32[]{:S(2)}) collective-permute-start(f32[4,16,128]{2,1,0:T(8,128)S(1)} %copy-done.15), channel_id=1, source_target_pairs={{32,0},{64,32},{96,64},{128,96},{160,128},{192,160},{224,192},{33,... | collective-permute-start | bytes 98312 | tf_op jit(solution)/shard_map/ppermute | solution.py:397
  61.7 0.6 copy-start.17
  66.0 1.0 copy-start
  66.1 1.1 copy-start.4
  66.1 1.3 copy-start.5
  66.1 1.5 copy-start.6
  74.1 38.9 %copy-start.3 = (f32[4,4,8,8,256]{4,3,2,1,0:T(8,128)S(1)}, f32[4,4,8,8,256]{4,3,2,1,0:T(8,128)}, u32[]{:S(2)}) copy-start(f32[4,4,8,8,256]{4,3,2,1,0:T(8,128)} %get-tuple-element.54) | copy-start | bytes 3145732
  74.1 38.9 %collective-permute-start.8 = (f32[4,4,8,8,256]{4,3,2,1,0:T(8,128)}, f32[4,4,8,8,256]{4,3,2,1,0:T(8,128)S(1)}, u32[]{:S(2)}, u32[]{:S(2)}) collective-permute-start(f32[4,4,8,8,256]{4,3,2,1,0:T(8,128)} %get-tuple-element.55), channel_id=1, source_target_pairs={{0,1},{1,0},{2,3},{3,2},{4,5},{5,4},{6,7},{7,6},{8,9},{9,8},{10,11... | collective-permute-start | bytes 3145736 | tf_op jit(solution)/shard_map/ppermute | solution.py:434
  81.6 77.4 %collective-permute-start.7 = (bf16[144,2048]{1,0:T(8,128)(2,1)}, bf16[144,2048]{1,0:T(8,128)(2,1)S(1)}, u32[]{:S(2)}, u32[]{:S(2)}) collective-permute-start(bf16[144,2048]{1,0:T(8,128)(2,1)} %get-tuple-element.51), channel_id=1, source_target_pairs={{0,32},{32,64},{64,96},{96,128},{128,160},{160,192},{192,224},{1,3... | collective-permute-start | bytes 1769480 | tf_op jit(solution)/shard_map/ppermute | solution.py:448
  113.9 7.3 %copy-start.20 = (bf16[64,2048]{1,0:T(8,128)(2,1)S(1)}, bf16[64,2048]{1,0:T(8,128)(2,1)}, u32[]{:S(2)}) copy-start(bf16[64,2048]{1,0:T(8,128)(2,1)} %get-tuple-element.50) | copy-start | bytes 786436
  113.9 20.9 %all-to-all-start = ((bf16[16,64,256]{2,1,0:T(8,128)(2,1)}), bf16[16,64,256]{2,1,0:T(8,128)(2,1)S(1)}, u32[]{:S(2)}, u32[]{:S(2)}) async-start(bf16[16,64,256]{2,1,0:T(8,128)(2,1)} %bitcast.5.refs_9_), calls=%async_computation | async-start | bytes 1048576 | tf_op jit(solution)/shard_map/all_to_all | solution.py:436
  121.2 45.9 %collective-permute-start.6 = (bf16[64,2048]{1,0:T(8,128)(2,1)S(1)}, bf16[64,2048]{1,0:T(8,128)(2,1)S(1)}, u32[]{:S(2)}, u32[]{:S(2)}) collective-permute-start(bf16[64,2048]{1,0:T(8,128)(2,1)S(1)} %copy-done.20), channel_id=1, source_target_pairs={{0,32},{32,0},{1,33},{33,1},{2,34},{34,2},{3,35},{35,3},{4,36},{36... | collective-permute-start | bytes 786440 | tf_op jit(solution)/shard_map/ppermute | solution.py:432
  135.5 39.2 %all-to-all-start.1 = ((bf16[8,8,256]{2,1,0:T(8,128)(2,1)}), bf16[8,8,256]{2,1,0:T(8,128)(2,1)S(1)}, u32[]{:S(2)}, u32[]{:S(2)}) async-start(bf16[8,8,256]{2,1,0:T(8,128)(2,1)} %bitcast.6), calls=%async_computation.1 | async-start | bytes 65536 | tf_op jit(solution)/shard_map/all_to_all | solution.py:438
  159.1 0.8 copy-start.7
  167.2 0.7 copy-start.16
  167.9 2.3 %copy-start.1 = (bf16[128,2048]{1,0:T(8,128)(2,1)S(1)}, bf16[128,2048]{1,0:T(8,128)(2,1)}, u32[]{:S(2)}) copy-start(bf16[128,2048]{1,0:T(8,128)(2,1)} %get-tuple-element.56.refs_3_) | copy-start | bytes 1572868
  170.2 1.1 copy-start.2
  171.3 1.1 copy-start.14
  172.5 1.1 copy-start.13

commit v5 on v4

--- a/solution.py
+++ b/solution.py
@@ -1,5 +1,3 @@
-import functools
-
 import jax
 import jax.numpy as jnp
 from jax import lax
@@ -80,10 +78,24 @@
     return jnp.concatenate([value[:n], value[n:]], axis=1)
 
 
-def join_body(q, g, out):
+def add_pieces(value, ref, rows):
+    for piece in range(3):
+        part = value.astype(BF)
+        value = value - part.astype(F32)
+        ref[rows:, piece * LANES : (piece + 1) * LANES] = part
+    ref[rows:, 3 * LANES :] = jnp.zeros((16, GROUP - 3 * LANES), BF)
+
+
+def from_pieces(ref, rows):
+    a, b, c = (ref[rows:, i * LANES : (i + 1) * LANES].astype(F32) for i in range(3))
+    return a + (b + c)
+
+
+def join_body(q, g, stats, out):
     rows = q.shape[0]
     out[:rows, :] = q[...]
-    out[rows:, :] = g[...]
+    out[rows : 2 * rows, :] = g[...]
+    add_pieces(stats[0], out, 2 * rows)
 
 
 def pack_body(at, x, g, codes, own, out):
@@ -301,15 +313,15 @@
     return grad_q, grad_k, grad_v
 
 
-def cross_body(qg, before, k, v, gq, gk, gv):
+def cross_body(qg, k, v, gq, gk, gv):
     rows, width = k.shape
     heads = width // HEAD
-    theirs = before[0]
+    theirs = from_pieces(qg, 2 * rows)
     seen = seen_mask(rows, True)
     logs, deltas = [], []
     for p in range(width // LANES):
         at = slice(p * LANES, (p + 1) * LANES)
-        q_pair, k_pair, g_pair = qg[:rows, at], k[:, at], qg[rows:, at]
+        q_pair, k_pair, g_pair = qg[:rows, at], k[:, at], qg[rows : 2 * rows, at]
         ps, ds = [], []
         for j, (s, d) in enumerate(softened(k_pair, v[:, at], q_pair, g_pair, seen)):
             h = 2 * p + j
@@ -327,12 +339,7 @@
         gq[:rows, at] = a.astype(BF)
         gk[:, at] = b
         gv[:, at] = c
-    rest = jnp.concatenate(logs + deltas, axis=0)
-    for piece in range(3):
-        part = rest.astype(BF)
-        rest = rest - part.astype(F32)
-        gq[rows:, piece * LANES : (piece + 1) * LANES] = part
-    gq[rows:, 3 * LANES :] = jnp.zeros((16, GROUP - 3 * LANES), BF)
+    add_pieces(jnp.concatenate(logs + deltas, axis=0), gq, rows)
 
 
 def own_body(at_ref, q, k, v, g, ours, gq_far, gk_far, gv_far, gq, gk, gv):
@@ -341,8 +348,7 @@
     seen = seen_mask(rows, False)
     begins = at_ref[2] == 0
     near = ours[0]
-    pieces = (gq_far[rows:, i * LANES : (i + 1) * LANES].astype(F32) for i in range(3))
-    away = functools.reduce(lambda a, b: a + b, pieces)
+    away = from_pieces(gq_far, rows)
     for p in range(width // LANES):
         at = slice(p * LANES, (p + 1) * LANES)
         q_pair, k_pair, g_pair = q[:, at], k[:, at], g[:, at]
@@ -394,8 +400,7 @@
     steps = width // GROUP
     stats = ((steps, 2 * GROUP // HEAD, rows), F32)
     stats_own = call(stats_body, [stats], [], [q2, k2, v2, g2], steps=steps)[0]
-    stats_next = lax.ppermute(stats_own, TM, to_prev)
-    qg = call(join_body, [((2 * rows, width), BF)], [], [q2, g2])[0]
+    qg = call(join_body, [((2 * rows + 16, width), BF)], [], [q2, g2, stats_own], steps=steps)[0]
     qg_next = lax.ppermute(qg, TM, to_prev)
 
     wide = (rows, width)
@@ -408,7 +413,7 @@
         + [(state, BF)] * 3,
         [at],
         [own, got, bc_weight, rate_wide],
-        [stats_own],
+        [qg],
     )
     m1, m2, m3 = (
         lax.ppermute(m, "y", [(i, (i + s) % ny) for i in range(ny)])
@@ -419,7 +424,6 @@
         [(wide, F32), (square, F32), (square, F32), ((width, rows), BF)],
         [decay_rates],
         [xs, gs, bc, sums, sums_t],
-        [stats_next],
     )
     order = 1.0 / (rows * tm * lax.axis_size(("zl", "x", "c")))
     keep, give, mine, yours = call(
@@ -442,21 +446,22 @@
         cross_body,
         [((rows + 16, width), BF), (wide, F32), (wide, F32)],
         [],
-        [qg_next, stats_next, k2, v2],
+        [qg_next, k2, v2],
         steps=steps,
     )
     gq_far = lax.ppermute(gq_out, TM, to_next)
+    grad_x = call(unpack_body, [(wide, BF)], [at], [keep, gx_far], [chip])[0]
+    grad_x = grad_x.reshape(length, blocks, width)
     gq, gk, gv = call(
         own_body,
         [(wide, BF)] * 3,
         [at],
         [q2, k2, v2, g2, stats_own, gq_far, gk_far, gv_far],
-        [chip],
+        [chip, grad_x],
         steps=steps,
     )
     shape = (length, blocks, width)
-    grad_x = call(unpack_body, [(wide, BF)], [at], [keep, gx_far], [gk])[0]
-    return grad_x.reshape(shape), gq.reshape(shape), gk.reshape(shape), gv.reshape(shape), grad_bc
+    return grad_x, gq.reshape(shape), gk.reshape(shape), gv.reshape(shape), grad_bc
 
 
 def solution(mesh):

time: 177 us -> 175 us (0.989)
  starting transfers between devices: 78.1 us -> 70.3 us
  waiting for transfers between devices: 34.8 us -> 38.7 us
    ppermute x1 -> x0, waiting for transfers between devices: 17.4 us -> none  [local(): stats_next = lax.ppermute(stats_own, TM, to_prev)]
    ppermute x1, waiting for transfers between devices: 0.01 us -> 14.9 us  [local(): qg_next = lax.ppermute(qg, TM, to_prev)]
    all_to_all x1, starting transfers between devices: 23.6 us -> 11.2 us  [local(): spread = lax.all_to_all(plane, ('zh', 'zl'), 0, 0, tiled=True)]
    ppermute x1, waiting for transfers between devices: 0.01 us -> 8.16 us  [local(): gx_far = lax.ppermute(give, 'zh', flip)]
    ppermute x3, starting transfers between devices: 5.83 us -> 10.4 us  [local(): lax.ppermute(m, 'y', [(i, (i + s) % ny) for i in range(ny)])]
    ppermute x1, starting transfers between devices: 0.1 us -> 3.54 us  [local(): gx_far = lax.ppermute(give, 'zh', flip)]
    ppermute x1, starting transfers between devices: 31.3 us -> 29.3 us  [local(): gq_far = lax.ppermute(gq_out, TM, to_next)]
    ppermute x1, waiting for transfers between devices: 3.96 us -> 2.04 us  [local(): got = lax.ppermute(out, 'zh', flip)]
  transfers between devices with their start and end apart: 11 -> 10, of which waited for: 3 -> 4; matrix products, arithmetic and copies ran while one was open for 6% -> 7% of each run, Pallas kernels for 19% -> 20%
where the time goes in v5:
time: 175 us; the launch traced here: 174 us
  starting transfers between devices  70.3 us (40%)
  Pallas kernels  43.2 us (25%)
  waiting for transfers between devices  38.7 us (22%)
  local copies, waits for them, and re-layouts  18.2 us (10%)
  other arithmetic  2.84 us (2%)
    pallas_call x9, Pallas kernels, call(): pl.pallas_call(run, out_shape=[jax.ShapeDtypeStruct(s, d) for s, d in out...  43.2 us
    ppermute x1, starting transfers between devices, local(): gq_far = lax.ppermute(gq_out, TM, to_next)  29.3 us
    ppermute x1, waiting for transfers between devices, local(): qg_next = lax.ppermute(qg, TM, to_prev)  14.9 us
    all_to_all x1, waiting for transfers between devices, local(): spread = lax.all_to_all(chip, ('y', 'x'), 0, 0, tiled=True)  13.6 us
    all_to_all x1, starting transfers between devices, local(): spread = lax.all_to_all(plane, ('zh', 'zl'), 0, 0, tiled=True)  11.2 us
    ppermute x3, starting transfers between devices, local(): lax.ppermute(m, 'y', [(i, (i + s) % ny) for i in range(ny)])  10.4 us
    ppermute x1, waiting for transfers between devices, local(): gx_far = lax.ppermute(give, 'zh', flip)  8.16 us
    all_to_all x1, starting transfers between devices, local(): spread = lax.all_to_all(chip, ('y', 'x'), 0, 0, tiled=True)  7.25 us
  transfers between devices with their start and end apart: 10, of which 4 were waited for; matrix products, arithmetic and copies ran while one was open for 7% of the time, Pallas kernels for 20%

profile of v5, /device:TPU:2, one launch (start us, length us, event | category | flops | bytes accessed | tf_op | source)
XLA Modules:
  0.0 174.0 jit_solution(6142406821594061659)
XLA Ops:
  0.6 2.1 %reshape.44.refs_2_.refs_3_.refs_1_.refs_4_ = bf16[128,2048]{1,0:T(8,128)(2,1)} reshape(bf16[64,2,2048]{2,1,0:T(2,128)(2,1)} %param.17) | data formatting | bytes 1048576 | tf_op jit(solution)/shard_map/reshape | solution.py:389
  2.7 1.0 reshape.43.refs_1_
  3.7 0.6 pad_add_fusion.refs_0_
  4.3 2.5 %shard_map.128 = (bf16[64,4224]{1,0:T(8,128)(2,1)}, bf16[64,4224]{1,0:T(8,128)(2,1)}) custom-call(s32[4]{0:T(128)} %pad_add_fusion.refs_0_, bf16[128,2048]{1,0:T(8,128)(2,1)} %reshape.43.refs_1_, bf16[128,2048]{1,0:T(8,128)(2,1)} %reshape.44.refs_2_.refs_3_.refs_1_.refs_4_, s32[2,32,64]{2,1,0:T(8,128)} %bitcast.7), custom_call_target="tpu_custom_call" | custom-call | flops 1 | bytes 1 | tf_op jit(solution)/shard_map/pallas_call | solution.py:37
  6.9 7.2 %collective-permute-start = (bf16[64,4224]{1,0:T(8,128)(2,1)}, bf16[64,4224]{1,0:T(8,128)(2,1)S(1)}, u32[]{:S(2)}, u32[]{:S(2)}) collective-permute-start(bf16[64,4224]{1,0:T(8,128)(2,1)} %get-tuple-element.33), channel_id=1, source_target_pairs={{0,32},{32,0},{1,33},{33,1},{2,34},{34,2},{3,35},{35,3},{4,36},{36... | collective-permute-start | bytes 1622024 | tf_op jit(solution)/shard_map/ppermute | solution.py:398
  14.1 1.0 reshape.45.refs_0_.refs_1_
  15.1 1.0 reshape.46.refs_1_.refs_2_
  16.1 1.0 reshape.47.refs_2_.refs_3_
  17.0 4.1 %shard_map.129.refs_2_.refs_5_ = f32[4,16,128]{2,1,0:T(8,128)} custom-call(bf16[128,2048]{1,0:T(8,128)(2,1)} %reshape.45.refs_0_.refs_1_, bf16[128,2048]{1,0:T(8,128)(2,1)} %reshape.46.refs_1_.refs_2_, bf16[128,2048]{1,0:T(8,128)(2,1)} %reshape.47.refs_2_.refs_3_, bf16[128,2048]{1,0:T(8,128)(2,1)} %reshape.44.refs_2_.refs_3_.refs_1_.refs_4_), custom_call_target="tpu_custom_call" | custom-call | flops 1 | bytes 1 | tf_op jit(solution)/shard_map/pallas_call | solution.py:37
  21.2 3.5 %shard_map.130.refs_5_ = bf16[272,2048]{1,0:T(8,128)(2,1)} custom-call(bf16[128,2048]{1,0:T(8,128)(2,1)} %reshape.45.refs_0_.refs_1_, bf16[128,2048]{1,0:T(8,128)(2,1)} %reshape.44.refs_2_.refs_3_.refs_1_.refs_4_, f32[4,16,128]{2,1,0:T(8,128)} %shard_map.129.refs_2_.refs_5_), custom_call_target="tpu_custom_call" | custom-call | flops 1 | bytes 1 | tf_op jit(solution)/shard_map/pallas_call | solution.py:37
  24.7 1.3 collective-permute-start.4
  26.0 0.1 broadcast_in_dim.6
  26.1 0.7 broadcast_in_dim_reshape.6.refs_4_
  26.7 2.0 %collective-permute-done.refs_2_ = bf16[64,4224]{1,0:T(8,128)(2,1)S(1)} collective-permute-done((bf16[64,4224]{1,0:T(8,128)(2,1)}, bf16[64,4224]{1,0:T(8,128)(2,1)S(1)}, u32[]{:S(2)}, u32[]{:S(2)}) %collective-permute-start) | collective-permute-done | bytes 540704 | tf_op jit(solution)/shard_map/ppermute | solution.py:398
  28.8 0.8 copy-done.6
  29.6 5.9 %shard_map.131 = (bf16[128,2048]{1,0:T(8,128)(2,1)}, bf16[128,2048]{1,0:T(8,128)(2,1)}, bf16[128,256]{1,0:T(8,128)(2,1)}, f32[128,128]{1,0:T(8,128)}, f32[128,12...) custom-call(s32[4]{0:T(128)} %pad_add_fusion.refs_0_, ...), custom_call_target="tpu_custom_call" | custom-call | flops 1 | bytes 1 | tf_op jit(solution)/shard_map/pallas_call | solution.py:37
  35.5 6.2 %collective-permute-start.1 = (bf16[144,2048]{1,0:T(8,128)(2,1)}, bf16[144,2048]{1,0:T(8,128)(2,1)S(1)}, u32[]{:S(2)}, u32[]{:S(2)}) collective-permute-start(bf16[144,2048]{1,0:T(8,128)(2,1)} %get-tuple-element.34), channel_id=1, source_target_pairs={{0,64},{64,128},{128,192},{192,0},{1,65},{65,129},{129,193},{193,1... | collective-permute-start | bytes 1769480 | tf_op jit(solution)/shard_map/ppermute | solution.py:419
  41.7 2.9 %collective-permute-start.2 = (bf16[144,2048]{1,0:T(8,128)(2,1)}, bf16[144,2048]{1,0:T(8,128)(2,1)S(1)}, u32[]{:S(2)}, u32[]{:S(2)}) collective-permute-start(bf16[144,2048]{1,0:T(8,128)(2,1)} %get-tuple-element.35), channel_id=1, source_target_pairs={{0,128},{64,192},{128,0},{192,64},{1,129},{65,193},{129,1},{193,65... | collective-permute-start | bytes 1769480 | tf_op jit(solution)/shard_map/ppermute | solution.py:419
  44.5 1.4 collective-permute-start.3
  45.9 0.1 broadcast_in_dim.7
  46.0 0.7 broadcast_in_dim_reshape.7.refs_5_
  46.6 3.7 %shard_map.132 = (f32[128,2048]{1,0:T(8,128)}, f32[128,128]{1,0:T(8,128)}, f32[128,128]{1,0:T(8,128)}, bf16[2048,128]{1,0:T(8,128)(2,1)}) custom-call(f32[32]{0:T(128)} %refs_0_.1, bf16[128,2048]{1,0:T(8,128)(2,1)} %get-tuple-element.42.refs_1_, bf16[128,2048]{1,0:T(8,128)(2,1)} %get-tuple-element.37.refs_2_.refs_7_, ...), custom_call_target="tpu_custom_call" | custom-call | flops 1 | bytes 1 | tf_op jit(solution)/shard_map/pallas_call | solution.py:37
  50.4 14.9 %collective-permute-done.4.refs_16_.refs_0_ = bf16[272,2048]{1,0:T(8,128)(2,1)S(1)} collective-permute-done((bf16[272,2048]{1,0:T(8,128)(2,1)}, bf16[272,2048]{1,0:T(8,128)(2,1)S(1)}, u32[]{:S(2)}, u32[]{:S(2)}) %collective-permute-start.4) | collective-permute-done | bytes 1114144 | tf_op jit(solution)/shard_map/ppermute | solution.py:404
  65.3 0.0 collective-permute-done.2.refs_2_
  65.3 1.0 copy-done
  66.3 0.2 copy-done.3
  66.5 0.2 copy-done.4
  66.6 0.2 copy-done.5
  66.8 6.5 %shard_map.133 = (bf16[64,2048]{1,0:T(8,128)(2,1)}, bf16[64,2048]{1,0:T(8,128)(2,1)}, f32[4,4,8,8,256]{4,3,2,1,0:T(8,128)}, f32[4,4,8,8,256]{4,3,2,1,0:T(8,128)}) custom-call(s32[4]{0:T(128)} %pad_add_fusion.refs_0_, bf16[144,2048]{1,0:T(8,128)(2,1)} %copy-done.3, bf16[144,2048]{1,0:T(8,128)(2,1)} %copy-done.4, bf16[144,2048]{1,0:T(8,128)(2,1)} %copy-done.5, ...), custom_call_target="tpu_custom_call" | custom-call | flops 1 | bytes 1 | tf_op jit(solution)/shard_map/pallas_call | solution.py:37
  73.4 0.1 collective-permute-start.6
  73.4 7.5 %shard_map.135 = (bf16[144,2048]{1,0:T(8,128)(2,1)}, f32[128,2048]{1,0:T(8,128)}, f32[128,2048]{1,0:T(8,128)}) custom-call(bf16[272,2048]{1,0:T(8,128)(2,1)} %copy-done, bf16[128,2048]{1,0:T(8,128)(2,1)} %reshape.46.refs_1_.refs_2_, bf16[128,2048]{1,0:T(8,128)(2,1)} %reshape.47.refs_2_.refs_3_), custom_call_target="tpu_custom_call" | custom-call | flops 1 | bytes 1 | tf_op jit(solution)/shard_map/pallas_call | solution.py:37
  80.9 29.3 %collective-permute-start.7 = (bf16[144,2048]{1,0:T(8,128)(2,1)}, bf16[144,2048]{1,0:T(8,128)(2,1)S(1)}, u32[]{:S(2)}, u32[]{:S(2)}) collective-permute-start(bf16[144,2048]{1,0:T(8,128)(2,1)} %get-tuple-element.53), channel_id=1, source_target_pairs={{0,32},{32,64},{64,96},{96,128},{128,160},{160,192},{192,224},{1,3... | collective-permute-start | bytes 1769480 | tf_op jit(solution)/shard_map/ppermute | solution.py:452
  110.3 0.9 add_convert_fusion
  111.2 7.3 %all-to-all-start = ((bf16[16,64,256]{2,1,0:T(8,128)(2,1)}), bf16[16,64,256]{2,1,0:T(8,128)(2,1)S(1)}, u32[]{:S(2)}, u32[]{:S(2)}) async-start(bf16[16,64,256]{2,1,0:T(8,128)(2,1)} %bitcast.5.refs_3_.refs_9_), calls=%async_computation | async-start | bytes 1048576 | tf_op jit(solution)/shard_map/all_to_all | solution.py:440
  118.5 3.5 %collective-permute-start.5 = (bf16[64,2048]{1,0:T(8,128)(2,1)S(1)}, bf16[64,2048]{1,0:T(8,128)(2,1)S(1)}, u32[]{:S(2)}, u32[]{:S(2)}) collective-permute-start(bf16[64,2048]{1,0:T(8,128)(2,1)S(1)} %copy-done.16), channel_id=1, source_target_pairs={{0,32},{32,0},{1,33},{33,1},{2,34},{34,2},{3,35},{35,3},{4,36},{36... | collective-permute-start | bytes 786440 | tf_op jit(solution)/shard_map/ppermute | solution.py:436
  122.0 13.6 %all-to-all-done = bf16[16,64,256]{2,1,0:T(8,128)(2,1)S(1)} async-done(((bf16[16,64,256]{2,1,0:T(8,128)(2,1)}), bf16[16,64,256]{2,1,0:T(8,128)(2,1)S(1)}, u32[]{:S(2)}, u32[]{:S(2)}) %all-to-all-start) | async-done | bytes 524320 | tf_op jit(solution)/shard_map/all_to_all | solution.py:440
  135.6 0.7 reduce_sum.21
  136.3 11.2 %all-to-all-start.1 = ((bf16[8,8,256]{2,1,0:T(8,128)(2,1)}), bf16[8,8,256]{2,1,0:T(8,128)(2,1)S(1)}, u32[]{:S(2)}, u32[]{:S(2)}) async-start(bf16[8,8,256]{2,1,0:T(8,128)(2,1)} %bitcast.6), calls=%async_computation.1 | async-start | bytes 65536 | tf_op jit(solution)/shard_map/all_to_all | solution.py:442
  147.5 8.2 %collective-permute-done.5.refs_2_ = bf16[64,2048]{1,0:T(8,128)(2,1)S(1)} collective-permute-done((bf16[64,2048]{1,0:T(8,128)(2,1)S(1)}, bf16[64,2048]{1,0:T(8,128)(2,1)S(1)}, u32[]{:S(2)}, u32[]{:S(2)}) %collective-permute-start.5) | collective-permute-done | bytes 262176 | tf_op jit(solution)/shard_map/ppermute | solution.py:436
  155.7 0.7 copy-done.13
  156.4 2.3 %shard_map.134 = bf16[128,2048]{1,0:T(8,128)(2,1)} custom-call(s32[4]{0:T(128)} %pad_add_fusion.refs_0_, bf16[64,2048]{1,0:T(8,128)(2,1)} %get-tuple-element.49.refs_1_, bf16[64,2048]{1,0:T(8,128)(2,1)} %copy-done.13, bf16[16,64,256]{2,1,0:T(8,128)(2,1)} %bitcast.5.refs_3_.refs_9_), custom_call_target="tpu_custom_call" | custom-call | flops 1 | bytes 1 | tf_op jit(solution)/shard_map/pallas_call | solution.py:37
  158.6 2.2 %reshape.49.refs_10_ = bf16[64,2,2048]{2,1,0:T(2,128)(2,1)} reshape(bf16[128,2048]{1,0:T(8,128)(2,1)} %shard_map.134) | data formatting | bytes 1048576 | tf_op jit(solution)/shard_map/reshape | solution.py:454
  160.8 0.8 copy-done.2
  161.6 7.2 %shard_map.136 = (bf16[128,2048]{1,0:T(8,128)(2,1)}, bf16[128,2048]{1,0:T(8,128)(2,1)}, bf16[128,2048]{1,0:T(8,128)(2,1)}) custom-call(s32[4]{0:T(128)} %pad_add_fusion.refs_0_, bf16[128,2048]{1,0:T(8,128)(2,1)} %reshape.45.refs_0_.refs_1_, bf16[128,2048]{1,0:T(8,128)(2,1)} %reshape.46.refs_1_.refs_2_, bf16[128,2048]{1,0:T(8,128)(2,1)} %reshape.47.refs_2_.refs_3_, ...), custom_call_target="tpu_custom_call" | custom-call | flops 1 | bytes 1 | tf_op jit(solution)/shard_map/pallas_call | solution.py:37
  168.9 2.3 %reshape.50 = bf16[64,2,2048]{2,1,0:T(2,128)(2,1)} reshape(bf16[128,2048]{1,0:T(8,128)(2,1)} %get-tuple-element.56) | data formatting | bytes 1048576 | tf_op jit(solution)/shard_map/reshape | solution.py:464
  171.1 1.1 reshape.51
  172.3 1.1 reshape.52
  173.4 0.6 convert_reduce_fusion
  (32 shorter events, 0.1 us)
Async XLA Ops:
  0.6 2.1 %copy-start.7 = (bf16[64,2,2048]{2,1,0:T(2,128)(2,1)S(1)}, bf16[64,2,2048]{2,1,0:T(2,128)(2,1)}, u32[]{:S(2)}) copy-start(bf16[64,2,2048]{2,1,0:T(2,128)(2,1)} %param.9) | copy-start | bytes 1572868
  2.7 11.3 %copy-start.8 = (bf16[64,2,2048]{2,1,0:T(2,128)(2,1)S(1)}, bf16[64,2,2048]{2,1,0:T(2,128)(2,1)}, u32[]{:S(2)}) copy-start(bf16[64,2,2048]{2,1,0:T(2,128)(2,1)} %param.14) | copy-start | bytes 1572868
  3.7 11.3 %copy-start.9 = (bf16[64,2,2048]{2,1,0:T(2,128)(2,1)S(1)}, bf16[64,2,2048]{2,1,0:T(2,128)(2,1)}, u32[]{:S(2)}) copy-start(bf16[64,2,2048]{2,1,0:T(2,128)(2,1)} %param.15) | copy-start | bytes 1572868
  6.9 9.2 %copy-start.10 = (bf16[64,2,2048]{2,1,0:T(2,128)(2,1)S(1)}, bf16[64,2,2048]{2,1,0:T(2,128)(2,1)}, u32[]{:S(2)}) copy-start(bf16[64,2,2048]{2,1,0:T(2,128)(2,1)} %param.16) | copy-start | bytes 1572868
  6.9 21.9 %collective-permute-start = (bf16[64,4224]{1,0:T(8,128)(2,1)}, bf16[64,4224]{1,0:T(8,128)(2,1)S(1)}, u32[]{:S(2)}, u32[]{:S(2)}) collective-permute-start(bf16[64,4224]{1,0:T(8,128)(2,1)} %get-tuple-element.33), channel_id=1, source_target_pairs={{0,32},{32,0},{1,33},{33,1},{2,34},{34,2},{3,35},{35,3},{4,36},{36... | collective-permute-start | bytes 1622024 | tf_op jit(solution)/shard_map/ppermute | solution.py:398
  21.2 4.8 %copy-start.14 = (f32[32]{0:T(128)S(1)}, f32[32]{0:T(128)}, u32[]{:S(2)}) copy-start(f32[32]{0:T(128)} %refs_0_.1) | copy-start | bytes 388
  24.7 40.6 %collective-permute-start.4 = (bf16[272,2048]{1,0:T(8,128)(2,1)}, bf16[272,2048]{1,0:T(8,128)(2,1)S(1)}, u32[]{:S(2)}, u32[]{:S(2)}) collective-permute-start(bf16[272,2048]{1,0:T(8,128)(2,1)} %shard_map.130.refs_5_), channel_id=1, source_target_pairs={{32,0},{64,32},{96,64},{128,96},{160,128},{192,160},{224,192},{33,... | collective-permute-start | bytes 3342344 | tf_op jit(solution)/shard_map/ppermute | solution.py:404
  28.8 0.8 copy-start.6
  29.6 16.3 %copy-start.15 = (f32[32]{0:T(128)S(1)}, f32[32]{0:T(128)}, u32[]{:S(2)}) copy-start(f32[32]{0:T(128)} %param.13) | copy-start | bytes 388
  35.5 29.8 %collective-permute-start.1 = (bf16[144,2048]{1,0:T(8,128)(2,1)}, bf16[144,2048]{1,0:T(8,128)(2,1)S(1)}, u32[]{:S(2)}, u32[]{:S(2)}) collective-permute-start(bf16[144,2048]{1,0:T(8,128)(2,1)} %get-tuple-element.34), channel_id=1, source_target_pairs={{0,64},{64,128},{128,192},{192,0},{1,65},{65,129},{129,193},{193,1... | collective-permute-start | bytes 1769480 | tf_op jit(solution)/shard_map/ppermute | solution.py:419
  41.7 23.6 %collective-permute-start.2 = (bf16[144,2048]{1,0:T(8,128)(2,1)}, bf16[144,2048]{1,0:T(8,128)(2,1)S(1)}, u32[]{:S(2)}, u32[]{:S(2)}) collective-permute-start(bf16[144,2048]{1,0:T(8,128)(2,1)} %get-tuple-element.35), channel_id=1, source_target_pairs={{0,128},{64,192},{128,0},{192,64},{1,129},{65,193},{129,1},{193,65... | collective-permute-start | bytes 1769480 | tf_op jit(solution)/shard_map/ppermute | solution.py:419
  44.5 20.7 %collective-permute-start.3 = (bf16[144,2048]{1,0:T(8,128)(2,1)}, bf16[144,2048]{1,0:T(8,128)(2,1)S(1)}, u32[]{:S(2)}, u32[]{:S(2)}) collective-permute-start(bf16[144,2048]{1,0:T(8,128)(2,1)} %get-tuple-element.36), channel_id=1, source_target_pairs={{0,192},{64,0},{128,64},{192,128},{1,193},{65,1},{129,65},{193,129... | collective-permute-start | bytes 1769480 | tf_op jit(solution)/shard_map/ppermute | solution.py:419
  65.3 1.0 copy-start
  65.3 1.2 copy-start.3
  65.3 1.4 copy-start.4
  65.3 1.6 copy-start.5
  73.3 36.9 %copy-start.1 = (f32[4,4,8,8,256]{4,3,2,1,0:T(8,128)S(1)}, f32[4,4,8,8,256]{4,3,2,1,0:T(8,128)}, u32[]{:S(2)}) copy-start(f32[4,4,8,8,256]{4,3,2,1,0:T(8,128)} %get-tuple-element.51) | copy-start | bytes 3145732
  73.4 36.9 %collective-permute-start.6 = (f32[4,4,8,8,256]{4,3,2,1,0:T(8,128)}, f32[4,4,8,8,256]{4,3,2,1,0:T(8,128)S(1)}, u32[]{:S(2)}, u32[]{:S(2)}) collective-permute-start(f32[4,4,8,8,256]{4,3,2,1,0:T(8,128)} %get-tuple-element.52), channel_id=1, source_target_pairs={{0,1},{1,0},{2,3},{3,2},{4,5},{5,4},{6,7},{7,6},{8,9},{9,8},{10,11... | collective-permute-start | bytes 3145736 | tf_op jit(solution)/shard_map/ppermute | solution.py:438
  80.9 79.9 %collective-permute-start.7 = (bf16[144,2048]{1,0:T(8,128)(2,1)}, bf16[144,2048]{1,0:T(8,128)(2,1)S(1)}, u32[]{:S(2)}, u32[]{:S(2)}) collective-permute-start(bf16[144,2048]{1,0:T(8,128)(2,1)} %get-tuple-element.53), channel_id=1, source_target_pairs={{0,32},{32,64},{64,96},{96,128},{128,160},{160,192},{192,224},{1,3... | collective-permute-start | bytes 1769480 | tf_op jit(solution)/shard_map/ppermute | solution.py:452
  110.3 8.2 %copy-start.16 = (bf16[64,2048]{1,0:T(8,128)(2,1)S(1)}, bf16[64,2048]{1,0:T(8,128)(2,1)}, u32[]{:S(2)}) copy-start(bf16[64,2048]{1,0:T(8,128)(2,1)} %get-tuple-element.50) | copy-start | bytes 786436
  111.2 24.4 %all-to-all-start = ((bf16[16,64,256]{2,1,0:T(8,128)(2,1)}), bf16[16,64,256]{2,1,0:T(8,128)(2,1)S(1)}, u32[]{:S(2)}, u32[]{:S(2)}) async-start(bf16[16,64,256]{2,1,0:T(8,128)(2,1)} %bitcast.5.refs_3_.refs_9_), calls=%async_computation | async-start | bytes 1048576 | tf_op jit(solution)/shard_map/all_to_all | solution.py:440
  118.5 37.2 %collective-permute-start.5 = (bf16[64,2048]{1,0:T(8,128)(2,1)S(1)}, bf16[64,2048]{1,0:T(8,128)(2,1)S(1)}, u32[]{:S(2)}, u32[]{:S(2)}) collective-permute-start(bf16[64,2048]{1,0:T(8,128)(2,1)S(1)} %copy-done.16), channel_id=1, source_target_pairs={{0,32},{32,0},{1,33},{33,1},{2,34},{34,2},{3,35},{35,3},{4,36},{36... | collective-permute-start | bytes 786440 | tf_op jit(solution)/shard_map/ppermute | solution.py:436
  136.3 37.1 %all-to-all-start.1 = ((bf16[8,8,256]{2,1,0:T(8,128)(2,1)}), bf16[8,8,256]{2,1,0:T(8,128)(2,1)S(1)}, u32[]{:S(2)}, u32[]{:S(2)}) async-start(bf16[8,8,256]{2,1,0:T(8,128)(2,1)} %bitcast.6), calls=%async_computation.1 | async-start | bytes 65536 | tf_op jit(solution)/shard_map/all_to_all | solution.py:442
  155.7 0.7 copy-start.13
  160.8 0.8 copy-start.2
  168.8 2.3 %copy-start.12 = (bf16[128,2048]{1,0:T(8,128)(2,1)S(1)}, bf16[128,2048]{1,0:T(8,128)(2,1)}, u32[]{:S(2)}) copy-start(bf16[128,2048]{1,0:T(8,128)(2,1)} %get-tuple-element.57) | copy-start | bytes 1572868
  168.8 3.4 %copy-start.11 = (bf16[128,2048]{1,0:T(8,128)(2,1)S(1)}, bf16[128,2048]{1,0:T(8,128)(2,1)}, u32[]{:S(2)}) copy-start(bf16[128,2048]{1,0:T(8,128)(2,1)} %get-tuple-element.58) | copy-start | bytes 1572868

commit v6 on v5

--- a/solution.py
+++ b/solution.py
@@ -425,13 +425,20 @@
         [decay_rates],
         [xs, gs, bc, sums, sums_t],
     )
+    gq_out, gk_far, gv_far = call(
+        cross_body,
+        [((rows + 16, width), BF), (wide, F32), (wide, F32)],
+        [],
+        [qg_next, k2, v2],
+        steps=steps,
+    )
     order = 1.0 / (rows * tm * lax.axis_size(("zl", "x", "c")))
     keep, give, mine, yours = call(
         lambda at_ref, *refs: carry_body(at_ref, order, *refs),
         [((rows // 2, width), BF)] * 2 + [((ny, nx, nz, 8, 2 * LANES), F32)] * 2,
         [at],
         [m1, m2, m3, rate_wide, gain_wide, bc_weight, gs, bc, scaled_x, scaled_g, leave, gx, gb, gc, x_t],
-        [qg_next],
+        [gq_out],
     )
     gx_far = lax.ppermute(give, "zh", flip)
 
@@ -442,26 +449,18 @@
     spread = lax.all_to_all(plane, ("zh", "zl"), 0, 0, tiled=True)
     grad_bc = jnp.sum(spread.astype(F32), axis=0)
 
-    gq_out, gk_far, gv_far = call(
-        cross_body,
-        [((rows + 16, width), BF), (wide, F32), (wide, F32)],
-        [],
-        [qg_next, k2, v2],
-        steps=steps,
-    )
     gq_far = lax.ppermute(gq_out, TM, to_next)
-    grad_x = call(unpack_body, [(wide, BF)], [at], [keep, gx_far], [chip])[0]
-    grad_x = grad_x.reshape(length, blocks, width)
     gq, gk, gv = call(
         own_body,
         [(wide, BF)] * 3,
         [at],
         [q2, k2, v2, g2, stats_own, gq_far, gk_far, gv_far],
-        [chip, grad_x],
+        [chip],
         steps=steps,
     )
     shape = (length, blocks, width)
-    return grad_x, gq.reshape(shape), gk.reshape(shape), gv.reshape(shape), grad_bc
+    grad_x = call(unpack_body, [(wide, BF)], [at], [keep, gx_far], [gk])[0]
+    return grad_x.reshape(shape), gq.reshape(shape), gk.reshape(shape), gv.reshape(shape), grad_bc
 
 
 def solution(mesh):

time: 175 us -> 165 us (0.943)
  waiting for transfers between devices: 38.7 us -> 23.9 us
  starting transfers between devices: 70.3 us -> 75.1 us
    ppermute x1, waiting for transfers between devices: 8.16 us -> 0.01 us  [local(): gx_far = lax.ppermute(give, 'zh', flip)]
    all_to_all x1, waiting for transfers between devices: 13.6 us -> 6.9 us  [local(): spread = lax.all_to_all(chip, ('y', 'x'), 0, 0, tiled=True)]
    all_to_all x1, starting transfers between devices: 11.2 us -> 16 us  [local(): spread = lax.all_to_all(plane, ('zh', 'zl'), 0, 0, tiled=True)]
    unnamed x34 -> x38, local copies, waits for them, and re-layouts: 3.95 us -> 4.58 us
  transfers between devices with their start and end apart: 10 -> 10, of which waited for: 4 -> 3; matrix products, arithmetic and copies ran while one was open for 7% -> 7% of each run, Pallas kernels for 20% -> 21%
where the time goes in v6:
time: 165 us; the launch traced here: 164 us
  starting transfers between devices  75.1 us (46%)
  Pallas kernels  43.2 us (26%)
  waiting for transfers between devices  23.9 us (14%)
  local copies, waits for them, and re-layouts  16.7 us (10%)
  other arithmetic  4.08 us (2%)
    pallas_call x9, Pallas kernels, call(): pl.pallas_call(run, out_shape=[jax.ShapeDtypeStruct(s, d) for s, d in out...  43.2 us
    ppermute x1, starting transfers between devices, local(): gq_far = lax.ppermute(gq_out, TM, to_next)  29.5 us
    all_to_all x1, starting transfers between devices, local(): spread = lax.all_to_all(plane, ('zh', 'zl'), 0, 0, tiled=True)  16 us
    ppermute x1, waiting for transfers between devices, local(): qg_next = lax.ppermute(qg, TM, to_prev)  14.9 us
    ppermute x3, starting transfers between devices, local(): lax.ppermute(m, 'y', [(i, (i + s) % ny) for i in range(ny)])  10.3 us
    ppermute x1, starting transfers between devices, local(): got = lax.ppermute(out, 'zh', flip)  7.18 us
    all_to_all x1, starting transfers between devices, local(): spread = lax.all_to_all(chip, ('y', 'x'), 0, 0, tiled=True)  7.14 us
    all_to_all x1, waiting for transfers between devices, local(): spread = lax.all_to_all(chip, ('y', 'x'), 0, 0, tiled=True)  6.9 us
  transfers between devices with their start and end apart: 10, of which 3 were waited for; matrix products, arithmetic and copies ran while one was open for 7% of the time, Pallas kernels for 21%

profile of v6, /device:TPU:2, one launch (start us, length us, event | category | flops | bytes accessed | tf_op | source)
XLA Modules:
  0.0 163.7 jit_solution(8800602850083953919)
XLA Ops:
  0.6 2.1 %reshape.44.refs_2_.refs_3_.refs_1_.refs_4_ = bf16[128,2048]{1,0:T(8,128)(2,1)} reshape(bf16[64,2,2048]{2,1,0:T(2,128)(2,1)} %param.17) | data formatting | bytes 1048576 | tf_op jit(solution)/shard_map/reshape | solution.py:389
  2.7 1.0 reshape.43.refs_1_
  3.7 0.6 pad_add_fusion.refs_0_
  4.4 2.5 %shard_map.128 = (bf16[64,4224]{1,0:T(8,128)(2,1)}, bf16[64,4224]{1,0:T(8,128)(2,1)}) custom-call(s32[4]{0:T(128)} %pad_add_fusion.refs_0_, bf16[128,2048]{1,0:T(8,128)(2,1)} %reshape.43.refs_1_, bf16[128,2048]{1,0:T(8,128)(2,1)} %reshape.44.refs_2_.refs_3_.refs_1_.refs_4_, s32[2,32,64]{2,1,0:T(8,128)} %bitcast.7), custom_call_target="tpu_custom_call" | custom-call | flops 1 | bytes 1 | tf_op jit(solution)/shard_map/pallas_call | solution.py:37
  6.9 7.2 %collective-permute-start = (bf16[64,4224]{1,0:T(8,128)(2,1)}, bf16[64,4224]{1,0:T(8,128)(2,1)S(1)}, u32[]{:S(2)}, u32[]{:S(2)}) collective-permute-start(bf16[64,4224]{1,0:T(8,128)(2,1)} %get-tuple-element.33), channel_id=1, source_target_pairs={{0,32},{32,0},{1,33},{33,1},{2,34},{34,2},{3,35},{35,3},{4,36},{36... | collective-permute-start | bytes 1622024 | tf_op jit(solution)/shard_map/ppermute | solution.py:398
  14.1 1.0 reshape.45.refs_0_.refs_1_
  15.0 1.0 reshape.46.refs_1_.refs_2_
  16.0 1.0 reshape.47.refs_2_.refs_3_
  17.0 4.1 %shard_map.129.refs_2_.refs_5_ = f32[4,16,128]{2,1,0:T(8,128)} custom-call(bf16[128,2048]{1,0:T(8,128)(2,1)} %reshape.45.refs_0_.refs_1_, bf16[128,2048]{1,0:T(8,128)(2,1)} %reshape.46.refs_1_.refs_2_, bf16[128,2048]{1,0:T(8,128)(2,1)} %reshape.47.refs_2_.refs_3_, bf16[128,2048]{1,0:T(8,128)(2,1)} %reshape.44.refs_2_.refs_3_.refs_1_.refs_4_), custom_call_target="tpu_custom_call" | custom-call | flops 1 | bytes 1 | tf_op jit(solution)/shard_map/pallas_call | solution.py:37
  21.1 3.5 %shard_map.130.refs_5_ = bf16[272,2048]{1,0:T(8,128)(2,1)} custom-call(bf16[128,2048]{1,0:T(8,128)(2,1)} %reshape.45.refs_0_.refs_1_, bf16[128,2048]{1,0:T(8,128)(2,1)} %reshape.44.refs_2_.refs_3_.refs_1_.refs_4_, f32[4,16,128]{2,1,0:T(8,128)} %shard_map.129.refs_2_.refs_5_), custom_call_target="tpu_custom_call" | custom-call | flops 1 | bytes 1 | tf_op jit(solution)/shard_map/pallas_call | solution.py:37
  24.7 1.3 collective-permute-start.4
  26.0 0.1 broadcast_in_dim.6
  26.0 0.7 broadcast_in_dim_reshape.6.refs_4_
  26.7 2.1 %collective-permute-done.refs_2_ = bf16[64,4224]{1,0:T(8,128)(2,1)S(1)} collective-permute-done((bf16[64,4224]{1,0:T(8,128)(2,1)}, bf16[64,4224]{1,0:T(8,128)(2,1)S(1)}, u32[]{:S(2)}, u32[]{:S(2)}) %collective-permute-start) | collective-permute-done | bytes 540704 | tf_op jit(solution)/shard_map/ppermute | solution.py:398
  28.8 0.8 copy-done.8
  29.6 5.9 %shard_map.131 = (bf16[128,2048]{1,0:T(8,128)(2,1)}, bf16[128,2048]{1,0:T(8,128)(2,1)}, bf16[128,256]{1,0:T(8,128)(2,1)}, f32[128,128]{1,0:T(8,128)}, f32[128,12...) custom-call(s32[4]{0:T(128)} %pad_add_fusion.refs_0_, ...), custom_call_target="tpu_custom_call" | custom-call | flops 1 | bytes 1 | tf_op jit(solution)/shard_map/pallas_call | solution.py:37
  35.5 6.1 %collective-permute-start.1 = (bf16[144,2048]{1,0:T(8,128)(2,1)}, bf16[144,2048]{1,0:T(8,128)(2,1)S(1)}, u32[]{:S(2)}, u32[]{:S(2)}) collective-permute-start(bf16[144,2048]{1,0:T(8,128)(2,1)} %get-tuple-element.34), channel_id=1, source_target_pairs={{0,64},{64,128},{128,192},{192,0},{1,65},{65,129},{129,193},{193,1... | collective-permute-start | bytes 1769480 | tf_op jit(solution)/shard_map/ppermute | solution.py:419
  41.7 2.8 %collective-permute-start.2 = (bf16[144,2048]{1,0:T(8,128)(2,1)}, bf16[144,2048]{1,0:T(8,128)(2,1)S(1)}, u32[]{:S(2)}, u32[]{:S(2)}) collective-permute-start(bf16[144,2048]{1,0:T(8,128)(2,1)} %get-tuple-element.35), channel_id=1, source_target_pairs={{0,128},{64,192},{128,0},{192,64},{1,129},{65,193},{129,1},{193,65... | collective-permute-start | bytes 1769480 | tf_op jit(solution)/shard_map/ppermute | solution.py:419
  44.5 1.4 collective-permute-start.3
  45.9 0.1 broadcast_in_dim.7
  46.0 0.7 broadcast_in_dim_reshape.7.refs_5_
  46.6 3.7 %shard_map.132 = (f32[128,2048]{1,0:T(8,128)}, f32[128,128]{1,0:T(8,128)}, f32[128,128]{1,0:T(8,128)}, bf16[2048,128]{1,0:T(8,128)(2,1)}) custom-call(f32[32]{0:T(128)} %refs_0_.1, bf16[128,2048]{1,0:T(8,128)(2,1)} %get-tuple-element.42.refs_1_, bf16[128,2048]{1,0:T(8,128)(2,1)} %get-tuple-element.37.refs_2_.refs_7_, ...), custom_call_target="tpu_custom_call" | custom-call | flops 1 | bytes 1 | tf_op jit(solution)/shard_map/pallas_call | solution.py:37
  50.3 14.9 %collective-permute-done.4.refs_0_ = bf16[272,2048]{1,0:T(8,128)(2,1)S(1)} collective-permute-done((bf16[272,2048]{1,0:T(8,128)(2,1)}, bf16[272,2048]{1,0:T(8,128)(2,1)S(1)}, u32[]{:S(2)}, u32[]{:S(2)}) %collective-permute-start.4) | collective-permute-done | bytes 1114144 | tf_op jit(solution)/shard_map/ppermute | solution.py:404
  65.2 1.0 copy-done.2
  66.2 7.3 %shard_map.133 = (bf16[144,2048]{1,0:T(8,128)(2,1)}, f32[128,2048]{1,0:T(8,128)}, f32[128,2048]{1,0:T(8,128)}) custom-call(bf16[272,2048]{1,0:T(8,128)(2,1)} %copy-done.2, bf16[128,2048]{1,0:T(8,128)(2,1)} %reshape.46.refs_1_.refs_2_, bf16[128,2048]{1,0:T(8,128)(2,1)} %reshape.47.refs_2_.refs_3_), custom_call_target="tpu_custom_call" | custom-call | flops 1 | bytes 1 | tf_op jit(solution)/shard_map/pallas_call | solution.py:37
  73.6 0.0 collective-permute-done.2.refs_2_
  73.6 0.8 copy-done.5
  74.5 0.2 copy-done.6
  74.6 0.2 copy-done.7
  74.8 6.5 %shard_map.134 = (bf16[64,2048]{1,0:T(8,128)(2,1)}, bf16[64,2048]{1,0:T(8,128)(2,1)}, f32[4,4,8,8,256]{4,3,2,1,0:T(8,128)}, f32[4,4,8,8,256]{4,3,2,1,0:T(8,128)}) custom-call(s32[4]{0:T(128)} %pad_add_fusion.refs_0_, bf16[144,2048]{1,0:T(8,128)(2,1)} %copy-done.5, bf16[144,2048]{1,0:T(8,128)(2,1)} %copy-done.6, bf16[144,2048]{1,0:T(8,128)(2,1)} %copy-done.7, ...), custom_call_target="tpu_custom_call" | custom-call | flops 1 | bytes 1 | tf_op jit(solution)/shard_map/pallas_call | solution.py:37
  81.4 0.0 collective-permute-start.7
  81.4 29.5 %collective-permute-start.6 = (bf16[144,2048]{1,0:T(8,128)(2,1)S(1)}, bf16[144,2048]{1,0:T(8,128)(2,1)S(1)}, u32[]{:S(2)}, u32[]{:S(2)}) collective-permute-start(bf16[144,2048]{1,0:T(8,128)(2,1)S(1)} %copy-done.4), channel_id=1, source_target_pairs={{0,32},{32,64},{64,96},{96,128},{128,160},{160,192},{192,224},{1,3... | collective-permute-start | bytes 1769480 | tf_op jit(solution)/shard_map/ppermute | solution.py:452
  110.9 2.2 %add_convert_fusion = bf16[4,4,8,8,256]{4,3,2,1,0:T(8,128)(2,1)} fusion(f32[4,4,8,8,256]{4,3,2,1,0:T(8,128)} %get-tuple-element.54, f32[4,4,8,8,256]{4,3,2,1,0:T(8,128)S(1)} %collective-permute-done.7), kind=kLoop, calls=%fused_computation | loop fusion | flops 524288 | bytes 2621440 | tf_op jit(solution)/shard_map/convert_element_type | solution.py:445
  113.1 7.1 %all-to-all-start = ((bf16[16,64,256]{2,1,0:T(8,128)(2,1)}), bf16[16,64,256]{2,1,0:T(8,128)(2,1)S(1)}, u32[]{:S(2)}, u32[]{:S(2)}) async-start(bf16[16,64,256]{2,1,0:T(8,128)(2,1)} %bitcast.5.refs_9_), calls=%async_computation | async-start | bytes 1048576 | tf_op jit(solution)/shard_map/all_to_all | solution.py:447
  120.3 3.6 %collective-permute-start.5 = (bf16[64,2048]{1,0:T(8,128)(2,1)S(1)}, bf16[64,2048]{1,0:T(8,128)(2,1)S(1)}, u32[]{:S(2)}, u32[]{:S(2)}) collective-permute-start(bf16[64,2048]{1,0:T(8,128)(2,1)S(1)} %copy-done.18), channel_id=1, source_target_pairs={{0,32},{32,0},{1,33},{33,1},{2,34},{34,2},{3,35},{35,3},{4,36},{36... | collective-permute-start | bytes 786440 | tf_op jit(solution)/shard_map/ppermute | solution.py:443
  123.9 6.9 %all-to-all-done = bf16[16,64,256]{2,1,0:T(8,128)(2,1)S(1)} async-done(((bf16[16,64,256]{2,1,0:T(8,128)(2,1)}), bf16[16,64,256]{2,1,0:T(8,128)(2,1)S(1)}, u32[]{:S(2)}, u32[]{:S(2)}) %all-to-all-start) | async-done | bytes 524320 | tf_op jit(solution)/shard_map/all_to_all | solution.py:447
  130.8 0.7 reduce_sum.21
  131.5 16.0 %all-to-all-start.1 = ((bf16[8,8,256]{2,1,0:T(8,128)(2,1)}), bf16[8,8,256]{2,1,0:T(8,128)(2,1)S(1)}, u32[]{:S(2)}, u32[]{:S(2)}) async-start(bf16[8,8,256]{2,1,0:T(8,128)(2,1)} %bitcast.6), calls=%async_computation.1 | async-start | bytes 65536 | tf_op jit(solution)/shard_map/all_to_all | solution.py:449
  147.5 0.8 copy-done.3
  148.3 7.2 %shard_map.135 = (bf16[128,2048]{1,0:T(8,128)(2,1)}, bf16[128,2048]{1,0:T(8,128)(2,1)}, bf16[128,2048]{1,0:T(8,128)(2,1)}) custom-call(s32[4]{0:T(128)} %pad_add_fusion.refs_0_, bf16[128,2048]{1,0:T(8,128)(2,1)} %reshape.45.refs_0_.refs_1_, bf16[128,2048]{1,0:T(8,128)(2,1)} %reshape.46.refs_1_.refs_2_, bf16[128,2048]{1,0:T(8,128)(2,1)} %reshape.47.refs_2_.refs_3_, ...), custom_call_target="tpu_custom_call" | custom-call | flops 1 | bytes 1 | tf_op jit(solution)/shard_map/pallas_call | solution.py:37
  155.5 0.0 copy-start.15
  155.5 0.7 copy-done.15
  156.2 2.2 %shard_map.136 = bf16[128,2048]{1,0:T(8,128)(2,1)} custom-call(s32[4]{0:T(128)} %pad_add_fusion.refs_0_, bf16[64,2048]{1,0:T(8,128)(2,1)} %get-tuple-element.50.refs_1_, bf16[64,2048]{1,0:T(8,128)(2,1)} %copy-done.15, bf16[128,2048]{1,0:T(8,128)(2,1)} %get-tuple-element.56.refs_3_), custom_call_target="tpu_custom_call" | custom-call | flops 1 | bytes 1 | tf_op jit(solution)/shard_map/pallas_call | solution.py:37
  158.5 1.1 reshape.51
  159.6 1.1 reshape.49
  160.8 1.1 reshape.50
  161.9 1.1 reshape.52
  163.0 0.6 convert_reduce_fusion
  (36 shorter events, 0.1 us)
Async XLA Ops:
  0.6 2.1 %copy-start.9 = (bf16[64,2,2048]{2,1,0:T(2,128)(2,1)S(1)}, bf16[64,2,2048]{2,1,0:T(2,128)(2,1)}, u32[]{:S(2)}) copy-start(bf16[64,2,2048]{2,1,0:T(2,128)(2,1)} %param.9) | copy-start | bytes 1572868
  2.7 11.3 %copy-start.10 = (bf16[64,2,2048]{2,1,0:T(2,128)(2,1)S(1)}, bf16[64,2,2048]{2,1,0:T(2,128)(2,1)}, u32[]{:S(2)}) copy-start(bf16[64,2,2048]{2,1,0:T(2,128)(2,1)} %param.14) | copy-start | bytes 1572868
  3.7 11.3 %copy-start.11 = (bf16[64,2,2048]{2,1,0:T(2,128)(2,1)S(1)}, bf16[64,2,2048]{2,1,0:T(2,128)(2,1)}, u32[]{:S(2)}) copy-start(bf16[64,2,2048]{2,1,0:T(2,128)(2,1)} %param.15) | copy-start | bytes 1572868
  6.9 9.2 %copy-start.12 = (bf16[64,2,2048]{2,1,0:T(2,128)(2,1)S(1)}, bf16[64,2,2048]{2,1,0:T(2,128)(2,1)}, u32[]{:S(2)}) copy-start(bf16[64,2,2048]{2,1,0:T(2,128)(2,1)} %param.16) | copy-start | bytes 1572868
  6.9 21.9 %collective-permute-start = (bf16[64,4224]{1,0:T(8,128)(2,1)}, bf16[64,4224]{1,0:T(8,128)(2,1)S(1)}, u32[]{:S(2)}, u32[]{:S(2)}) collective-permute-start(bf16[64,4224]{1,0:T(8,128)(2,1)} %get-tuple-element.33), channel_id=1, source_target_pairs={{0,32},{32,0},{1,33},{33,1},{2,34},{34,2},{3,35},{35,3},{4,36},{36... | collective-permute-start | bytes 1622024 | tf_op jit(solution)/shard_map/ppermute | solution.py:398
  21.1 4.8 %copy-start.16 = (f32[32]{0:T(128)S(1)}, f32[32]{0:T(128)}, u32[]{:S(2)}) copy-start(f32[32]{0:T(128)} %refs_0_.1) | copy-start | bytes 388
  24.7 40.5 %collective-permute-start.4 = (bf16[272,2048]{1,0:T(8,128)(2,1)}, bf16[272,2048]{1,0:T(8,128)(2,1)S(1)}, u32[]{:S(2)}, u32[]{:S(2)}) collective-permute-start(bf16[272,2048]{1,0:T(8,128)(2,1)} %shard_map.130.refs_5_), channel_id=1, source_target_pairs={{32,0},{64,32},{96,64},{128,96},{160,128},{192,160},{224,192},{33,... | collective-permute-start | bytes 3342344 | tf_op jit(solution)/shard_map/ppermute | solution.py:404
  28.8 0.8 copy-start.8
  29.6 16.3 %copy-start.17 = (f32[32]{0:T(128)S(1)}, f32[32]{0:T(128)}, u32[]{:S(2)}) copy-start(f32[32]{0:T(128)} %param.13) | copy-start | bytes 388
  35.5 38.0 %collective-permute-start.1 = (bf16[144,2048]{1,0:T(8,128)(2,1)}, bf16[144,2048]{1,0:T(8,128)(2,1)S(1)}, u32[]{:S(2)}, u32[]{:S(2)}) collective-permute-start(bf16[144,2048]{1,0:T(8,128)(2,1)} %get-tuple-element.34), channel_id=1, source_target_pairs={{0,64},{64,128},{128,192},{192,0},{1,65},{65,129},{129,193},{193,1... | collective-permute-start | bytes 1769480 | tf_op jit(solution)/shard_map/ppermute | solution.py:419
  41.7 31.9 %collective-permute-start.2 = (bf16[144,2048]{1,0:T(8,128)(2,1)}, bf16[144,2048]{1,0:T(8,128)(2,1)S(1)}, u32[]{:S(2)}, u32[]{:S(2)}) collective-permute-start(bf16[144,2048]{1,0:T(8,128)(2,1)} %get-tuple-element.35), channel_id=1, source_target_pairs={{0,128},{64,192},{128,0},{192,64},{1,129},{65,193},{129,1},{193,65... | collective-permute-start | bytes 1769480 | tf_op jit(solution)/shard_map/ppermute | solution.py:419
  44.5 29.1 %collective-permute-start.3 = (bf16[144,2048]{1,0:T(8,128)(2,1)}, bf16[144,2048]{1,0:T(8,128)(2,1)S(1)}, u32[]{:S(2)}, u32[]{:S(2)}) collective-permute-start(bf16[144,2048]{1,0:T(8,128)(2,1)} %get-tuple-element.36), channel_id=1, source_target_pairs={{0,192},{64,0},{128,64},{192,128},{1,193},{65,1},{129,65},{193,129... | collective-permute-start | bytes 1769480 | tf_op jit(solution)/shard_map/ppermute | solution.py:419
  65.2 1.0 copy-start.2
  73.6 0.9 copy-start.5
  73.6 1.0 copy-start.6
  73.6 1.2 copy-start.7
  74.8 6.5 %copy-start.4 = (bf16[144,2048]{1,0:T(8,128)(2,1)S(1)}, bf16[144,2048]{1,0:T(8,128)(2,1)}, u32[]{:S(2)}) copy-start(bf16[144,2048]{1,0:T(8,128)(2,1)} %get-tuple-element.49.refs_16_) | copy-start | bytes 1769476
  81.4 29.5 %collective-permute-start.7 = (f32[4,4,8,8,256]{4,3,2,1,0:T(8,128)}, f32[4,4,8,8,256]{4,3,2,1,0:T(8,128)S(1)}, u32[]{:S(2)}, u32[]{:S(2)}) collective-permute-start(f32[4,4,8,8,256]{4,3,2,1,0:T(8,128)} %get-tuple-element.55), channel_id=1, source_target_pairs={{0,1},{1,0},{2,3},{3,2},{4,5},{5,4},{6,7},{7,6},{8,9},{9,8},{10,11... | collective-permute-start | bytes 3145736 | tf_op jit(solution)/shard_map/ppermute | solution.py:445
  81.4 66.1 %collective-permute-start.6 = (bf16[144,2048]{1,0:T(8,128)(2,1)S(1)}, bf16[144,2048]{1,0:T(8,128)(2,1)S(1)}, u32[]{:S(2)}, u32[]{:S(2)}) collective-permute-start(bf16[144,2048]{1,0:T(8,128)(2,1)S(1)} %copy-done.4), channel_id=1, source_target_pairs={{0,32},{32,64},{64,96},{96,128},{128,160},{160,192},{192,224},{1,3... | collective-permute-start | bytes 1769480 | tf_op jit(solution)/shard_map/ppermute | solution.py:452
  110.9 9.3 %copy-start.18 = (bf16[64,2048]{1,0:T(8,128)(2,1)S(1)}, bf16[64,2048]{1,0:T(8,128)(2,1)}, u32[]{:S(2)}) copy-start(bf16[64,2048]{1,0:T(8,128)(2,1)} %get-tuple-element.51) | copy-start | bytes 786436
  113.1 17.7 %all-to-all-start = ((bf16[16,64,256]{2,1,0:T(8,128)(2,1)}), bf16[16,64,256]{2,1,0:T(8,128)(2,1)S(1)}, u32[]{:S(2)}, u32[]{:S(2)}) async-start(bf16[16,64,256]{2,1,0:T(8,128)(2,1)} %bitcast.5.refs_9_), calls=%async_computation | async-start | bytes 1048576 | tf_op jit(solution)/shard_map/all_to_all | solution.py:447
  120.3 35.3 %collective-permute-start.5 = (bf16[64,2048]{1,0:T(8,128)(2,1)S(1)}, bf16[64,2048]{1,0:T(8,128)(2,1)S(1)}, u32[]{:S(2)}, u32[]{:S(2)}) collective-permute-start(bf16[64,2048]{1,0:T(8,128)(2,1)S(1)} %copy-done.18), channel_id=1, source_target_pairs={{0,32},{32,0},{1,33},{33,1},{2,34},{34,2},{3,35},{35,3},{4,36},{36... | collective-permute-start | bytes 786440 | tf_op jit(solution)/shard_map/ppermute | solution.py:443
  131.5 31.6 %all-to-all-start.1 = ((bf16[8,8,256]{2,1,0:T(8,128)(2,1)}), bf16[8,8,256]{2,1,0:T(8,128)(2,1)S(1)}, u32[]{:S(2)}, u32[]{:S(2)}) async-start(bf16[8,8,256]{2,1,0:T(8,128)(2,1)} %bitcast.6), calls=%async_computation.1 | async-start | bytes 65536 | tf_op jit(solution)/shard_map/all_to_all | solution.py:449
  147.5 0.8 copy-start.3
  155.5 3.0 %copy-start = (bf16[128,2048]{1,0:T(8,128)(2,1)S(1)}, bf16[128,2048]{1,0:T(8,128)(2,1)}, u32[]{:S(2)}) copy-start(bf16[128,2048]{1,0:T(8,128)(2,1)} %get-tuple-element.56.refs_3_) | copy-start | bytes 1572868
  155.5 0.7 copy-start.15
  158.5 1.1 copy-start.1
  158.5 2.3 %copy-start.14 = (bf16[128,2048]{1,0:T(8,128)(2,1)S(1)}, bf16[128,2048]{1,0:T(8,128)(2,1)}, u32[]{:S(2)}) copy-start(bf16[128,2048]{1,0:T(8,128)(2,1)} %get-tuple-element.57) | copy-start | bytes 1572868
  159.6 2.3 %copy-start.13 = (bf16[128,2048]{1,0:T(8,128)(2,1)S(1)}, bf16[128,2048]{1,0:T(8,128)(2,1)}, u32[]{:S(2)}) copy-start(bf16[128,2048]{1,0:T(8,128)(2,1)} %get-tuple-element.58) | copy-start | bytes 1572868

commit v7 on v6

--- a/solution.py
+++ b/solution.py
@@ -160,7 +160,7 @@
     sg = (gs[...].astype(F32) * growth).astype(BF)
     scaled_x[...] = sx
     scaled_g[...] = sg
-    leave[...] = to_end
+    leave[...] = to_end.astype(BF)
     state = (tn(bc_rows[:, :LANES], sx) * INJECT).astype(BF)
     back = tn(bc_rows[:, LANES:], sg).astype(BF)
     tail = jnp.concatenate(lasts + [jnp.zeros((13, width), F32)], axis=0).astype(BF)
@@ -196,7 +196,7 @@
             decay = jnp.exp(jnp.where(ahead, gap * (rate[h] * (-1.0 / CODE_UNIT)), LOW))
             mixing = mixing + decay * both[k * rows : (k + 1) * rows]
             parts.append((decay * kernel).astype(BF))
-        gx[:, at] = nn(jnp.concatenate(parts, axis=1), halves(g_pair))
+        gx[:, at] = nn(jnp.concatenate(parts, axis=1), halves(g_pair)).astype(BF)
         x_t[at, :] = x_pair.astype(F32).T.astype(BF)
     mixed = (mixing * INJECT).astype(BF)
     gb[...] = nn(mixed, c_rows)
@@ -228,7 +228,7 @@
     b_cot = gb[...] + nt(scaled_x[...], back) * INJECT
     c_cot = gc[...] + nt(scaled_g[...], state)
     cot = jnp.concatenate([b_cot, c_cot], axis=1).astype(BF)
-    out = gx[...] + leave[...] * (nn(bc[:, :LANES], back) * INJECT)
+    out = gx[...].astype(F32) + leave[...].astype(F32) * (nn(bc[:, :LANES], back) * INJECT)
     out = out + gs[...].astype(F32) * gain[...] + nt(cot, w[...])
 
     @pl.when(z == 0)
@@ -248,8 +248,8 @@
         @pl.when(core == side)
         def _():
             for x in range(4):
-                mine[:, x] = grad[:, :, x, side]
-                yours[:, x] = grad[:, :, x, 1 - side]
+                for ref, c in ((mine, side), (yours, 1 - side)):
+                    ref[:, x] = grad[:, :, x, c].reshape(4, 64, 2 * LANES).astype(BF)
 
 
 def unpack_body(at, keep, far, out):
@@ -337,8 +337,8 @@
             ds.append((prob * (d - delta)).astype(BF))
         a, b, c = products(ps, ds, q_pair, k_pair, g_pair)
         gq[:rows, at] = a.astype(BF)
-        gk[:, at] = b
-        gv[:, at] = c
+        gk[:, at] = b.astype(BF)
+        gv[:, at] = c.astype(BF)
     add_pieces(jnp.concatenate(logs + deltas, axis=0), gq, rows)
 
 
@@ -367,8 +367,8 @@
             ds.append((prob * (d - delta)).astype(BF))
         a, b, c = products(ps, ds, q_pair, k_pair, g_pair)
         gq[:, at] = (a + gq_far[:rows, at].astype(F32)).astype(BF)
-        gk[:, at] = (b + gk_far[:, at]).astype(BF)
-        gv[:, at] = (c + gv_far[:, at]).astype(BF)
+        gk[:, at] = (b + gk_far[:, at].astype(F32)).astype(BF)
+        gv[:, at] = (c + gv_far[:, at].astype(F32)).astype(BF)
 
 
 def local(
@@ -409,7 +409,7 @@
     xs, gs, bc, sums, sums_t, scaled_x, scaled_g, leave, m1, m2, m3 = call(
         summary_body,
         [(wide, BF), (wide, BF), ((rows, 2 * LANES), BF), (square, F32), (square, F32)]
-        + [(wide, BF), (wide, BF), (wide, F32)]
+        + [(wide, BF)] * 3
         + [(state, BF)] * 3,
         [at],
         [own, got, bc_weight, rate_wide],
@@ -421,13 +421,13 @@
     )
     gx, gb, gc, x_t = call(
         inner_body,
-        [(wide, F32), (square, F32), (square, F32), ((width, rows), BF)],
+        [(wide, BF), (square, F32), (square, F32), ((width, rows), BF)],
         [decay_rates],
         [xs, gs, bc, sums, sums_t],
     )
     gq_out, gk_far, gv_far = call(
         cross_body,
-        [((rows + 16, width), BF), (wide, F32), (wide, F32)],
+        [((rows + 16, width), BF), (wide, BF), (wide, BF)],
         [],
         [qg_next, k2, v2],
         steps=steps,
@@ -435,14 +435,14 @@
     order = 1.0 / (rows * tm * lax.axis_size(("zl", "x", "c")))
     keep, give, mine, yours = call(
         lambda at_ref, *refs: carry_body(at_ref, order, *refs),
-        [((rows // 2, width), BF)] * 2 + [((ny, nx, nz, 8, 2 * LANES), F32)] * 2,
+        [((rows // 2, width), BF)] * 2 + [((ny, nx, nz * 8, 2 * LANES), BF)] * 2,
         [at],
         [m1, m2, m3, rate_wide, gain_wide, bc_weight, gs, bc, scaled_x, scaled_g, leave, gx, gb, gc, x_t],
         [gq_out],
     )
     gx_far = lax.ppermute(give, "zh", flip)
 
-    chip = (mine + lax.ppermute(yours, "c", flip)).astype(BF)
+    chip = (mine.astype(F32) + lax.ppermute(yours, "c", flip).astype(F32)).astype(BF)
     chip = chip.reshape(ny * nx, nz * 8, 2 * LANES)
     spread = lax.all_to_all(chip, ("y", "x"), 0, 0, tiled=True)
     plane = jnp.sum(spread.astype(F32), axis=0).astype(BF).reshape(nz, 8, 2 * LANES)

time: 165 us -> 164 us (level)
  no operation moved by 1% of the time
where the time goes in v7:
time: 164 us; the launch traced here: 163 us
  starting transfers between devices  75.8 us (46%)
  Pallas kernels  41.9 us (26%)
  waiting for transfers between devices  24.2 us (15%)
  local copies, waits for them, and re-layouts  16.6 us (10%)
  other arithmetic  3.92 us (2%)
    pallas_call x9, Pallas kernels, call(): pl.pallas_call(run, out_shape=[jax.ShapeDtypeStruct(s, d) for s, d in out...  41.9 us
    ppermute x1, starting transfers between devices, local(): gq_far = lax.ppermute(gq_out, TM, to_next)  29.5 us
    all_to_all x1, starting transfers between devices, local(): spread = lax.all_to_all(plane, ('zh', 'zl'), 0, 0, tiled=True)  16.6 us
    ppermute x1, waiting for transfers between devices, local(): qg_next = lax.ppermute(qg, TM, to_prev)  15.2 us
    ppermute x3, starting transfers between devices, local(): lax.ppermute(m, 'y', [(i, (i + s) % ny) for i in range(ny)])  10.4 us
    ppermute x1, starting transfers between devices, local(): got = lax.ppermute(out, 'zh', flip)  7.2 us
    all_to_all x1, starting transfers between devices, local(): spread = lax.all_to_all(chip, ('y', 'x'), 0, 0, tiled=True)  7.15 us
    all_to_all x1, waiting for transfers between devices, local(): spread = lax.all_to_all(chip, ('y', 'x'), 0, 0, tiled=True)  6.91 us
  transfers between devices with their start and end apart: 10, of which 3 were waited for; matrix products, arithmetic and copies ran while one was open for 7% of the time, Pallas kernels for 21%

profile of v7, /device:TPU:2, one launch (start us, length us, event | category | flops | bytes accessed | tf_op | source)
XLA Modules:
  0.0 163.2 jit_solution(868385460839777161)
XLA Ops:
  0.6 2.1 %reshape.44.refs_2_.refs_3_.refs_1_.refs_4_ = bf16[128,2048]{1,0:T(8,128)(2,1)} reshape(bf16[64,2,2048]{2,1,0:T(2,128)(2,1)} %param.17) | data formatting | bytes 1048576 | tf_op jit(solution)/shard_map/reshape | solution.py:389
  2.7 1.0 reshape.43.refs_1_
  3.7 0.6 pad_add_fusion.refs_0_
  4.3 2.5 %shard_map.128 = (bf16[64,4224]{1,0:T(8,128)(2,1)}, bf16[64,4224]{1,0:T(8,128)(2,1)}) custom-call(s32[4]{0:T(128)} %pad_add_fusion.refs_0_, bf16[128,2048]{1,0:T(8,128)(2,1)} %reshape.43.refs_1_, bf16[128,2048]{1,0:T(8,128)(2,1)} %reshape.44.refs_2_.refs_3_.refs_1_.refs_4_, s32[2,32,64]{2,1,0:T(8,128)} %bitcast.7), custom_call_target="tpu_custom_call" | custom-call | flops 1 | bytes 1 | tf_op jit(solution)/shard_map/pallas_call | solution.py:37
  6.8 7.2 %collective-permute-start = (bf16[64,4224]{1,0:T(8,128)(2,1)}, bf16[64,4224]{1,0:T(8,128)(2,1)S(1)}, u32[]{:S(2)}, u32[]{:S(2)}) collective-permute-start(bf16[64,4224]{1,0:T(8,128)(2,1)} %get-tuple-element.33), channel_id=1, source_target_pairs={{0,32},{32,0},{1,33},{33,1},{2,34},{34,2},{3,35},{35,3},{4,36},{36... | collective-permute-start | bytes 1622024 | tf_op jit(solution)/shard_map/ppermute | solution.py:398
  14.0 1.0 reshape.45.refs_0_.refs_1_
  15.0 1.0 reshape.46.refs_1_.refs_2_
  16.0 1.0 reshape.47.refs_2_.refs_3_
  17.0 4.1 %shard_map.129.refs_2_.refs_5_ = f32[4,16,128]{2,1,0:T(8,128)} custom-call(bf16[128,2048]{1,0:T(8,128)(2,1)} %reshape.45.refs_0_.refs_1_, bf16[128,2048]{1,0:T(8,128)(2,1)} %reshape.46.refs_1_.refs_2_, bf16[128,2048]{1,0:T(8,128)(2,1)} %reshape.47.refs_2_.refs_3_, bf16[128,2048]{1,0:T(8,128)(2,1)} %reshape.44.refs_2_.refs_3_.refs_1_.refs_4_), custom_call_target="tpu_custom_call" | custom-call | flops 1 | bytes 1 | tf_op jit(solution)/shard_map/pallas_call | solution.py:37
  21.1 3.5 %shard_map.130.refs_5_ = bf16[272,2048]{1,0:T(8,128)(2,1)} custom-call(bf16[128,2048]{1,0:T(8,128)(2,1)} %reshape.45.refs_0_.refs_1_, bf16[128,2048]{1,0:T(8,128)(2,1)} %reshape.44.refs_2_.refs_3_.refs_1_.refs_4_, f32[4,16,128]{2,1,0:T(8,128)} %shard_map.129.refs_2_.refs_5_), custom_call_target="tpu_custom_call" | custom-call | flops 1 | bytes 1 | tf_op jit(solution)/shard_map/pallas_call | solution.py:37
  24.7 1.3 collective-permute-start.4
  26.0 0.1 broadcast_in_dim.6
  26.0 0.7 broadcast_in_dim_reshape.6.refs_4_
  26.7 2.0 %collective-permute-done.refs_2_ = bf16[64,4224]{1,0:T(8,128)(2,1)S(1)} collective-permute-done((bf16[64,4224]{1,0:T(8,128)(2,1)}, bf16[64,4224]{1,0:T(8,128)(2,1)S(1)}, u32[]{:S(2)}, u32[]{:S(2)}) %collective-permute-start) | collective-permute-done | bytes 540704 | tf_op jit(solution)/shard_map/ppermute | solution.py:398
  28.8 0.8 copy-done.8
  29.6 5.8 %shard_map.131 = (bf16[128,2048]{1,0:T(8,128)(2,1)}, bf16[128,2048]{1,0:T(8,128)(2,1)}, bf16[128,256]{1,0:T(8,128)(2,1)}, f32[128,128]{1,0:T(8,128)}, f32[128,12...) custom-call(s32[4]{0:T(128)} %pad_add_fusion.refs_0_, ...), custom_call_target="tpu_custom_call" | custom-call | flops 1 | bytes 1 | tf_op jit(solution)/shard_map/pallas_call | solution.py:37
  35.3 6.2 %collective-permute-start.1 = (bf16[144,2048]{1,0:T(8,128)(2,1)}, bf16[144,2048]{1,0:T(8,128)(2,1)S(1)}, u32[]{:S(2)}, u32[]{:S(2)}) collective-permute-start(bf16[144,2048]{1,0:T(8,128)(2,1)} %get-tuple-element.34), channel_id=1, source_target_pairs={{0,64},{64,128},{128,192},{192,0},{1,65},{65,129},{129,193},{193,1... | collective-permute-start | bytes 1769480 | tf_op jit(solution)/shard_map/ppermute | solution.py:419
  41.5 2.9 %collective-permute-start.2 = (bf16[144,2048]{1,0:T(8,128)(2,1)}, bf16[144,2048]{1,0:T(8,128)(2,1)S(1)}, u32[]{:S(2)}, u32[]{:S(2)}) collective-permute-start(bf16[144,2048]{1,0:T(8,128)(2,1)} %get-tuple-element.35), channel_id=1, source_target_pairs={{0,128},{64,192},{128,0},{192,64},{1,129},{65,193},{129,1},{193,65... | collective-permute-start | bytes 1769480 | tf_op jit(solution)/shard_map/ppermute | solution.py:419
  44.4 1.4 collective-permute-start.3
  45.7 0.1 broadcast_in_dim.7
  45.8 0.7 broadcast_in_dim_reshape.7.refs_5_
  46.5 3.5 %shard_map.132 = (bf16[128,2048]{1,0:T(8,128)(2,1)}, f32[128,128]{1,0:T(8,128)}, f32[128,128]{1,0:T(8,128)}, bf16[2048,128]{1,0:T(8,128)(2,1)}) custom-call(f32[32]{0:T(128)} %refs_0_.1, bf16[128,2048]{1,0:T(8,128)(2,1)} %get-tuple-element.42.refs_1_, bf16[128,2048]{1,0:T(8,128)(2,1)} %get-tuple-element.37.refs_2_.refs_7_, ...), custom_call_target="tpu_custom_call" | custom-call | flops 1 | bytes 1 | tf_op jit(solution)/shard_map/pallas_call | solution.py:37
  50.0 15.2 %collective-permute-done.4.refs_0_ = bf16[272,2048]{1,0:T(8,128)(2,1)S(1)} collective-permute-done((bf16[272,2048]{1,0:T(8,128)(2,1)}, bf16[272,2048]{1,0:T(8,128)(2,1)S(1)}, u32[]{:S(2)}, u32[]{:S(2)}) %collective-permute-start.4) | collective-permute-done | bytes 1114144 | tf_op jit(solution)/shard_map/ppermute | solution.py:404
  65.2 1.0 copy-done.2
  66.2 7.2 %shard_map.133 = (bf16[144,2048]{1,0:T(8,128)(2,1)}, bf16[128,2048]{1,0:T(8,128)(2,1)}, bf16[128,2048]{1,0:T(8,128)(2,1)}) custom-call(bf16[272,2048]{1,0:T(8,128)(2,1)} %copy-done.2, bf16[128,2048]{1,0:T(8,128)(2,1)} %reshape.46.refs_1_.refs_2_, bf16[128,2048]{1,0:T(8,128)(2,1)} %reshape.47.refs_2_.refs_3_), custom_call_target="tpu_custom_call" | custom-call | flops 1 | bytes 1 | tf_op jit(solution)/shard_map/pallas_call | solution.py:37
  73.5 0.0 collective-permute-done.1.refs_1_
  73.5 0.0 collective-permute-done.3.refs_3_
  73.5 0.8 copy-done.5
  74.3 0.2 copy-done.6
  74.5 0.2 copy-done.7
  74.7 5.9 %shard_map.134 = (bf16[64,2048]{1,0:T(8,128)(2,1)}, bf16[64,2048]{1,0:T(8,128)(2,1)}, bf16[4,4,64,256]{3,2,1,0:T(8,128)(2,1)}, bf16[4,4,64,256]{3,2,1,0:T(8,128)(2,1)}) custom-call(s32[4]{0:T(128)} %pad_add_fusion.refs_0_, bf16[144,2048]{1,0:T(8,128)(2,1)} %copy-done.5, bf16[144,2048]{1,0:T(8,128)(2,1)} %copy-done.6, bf16[144,2048]{1,0:T(8,128)(2,1)} %copy-done.7, ...), custom_call_target="tpu_custom_call" | custom-call | flops 1 | bytes 1 | tf_op jit(solution)/shard_map/pallas_call | solution.py:37
  80.6 29.5 %collective-permute-start.6 = (bf16[144,2048]{1,0:T(8,128)(2,1)S(1)}, bf16[144,2048]{1,0:T(8,128)(2,1)S(1)}, u32[]{:S(2)}, u32[]{:S(2)}) collective-permute-start(bf16[144,2048]{1,0:T(8,128)(2,1)S(1)} %copy-done.4), channel_id=1, source_target_pairs={{0,32},{32,64},{64,96},{96,128},{128,160},{160,192},{192,224},{1,3... | collective-permute-start | bytes 1769480 | tf_op jit(solution)/shard_map/ppermute | solution.py:452
  110.2 2.0 %add_convert_fusion = bf16[4,4,64,256]{3,2,1,0:T(8,128)(2,1)} fusion(bf16[4,4,64,256]{3,2,1,0:T(8,128)(2,1)S(1)} %collective-permute-done.7, bf16[4,4,64,256]{3,2,1,0:T(8,128)(2,1)} %get-tuple-element.54), kind=kLoop, calls=%fused_computation | loop fusion | flops 1048576 | bytes 1572864 | tf_op jit(solution)/shard_map/convert_element_type | solution.py:445
  112.2 7.1 %all-to-all-start = ((bf16[16,64,256]{2,1,0:T(8,128)(2,1)}), bf16[16,64,256]{2,1,0:T(8,128)(2,1)S(1)}, u32[]{:S(2)}, u32[]{:S(2)}) async-start(bf16[16,64,256]{2,1,0:T(8,128)(2,1)} %bitcast.5.refs_9_), calls=%async_computation | async-start | bytes 1048576 | tf_op jit(solution)/shard_map/all_to_all | solution.py:447
  119.3 3.6 %collective-permute-start.5 = (bf16[64,2048]{1,0:T(8,128)(2,1)S(1)}, bf16[64,2048]{1,0:T(8,128)(2,1)S(1)}, u32[]{:S(2)}, u32[]{:S(2)}) collective-permute-start(bf16[64,2048]{1,0:T(8,128)(2,1)S(1)} %copy-done.18), channel_id=1, source_target_pairs={{0,32},{32,0},{1,33},{33,1},{2,34},{34,2},{3,35},{35,3},{4,36},{36... | collective-permute-start | bytes 786440 | tf_op jit(solution)/shard_map/ppermute | solution.py:443
  123.0 6.9 %all-to-all-done = bf16[16,64,256]{2,1,0:T(8,128)(2,1)S(1)} async-done(((bf16[16,64,256]{2,1,0:T(8,128)(2,1)}), bf16[16,64,256]{2,1,0:T(8,128)(2,1)S(1)}, u32[]{:S(2)}, u32[]{:S(2)}) %all-to-all-start) | async-done | bytes 524320 | tf_op jit(solution)/shard_map/all_to_all | solution.py:447
  129.9 0.7 reduce_sum.21
  130.6 16.6 %all-to-all-start.1 = ((bf16[8,8,256]{2,1,0:T(8,128)(2,1)}), bf16[8,8,256]{2,1,0:T(8,128)(2,1)S(1)}, u32[]{:S(2)}, u32[]{:S(2)}) async-start(bf16[8,8,256]{2,1,0:T(8,128)(2,1)} %bitcast.6), calls=%async_computation.1 | async-start | bytes 65536 | tf_op jit(solution)/shard_map/all_to_all | solution.py:449
  147.2 0.8 copy-done.3
  148.0 7.0 %shard_map.135 = (bf16[128,2048]{1,0:T(8,128)(2,1)}, bf16[128,2048]{1,0:T(8,128)(2,1)}, bf16[128,2048]{1,0:T(8,128)(2,1)}) custom-call(s32[4]{0:T(128)} %pad_add_fusion.refs_0_, bf16[128,2048]{1,0:T(8,128)(2,1)} %reshape.45.refs_0_.refs_1_, bf16[128,2048]{1,0:T(8,128)(2,1)} %reshape.46.refs_1_.refs_2_, bf16[128,2048]{1,0:T(8,128)(2,1)} %reshape.47.refs_2_.refs_3_, ...), custom_call_target="tpu_custom_call" | custom-call | flops 1 | bytes 1 | tf_op jit(solution)/shard_map/pallas_call | solution.py:37
  155.1 0.0 copy-start.15
  155.1 0.7 copy-done.15
  155.8 2.2 %shard_map.136 = bf16[128,2048]{1,0:T(8,128)(2,1)} custom-call(s32[4]{0:T(128)} %pad_add_fusion.refs_0_, bf16[64,2048]{1,0:T(8,128)(2,1)} %get-tuple-element.50.refs_1_, bf16[64,2048]{1,0:T(8,128)(2,1)} %copy-done.15, bf16[128,2048]{1,0:T(8,128)(2,1)} %get-tuple-element.56.refs_3_), custom_call_target="tpu_custom_call" | custom-call | flops 1 | bytes 1 | tf_op jit(solution)/shard_map/pallas_call | solution.py:37
  158.0 1.1 reshape.51
  159.2 1.1 reshape.49
  160.3 1.1 reshape.50
  161.5 1.1 reshape.52
  162.6 0.6 convert_reduce_fusion
  (36 shorter events, 0.1 us)
Async XLA Ops:
  0.6 2.1 %copy-start.9 = (bf16[64,2,2048]{2,1,0:T(2,128)(2,1)S(1)}, bf16[64,2,2048]{2,1,0:T(2,128)(2,1)}, u32[]{:S(2)}) copy-start(bf16[64,2,2048]{2,1,0:T(2,128)(2,1)} %param.9) | copy-start | bytes 1572868
  2.7 11.3 %copy-start.10 = (bf16[64,2,2048]{2,1,0:T(2,128)(2,1)S(1)}, bf16[64,2,2048]{2,1,0:T(2,128)(2,1)}, u32[]{:S(2)}) copy-start(bf16[64,2,2048]{2,1,0:T(2,128)(2,1)} %param.14) | copy-start | bytes 1572868
  3.7 11.3 %copy-start.11 = (bf16[64,2,2048]{2,1,0:T(2,128)(2,1)S(1)}, bf16[64,2,2048]{2,1,0:T(2,128)(2,1)}, u32[]{:S(2)}) copy-start(bf16[64,2,2048]{2,1,0:T(2,128)(2,1)} %param.15) | copy-start | bytes 1572868
  6.8 9.2 %copy-start.12 = (bf16[64,2,2048]{2,1,0:T(2,128)(2,1)S(1)}, bf16[64,2,2048]{2,1,0:T(2,128)(2,1)}, u32[]{:S(2)}) copy-start(bf16[64,2,2048]{2,1,0:T(2,128)(2,1)} %param.16) | copy-start | bytes 1572868
  6.8 21.9 %collective-permute-start = (bf16[64,4224]{1,0:T(8,128)(2,1)}, bf16[64,4224]{1,0:T(8,128)(2,1)S(1)}, u32[]{:S(2)}, u32[]{:S(2)}) collective-permute-start(bf16[64,4224]{1,0:T(8,128)(2,1)} %get-tuple-element.33), channel_id=1, source_target_pairs={{0,32},{32,0},{1,33},{33,1},{2,34},{34,2},{3,35},{35,3},{4,36},{36... | collective-permute-start | bytes 1622024 | tf_op jit(solution)/shard_map/ppermute | solution.py:398
  21.1 4.8 %copy-start.16 = (f32[32]{0:T(128)S(1)}, f32[32]{0:T(128)}, u32[]{:S(2)}) copy-start(f32[32]{0:T(128)} %refs_0_.1) | copy-start | bytes 388
  24.7 40.6 %collective-permute-start.4 = (bf16[272,2048]{1,0:T(8,128)(2,1)}, bf16[272,2048]{1,0:T(8,128)(2,1)S(1)}, u32[]{:S(2)}, u32[]{:S(2)}) collective-permute-start(bf16[272,2048]{1,0:T(8,128)(2,1)} %shard_map.130.refs_5_), channel_id=1, source_target_pairs={{32,0},{64,32},{96,64},{128,96},{160,128},{192,160},{224,192},{33,... | collective-permute-start | bytes 3342344 | tf_op jit(solution)/shard_map/ppermute | solution.py:404
  28.8 0.8 copy-start.8
  29.6 16.2 %copy-start.17 = (f32[32]{0:T(128)S(1)}, f32[32]{0:T(128)}, u32[]{:S(2)}) copy-start(f32[32]{0:T(128)} %param.13) | copy-start | bytes 388
  35.3 38.1 %collective-permute-start.1 = (bf16[144,2048]{1,0:T(8,128)(2,1)}, bf16[144,2048]{1,0:T(8,128)(2,1)S(1)}, u32[]{:S(2)}, u32[]{:S(2)}) collective-permute-start(bf16[144,2048]{1,0:T(8,128)(2,1)} %get-tuple-element.34), channel_id=1, source_target_pairs={{0,64},{64,128},{128,192},{192,0},{1,65},{65,129},{129,193},{193,1... | collective-permute-start | bytes 1769480 | tf_op jit(solution)/shard_map/ppermute | solution.py:419
  41.5 32.0 %collective-permute-start.2 = (bf16[144,2048]{1,0:T(8,128)(2,1)}, bf16[144,2048]{1,0:T(8,128)(2,1)S(1)}, u32[]{:S(2)}, u32[]{:S(2)}) collective-permute-start(bf16[144,2048]{1,0:T(8,128)(2,1)} %get-tuple-element.35), channel_id=1, source_target_pairs={{0,128},{64,192},{128,0},{192,64},{1,129},{65,193},{129,1},{193,65... | collective-permute-start | bytes 1769480 | tf_op jit(solution)/shard_map/ppermute | solution.py:419
  44.4 29.1 %collective-permute-start.3 = (bf16[144,2048]{1,0:T(8,128)(2,1)}, bf16[144,2048]{1,0:T(8,128)(2,1)S(1)}, u32[]{:S(2)}, u32[]{:S(2)}) collective-permute-start(bf16[144,2048]{1,0:T(8,128)(2,1)} %get-tuple-element.36), channel_id=1, source_target_pairs={{0,192},{64,0},{128,64},{192,128},{1,193},{65,1},{129,65},{193,129... | collective-permute-start | bytes 1769480 | tf_op jit(solution)/shard_map/ppermute | solution.py:419
  65.2 1.0 copy-start.2
  73.5 0.8 copy-start.5
  73.5 1.0 copy-start.6
  73.5 1.2 copy-start.7
  74.7 5.9 %copy-start.4 = (bf16[144,2048]{1,0:T(8,128)(2,1)S(1)}, bf16[144,2048]{1,0:T(8,128)(2,1)}, u32[]{:S(2)}) copy-start(bf16[144,2048]{1,0:T(8,128)(2,1)} %get-tuple-element.49.refs_16_) | copy-start | bytes 1769476
  80.6 29.5 %collective-permute-start.7 = (bf16[4,4,64,256]{3,2,1,0:T(8,128)(2,1)}, bf16[4,4,64,256]{3,2,1,0:T(8,128)(2,1)S(1)}, u32[]{:S(2)}, u32[]{:S(2)}) collective-permute-start(bf16[4,4,64,256]{3,2,1,0:T(8,128)(2,1)} %get-tuple-element.55), channel_id=1, source_target_pairs={{0,1},{1,0},{2,3},{3,2},{4,5},{5,4},{6,7},{7,6},{8,9},{9,8},{10,11... | collective-permute-start | bytes 1572872 | tf_op jit(solution)/shard_map/ppermute | solution.py:445
  80.6 66.6 %collective-permute-start.6 = (bf16[144,2048]{1,0:T(8,128)(2,1)S(1)}, bf16[144,2048]{1,0:T(8,128)(2,1)S(1)}, u32[]{:S(2)}, u32[]{:S(2)}) collective-permute-start(bf16[144,2048]{1,0:T(8,128)(2,1)S(1)} %copy-done.4), channel_id=1, source_target_pairs={{0,32},{32,64},{64,96},{96,128},{128,160},{160,192},{192,224},{1,3... | collective-permute-start | bytes 1769480 | tf_op jit(solution)/shard_map/ppermute | solution.py:452
  110.2 9.2 %copy-start.18 = (bf16[64,2048]{1,0:T(8,128)(2,1)S(1)}, bf16[64,2048]{1,0:T(8,128)(2,1)}, u32[]{:S(2)}) copy-start(bf16[64,2048]{1,0:T(8,128)(2,1)} %get-tuple-element.51) | copy-start | bytes 786436
  112.2 17.7 %all-to-all-start = ((bf16[16,64,256]{2,1,0:T(8,128)(2,1)}), bf16[16,64,256]{2,1,0:T(8,128)(2,1)S(1)}, u32[]{:S(2)}, u32[]{:S(2)}) async-start(bf16[16,64,256]{2,1,0:T(8,128)(2,1)} %bitcast.5.refs_9_), calls=%async_computation | async-start | bytes 1048576 | tf_op jit(solution)/shard_map/all_to_all | solution.py:447
  119.3 35.7 %collective-permute-start.5 = (bf16[64,2048]{1,0:T(8,128)(2,1)S(1)}, bf16[64,2048]{1,0:T(8,128)(2,1)S(1)}, u32[]{:S(2)}, u32[]{:S(2)}) collective-permute-start(bf16[64,2048]{1,0:T(8,128)(2,1)S(1)} %copy-done.18), channel_id=1, source_target_pairs={{0,32},{32,0},{1,33},{33,1},{2,34},{34,2},{3,35},{35,3},{4,36},{36... | collective-permute-start | bytes 786440 | tf_op jit(solution)/shard_map/ppermute | solution.py:443
  130.6 32.0 %all-to-all-start.1 = ((bf16[8,8,256]{2,1,0:T(8,128)(2,1)}), bf16[8,8,256]{2,1,0:T(8,128)(2,1)S(1)}, u32[]{:S(2)}, u32[]{:S(2)}) async-start(bf16[8,8,256]{2,1,0:T(8,128)(2,1)} %bitcast.6), calls=%async_computation.1 | async-start | bytes 65536 | tf_op jit(solution)/shard_map/all_to_all | solution.py:449
  147.2 0.8 copy-start.3
  155.1 3.0 %copy-start = (bf16[128,2048]{1,0:T(8,128)(2,1)S(1)}, bf16[128,2048]{1,0:T(8,128)(2,1)}, u32[]{:S(2)}) copy-start(bf16[128,2048]{1,0:T(8,128)(2,1)} %get-tuple-element.56.refs_3_) | copy-start | bytes 1572868
  155.1 0.7 copy-start.15
  158.0 1.1 copy-start.1
  158.0 2.3 %copy-start.14 = (bf16[128,2048]{1,0:T(8,128)(2,1)S(1)}, bf16[128,2048]{1,0:T(8,128)(2,1)}, u32[]{:S(2)}) copy-start(bf16[128,2048]{1,0:T(8,128)(2,1)} %get-tuple-element.57) | copy-start | bytes 1572868
  159.2 2.3 %copy-start.13 = (bf16[128,2048]{1,0:T(8,128)(2,1)S(1)}, bf16[128,2048]{1,0:T(8,128)(2,1)}, u32[]{:S(2)}) copy-start(bf16[128,2048]{1,0:T(8,128)(2,1)} %get-tuple-element.58) | copy-start | bytes 1572868

commit v8 on v7

--- a/solution.py
+++ b/solution.py
@@ -45,6 +45,17 @@
         cost_estimate=pl.CostEstimate(flops=1, bytes_accessed=1, transcendentals=0),
         compiler_params=pltpu.CompilerParams(vmem_limit_bytes=VMEM_BYTES),
     )(*scalars, *arrays, *first)
+
+
+def held_until(value, event):
+    anywhere = pl.BlockSpec(memory_space=pl.ANY)
+    return pl.pallas_call(
+        lambda *refs: None,
+        out_shape=jax.ShapeDtypeStruct(value.shape, value.dtype),
+        in_specs=[anywhere, anywhere],
+        out_specs=anywhere,
+        input_output_aliases={0: 0},
+    )(value, event)
 
 
 def nn(a, b):
@@ -313,7 +324,7 @@
     return grad_q, grad_k, grad_v
 
 
-def cross_body(qg, k, v, gq, gk, gv):
+def cross_body(qg, k, v, stats, gq, gk, gv):
     rows, width = k.shape
     heads = width // HEAD
     theirs = from_pieces(qg, 2 * rows)
@@ -336,19 +347,19 @@
             ps.append(prob.astype(BF))
             ds.append((prob * (d - delta)).astype(BF))
         a, b, c = products(ps, ds, q_pair, k_pair, g_pair)
-        gq[:rows, at] = a.astype(BF)
+        gq[:, at] = a.astype(BF)
         gk[:, at] = b.astype(BF)
         gv[:, at] = c.astype(BF)
-    add_pieces(jnp.concatenate(logs + deltas, axis=0), gq, rows)
-
-
-def own_body(at_ref, q, k, v, g, ours, gq_far, gk_far, gv_far, gq, gk, gv):
+    stats[0] = jnp.concatenate(logs + deltas, axis=0)
+
+
+def own_body(at_ref, q, k, v, g, ours, theirs, gk_far, gv_far, gq, gk, gv):
     rows, width = q.shape
     heads = width // HEAD
     seen = seen_mask(rows, False)
     begins = at_ref[2] == 0
     near = ours[0]
-    away = from_pieces(gq_far, rows)
+    away = theirs[0]
     for p in range(width // LANES):
         at = slice(p * LANES, (p + 1) * LANES)
         q_pair, k_pair, g_pair = q[:, at], k[:, at], g[:, at]
@@ -366,7 +377,7 @@
             ps.append(prob.astype(BF))
             ds.append((prob * (d - delta)).astype(BF))
         a, b, c = products(ps, ds, q_pair, k_pair, g_pair)
-        gq[:, at] = (a + gq_far[:rows, at].astype(F32)).astype(BF)
+        gq[:, at] = a
         gk[:, at] = (b + gk_far[:, at].astype(F32)).astype(BF)
         gv[:, at] = (c + gv_far[:, at].astype(F32)).astype(BF)
 
@@ -425,9 +436,9 @@
         [decay_rates],
         [xs, gs, bc, sums, sums_t],
     )
-    gq_out, gk_far, gv_far = call(
+    stats_out, gq_out, gk_far, gv_far = call(
         cross_body,
-        [((rows + 16, width), BF), (wide, BF), (wide, BF)],
+        [stats, (wide, BF), (wide, BF), (wide, BF)],
         [],
         [qg_next, k2, v2],
         steps=steps,
@@ -449,17 +460,19 @@
     spread = lax.all_to_all(plane, ("zh", "zl"), 0, 0, tiled=True)
     grad_bc = jnp.sum(spread.astype(F32), axis=0)
 
-    gq_far = lax.ppermute(gq_out, TM, to_next)
+    stats_far = lax.ppermute(stats_out, TM, to_next)
+    gq_far = lax.ppermute(held_until(gq_out, stats_far), TM, to_next)
     gq, gk, gv = call(
         own_body,
-        [(wide, BF)] * 3,
+        [(wide, F32), (wide, BF), (wide, BF)],
         [at],
-        [q2, k2, v2, g2, stats_own, gq_far, gk_far, gv_far],
+        [q2, k2, v2, g2, stats_own, stats_far, gk_far, gv_far],
         [chip],
         steps=steps,
     )
+    gq = (gq + gq_far.astype(F32)).astype(BF)
     shape = (length, blocks, width)
-    grad_x = call(unpack_body, [(wide, BF)], [at], [keep, gx_far], [gk])[0]
+    grad_x = call(unpack_body, [(wide, BF)], [at], [keep, gx_far], [plane])[0]
     return grad_x.reshape(shape), gq.reshape(shape), gk.reshape(shape), gv.reshape(shape), grad_bc
 
 

time: 164 us -> 169 us (1.030)
  starting transfers between devices: 75.8 us -> 83.1 us
  waiting for transfers between devices: 24.2 us -> 20.6 us
  local copies, waits for them, and re-layouts: 16.6 us -> 18.8 us
    ppermute x1 -> x2, starting transfers between devices: 29.5 us -> 37.8 us  [the longest x1 29.4 us: local(): stats_far = lax.ppermute(stats_out, TM, to_next)]
    all_to_all x1, waiting for transfers between devices: 6.91 us -> 0.01 us  [local(): spread = lax.all_to_all(chip, ('y', 'x'), 0, 0, tiled=True)]
    all_to_all x1, starting transfers between devices: 16.6 us -> 14.8 us  [local(): spread = lax.all_to_all(plane, ('zh', 'zl'), 0, 0, tiled=True)]
    unnamed x38 -> x36, local copies, waits for them, and re-layouts: 4.53 us -> 4.48 us
  transfers between devices with their start and end apart: 10 -> 11, of which waited for: 3 -> 4; matrix products, arithmetic and copies ran while one was open for 7% -> 8% of each run, Pallas kernels for 21% -> 20%
where the time goes in v8:
time: 169 us; the launch traced here: 168 us
  starting transfers between devices  83.1 us (49%)
  Pallas kernels  41.9 us (25%)
  waiting for transfers between devices  20.6 us (12%)
  local copies, waits for them, and re-layouts  18.8 us (11%)
  other arithmetic  3.02 us (2%)
    pallas_call x9, Pallas kernels, call(): pl.pallas_call(run, out_shape=[jax.ShapeDtypeStruct(s, d) for s, d in out...  41.9 us
    ppermute x1, starting transfers between devices, local(): stats_far = lax.ppermute(stats_out, TM, to_next)  29.4 us
    ppermute x1, waiting for transfers between devices, local(): qg_next = lax.ppermute(qg, TM, to_prev)  15.2 us
    all_to_all x1, starting transfers between devices, local(): spread = lax.all_to_all(plane, ('zh', 'zl'), 0, 0, tiled=True)  14.8 us
    ppermute x3, starting transfers between devices, local(): lax.ppermute(m, 'y', [(i, (i + s) % ny) for i in range(ny)])  10.4 us
    ppermute x1, starting transfers between devices, local(): gq_far = lax.ppermute(held_until(gq_out, stats_far), TM, to_next)  8.33 us
    ppermute x1, starting transfers between devices, local(): got = lax.ppermute(out, 'zh', flip)  7.18 us
    all_to_all x1, starting transfers between devices, local(): spread = lax.all_to_all(chip, ('y', 'x'), 0, 0, tiled=True)  7.15 us
  transfers between devices with their start and end apart: 11, of which 4 were waited for; matrix products, arithmetic and copies ran while one was open for 8% of the time, Pallas kernels for 20%

profile of v8, /device:TPU:2, one launch (start us, length us, event | category | flops | bytes accessed | tf_op | source)
XLA Modules:
  0.0 168.2 jit_solution(5561434508403447312)
XLA Ops:
  0.6 2.1 %reshape.44.refs_2_.refs_3_.refs_1_.refs_4_ = bf16[128,2048]{1,0:T(8,128)(2,1)} reshape(bf16[64,2,2048]{2,1,0:T(2,128)(2,1)} %param.17) | data formatting | bytes 1048576 | tf_op jit(solution)/shard_map/reshape | solution.py:400
  2.7 1.0 reshape.43.refs_1_
  3.7 0.7 pad_add_fusion.refs_0_
  4.4 2.6 %shard_map.128 = (bf16[64,4224]{1,0:T(8,128)(2,1)}, bf16[64,4224]{1,0:T(8,128)(2,1)}) custom-call(s32[4]{0:T(128)} %pad_add_fusion.refs_0_, bf16[128,2048]{1,0:T(8,128)(2,1)} %reshape.43.refs_1_, bf16[128,2048]{1,0:T(8,128)(2,1)} %reshape.44.refs_2_.refs_3_.refs_1_.refs_4_, s32[2,32,64]{2,1,0:T(8,128)} %bitcast.7), custom_call_target="tpu_custom_call" | custom-call | flops 1 | bytes 1 | tf_op jit(solution)/shard_map/pallas_call | solution.py:37
  7.0 7.2 %collective-permute-start = (bf16[64,4224]{1,0:T(8,128)(2,1)}, bf16[64,4224]{1,0:T(8,128)(2,1)S(1)}, u32[]{:S(2)}, u32[]{:S(2)}) collective-permute-start(bf16[64,4224]{1,0:T(8,128)(2,1)} %get-tuple-element.34), channel_id=1, source_target_pairs={{0,32},{32,0},{1,33},{33,1},{2,34},{34,2},{3,35},{35,3},{4,36},{36... | collective-permute-start | bytes 1622024 | tf_op jit(solution)/shard_map/ppermute | solution.py:409
  14.1 1.0 reshape.45.refs_0_.refs_1_
  15.1 1.0 reshape.46.refs_1_.refs_2_
  16.1 1.0 reshape.47.refs_2_.refs_3_
  17.1 4.1 %shard_map.129.refs_2_.refs_5_ = f32[4,16,128]{2,1,0:T(8,128)} custom-call(bf16[128,2048]{1,0:T(8,128)(2,1)} %reshape.45.refs_0_.refs_1_, bf16[128,2048]{1,0:T(8,128)(2,1)} %reshape.46.refs_1_.refs_2_, bf16[128,2048]{1,0:T(8,128)(2,1)} %reshape.47.refs_2_.refs_3_, bf16[128,2048]{1,0:T(8,128)(2,1)} %reshape.44.refs_2_.refs_3_.refs_1_.refs_4_), custom_call_target="tpu_custom_call" | custom-call | flops 1 | bytes 1 | tf_op jit(solution)/shard_map/pallas_call | solution.py:37
  21.2 3.5 %shard_map.130.refs_5_ = bf16[272,2048]{1,0:T(8,128)(2,1)} custom-call(bf16[128,2048]{1,0:T(8,128)(2,1)} %reshape.45.refs_0_.refs_1_, bf16[128,2048]{1,0:T(8,128)(2,1)} %reshape.44.refs_2_.refs_3_.refs_1_.refs_4_, f32[4,16,128]{2,1,0:T(8,128)} %shard_map.129.refs_2_.refs_5_), custom_call_target="tpu_custom_call" | custom-call | flops 1 | bytes 1 | tf_op jit(solution)/shard_map/pallas_call | solution.py:37
  24.7 1.3 collective-permute-start.4
  26.0 0.1 broadcast_in_dim.6
  26.1 0.7 broadcast_in_dim_reshape.6.refs_4_
  26.8 2.1 %collective-permute-done.refs_2_ = bf16[64,4224]{1,0:T(8,128)(2,1)S(1)} collective-permute-done((bf16[64,4224]{1,0:T(8,128)(2,1)}, bf16[64,4224]{1,0:T(8,128)(2,1)S(1)}, u32[]{:S(2)}, u32[]{:S(2)}) %collective-permute-start) | collective-permute-done | bytes 540704 | tf_op jit(solution)/shard_map/ppermute | solution.py:409
  28.9 0.8 copy-done.5
  29.7 5.7 %shard_map.131 = (bf16[128,2048]{1,0:T(8,128)(2,1)}, bf16[128,2048]{1,0:T(8,128)(2,1)}, bf16[128,256]{1,0:T(8,128)(2,1)}, f32[128,128]{1,0:T(8,128)}, f32[128,12...) custom-call(s32[4]{0:T(128)} %pad_add_fusion.refs_0_, ...), custom_call_target="tpu_custom_call" | custom-call | flops 1 | bytes 1 | tf_op jit(solution)/shard_map/pallas_call | solution.py:37
  35.4 6.1 %collective-permute-start.1 = (bf16[144,2048]{1,0:T(8,128)(2,1)}, bf16[144,2048]{1,0:T(8,128)(2,1)S(1)}, u32[]{:S(2)}, u32[]{:S(2)}) collective-permute-start(bf16[144,2048]{1,0:T(8,128)(2,1)} %get-tuple-element.35), channel_id=1, source_target_pairs={{0,64},{64,128},{128,192},{192,0},{1,65},{65,129},{129,193},{193,1... | collective-permute-start | bytes 1769480 | tf_op jit(solution)/shard_map/ppermute | solution.py:430
  41.5 2.9 %collective-permute-start.2 = (bf16[144,2048]{1,0:T(8,128)(2,1)}, bf16[144,2048]{1,0:T(8,128)(2,1)S(1)}, u32[]{:S(2)}, u32[]{:S(2)}) collective-permute-start(bf16[144,2048]{1,0:T(8,128)(2,1)} %get-tuple-element.36), channel_id=1, source_target_pairs={{0,128},{64,192},{128,0},{192,64},{1,129},{65,193},{129,1},{193,65... | collective-permute-start | bytes 1769480 | tf_op jit(solution)/shard_map/ppermute | solution.py:430
  44.4 1.4 collective-permute-start.3
  45.8 0.7 broadcast_in_dim_reshape.7.refs_5_
  46.5 3.6 %shard_map.132 = (bf16[128,2048]{1,0:T(8,128)(2,1)}, f32[128,128]{1,0:T(8,128)}, f32[128,128]{1,0:T(8,128)}, bf16[2048,128]{1,0:T(8,128)(2,1)}) custom-call(f32[32]{0:T(128)} %refs_0_.1, bf16[128,2048]{1,0:T(8,128)(2,1)} %get-tuple-element.43.refs_1_, bf16[128,2048]{1,0:T(8,128)(2,1)} %get-tuple-element.38.refs_2_.refs_7_, ...), custom_call_target="tpu_custom_call" | custom-call | flops 1 | bytes 1 | tf_op jit(solution)/shard_map/pallas_call | solution.py:37
  50.1 15.2 %collective-permute-done.4.refs_0_ = bf16[272,2048]{1,0:T(8,128)(2,1)S(1)} collective-permute-done((bf16[272,2048]{1,0:T(8,128)(2,1)}, bf16[272,2048]{1,0:T(8,128)(2,1)S(1)}, u32[]{:S(2)}, u32[]{:S(2)}) %collective-permute-start.4) | collective-permute-done | bytes 1114144 | tf_op jit(solution)/shard_map/ppermute | solution.py:415
  65.3 1.1 copy-done
  66.3 7.3 %shard_map.133 = (f32[4,16,128]{2,1,0:T(8,128)}, bf16[128,2048]{1,0:T(8,128)(2,1)}, bf16[128,2048]{1,0:T(8,128)(2,1)}, bf16[128,2048]{1,0:T(8,128)(2,1)}) custom-call(bf16[272,2048]{1,0:T(8,128)(2,1)} %copy-done, bf16[128,2048]{1,0:T(8,128)(2,1)} %reshape.46.refs_1_.refs_2_, bf16[128,2048]{1,0:T(8,128)(2,1)} %reshape.47.refs_2_.refs_3_), custom_call_target="tpu_custom_call" | custom-call | flops 1 | bytes 1 | tf_op jit(solution)/shard_map/pallas_call | solution.py:37
  73.7 0.8 copy-done.2
  74.5 0.2 copy-done.3
  74.7 0.3 copy-done.4
  74.9 5.8 %shard_map.134 = (bf16[64,2048]{1,0:T(8,128)(2,1)}, bf16[64,2048]{1,0:T(8,128)(2,1)}, bf16[4,4,64,256]{3,2,1,0:T(8,128)(2,1)}, bf16[4,4,64,256]{3,2,1,0:T(8,128)(2,1)}) custom-call(s32[4]{0:T(128)} %pad_add_fusion.refs_0_, bf16[144,2048]{1,0:T(8,128)(2,1)} %copy-done.2, bf16[144,2048]{1,0:T(8,128)(2,1)} %copy-done.3, bf16[144,2048]{1,0:T(8,128)(2,1)} %copy-done.4, ...), custom_call_target="tpu_custom_call" | custom-call | flops 1 | bytes 1 | tf_op jit(solution)/shard_map/pallas_call | solution.py:37
  80.8 0.1 collective-permute-start.6
  80.9 29.4 %collective-permute-start.7 = (f32[4,16,128]{2,1,0:T(8,128)S(1)}, f32[4,16,128]{2,1,0:T(8,128)S(1)}, u32[]{:S(2)}, u32[]{:S(2)}) collective-permute-start(f32[4,16,128]{2,1,0:T(8,128)S(1)} %copy-done.17), channel_id=1, source_target_pairs={{0,32},{32,64},{64,96},{96,128},{128,160},{160,192},{192,224},{1,3... | collective-permute-start | bytes 98312 | tf_op jit(solution)/shard_map/ppermute | solution.py:463
  110.3 1.6 collective-permute-done.7.refs_6_.refs_1_
  111.9 0.6 copy-done.13
  112.5 8.3 %collective-permute-start.8 = (bf16[128,2048]{1,0:T(8,128)(2,1)}, bf16[128,2048]{1,0:T(8,128)(2,1)S(1)}, u32[]{:S(2)}, u32[]{:S(2)}) collective-permute-start(bf16[128,2048]{1,0:T(8,128)(2,1)} %shard_map.137), channel_id=1, source_target_pairs={{0,32},{32,64},{64,96},{96,128},{128,160},{160,192},{192,224},{1,3... | collective-permute-start | bytes 1572872 | tf_op jit(solution)/shard_map/ppermute | solution.py:464
  120.9 1.0 add_convert_fusion.1
  121.8 7.2 %all-to-all-start = ((bf16[16,64,256]{2,1,0:T(8,128)(2,1)}), bf16[16,64,256]{2,1,0:T(8,128)(2,1)S(1)}, u32[]{:S(2)}, u32[]{:S(2)}) async-start(bf16[16,64,256]{2,1,0:T(8,128)(2,1)} %bitcast.5.refs_9_), calls=%async_computation | async-start | bytes 1048576 | tf_op jit(solution)/shard_map/all_to_all | solution.py:458
  129.0 4.5 %collective-permute-start.5 = (bf16[64,2048]{1,0:T(8,128)(2,1)S(1)}, bf16[64,2048]{1,0:T(8,128)(2,1)S(1)}, u32[]{:S(2)}, u32[]{:S(2)}) collective-permute-start(bf16[64,2048]{1,0:T(8,128)(2,1)S(1)} %copy-done.16), channel_id=1, source_target_pairs={{0,32},{32,0},{1,33},{33,1},{2,34},{34,2},{3,35},{35,3},{4,36},{36... | collective-permute-start | bytes 786440 | tf_op jit(solution)/shard_map/ppermute | solution.py:454
  133.5 7.1 %shard_map.136 = (f32[128,2048]{1,0:T(8,128)}, bf16[128,2048]{1,0:T(8,128)(2,1)}, bf16[128,2048]{1,0:T(8,128)(2,1)}) custom-call(s32[4]{0:T(128)} %pad_add_fusion.refs_0_, bf16[128,2048]{1,0:T(8,128)(2,1)} %reshape.45.refs_0_.refs_1_, bf16[128,2048]{1,0:T(8,128)(2,1)} %reshape.46.refs_1_.refs_2_, bf16[128,2048]{1,0:T(8,128)(2,1)} %reshape.47.refs_2_.refs_3_, ...), custom_call_target="tpu_custom_call" | custom-call | flops 1 | bytes 1 | tf_op jit(solution)/shard_map/pallas_call | solution.py:37
  140.6 2.3 %reshape.52 = bf16[64,2,2048]{2,1,0:T(2,128)(2,1)} reshape(bf16[128,2048]{1,0:T(8,128)(2,1)} %get-tuple-element.59) | data formatting | bytes 1048576 | tf_op jit(solution)/shard_map/reshape | solution.py:476
  142.9 1.1 reshape.53
  144.1 0.7 reduce_sum.21
  144.8 14.8 %all-to-all-start.1 = ((bf16[8,8,256]{2,1,0:T(8,128)(2,1)}), bf16[8,8,256]{2,1,0:T(8,128)(2,1)S(1)}, u32[]{:S(2)}, u32[]{:S(2)}) async-start(bf16[8,8,256]{2,1,0:T(8,128)(2,1)} %bitcast.6.refs_3_), calls=%async_computation.1 | async-start | bytes 65536 | tf_op jit(solution)/shard_map/all_to_all | solution.py:460
  159.6 0.1 add_convert_fusion
  159.7 1.1 reshape.51
  160.8 0.7 copy-done.12
  161.5 2.2 %shard_map.135 = bf16[128,2048]{1,0:T(8,128)(2,1)} custom-call(s32[4]{0:T(128)} %pad_add_fusion.refs_0_, bf16[64,2048]{1,0:T(8,128)(2,1)} %get-tuple-element.51.refs_1_, bf16[64,2048]{1,0:T(8,128)(2,1)} %copy-done.12, bf16[8,8,256]{2,1,0:T(8,128)(2,1)} %bitcast.6.refs_3_), custom_call_target="tpu_custom_call" | custom-call | flops 1 | bytes 1 | tf_op jit(solution)/shard_map/pallas_call | solution.py:37
  163.8 2.2 %reshape.50 = bf16[64,2,2048]{2,1,0:T(2,128)(2,1)} reshape(bf16[128,2048]{1,0:T(8,128)(2,1)} %shard_map.135) | data formatting | bytes 1048576 | tf_op jit(solution)/shard_map/reshape | solution.py:476
  165.9 1.6 all-to-all-done.1
  167.6 0.6 convert_reduce_fusion
  (38 shorter events, 0.1 us)
Async XLA Ops:
  0.6 2.1 %copy-start.7 = (bf16[64,2,2048]{2,1,0:T(2,128)(2,1)S(1)}, bf16[64,2,2048]{2,1,0:T(2,128)(2,1)}, u32[]{:S(2)}) copy-start(bf16[64,2,2048]{2,1,0:T(2,128)(2,1)} %param.9) | copy-start | bytes 1572868
  2.7 11.4 %copy-start.8 = (bf16[64,2,2048]{2,1,0:T(2,128)(2,1)S(1)}, bf16[64,2,2048]{2,1,0:T(2,128)(2,1)}, u32[]{:S(2)}) copy-start(bf16[64,2,2048]{2,1,0:T(2,128)(2,1)} %param.14) | copy-start | bytes 1572868
  3.7 11.4 %copy-start.9 = (bf16[64,2,2048]{2,1,0:T(2,128)(2,1)S(1)}, bf16[64,2,2048]{2,1,0:T(2,128)(2,1)}, u32[]{:S(2)}) copy-start(bf16[64,2,2048]{2,1,0:T(2,128)(2,1)} %param.15) | copy-start | bytes 1572868
  7.0 9.2 %copy-start.10 = (bf16[64,2,2048]{2,1,0:T(2,128)(2,1)S(1)}, bf16[64,2,2048]{2,1,0:T(2,128)(2,1)}, u32[]{:S(2)}) copy-start(bf16[64,2,2048]{2,1,0:T(2,128)(2,1)} %param.16) | copy-start | bytes 1572868
  7.0 21.9 %collective-permute-start = (bf16[64,4224]{1,0:T(8,128)(2,1)}, bf16[64,4224]{1,0:T(8,128)(2,1)S(1)}, u32[]{:S(2)}, u32[]{:S(2)}) collective-permute-start(bf16[64,4224]{1,0:T(8,128)(2,1)} %get-tuple-element.34), channel_id=1, source_target_pairs={{0,32},{32,0},{1,33},{33,1},{2,34},{34,2},{3,35},{35,3},{4,36},{36... | collective-permute-start | bytes 1622024 | tf_op jit(solution)/shard_map/ppermute | solution.py:409
  21.2 4.8 %copy-start.14 = (f32[32]{0:T(128)S(1)}, f32[32]{0:T(128)}, u32[]{:S(2)}) copy-start(f32[32]{0:T(128)} %refs_0_.1) | copy-start | bytes 388
  24.7 40.6 %collective-permute-start.4 = (bf16[272,2048]{1,0:T(8,128)(2,1)}, bf16[272,2048]{1,0:T(8,128)(2,1)S(1)}, u32[]{:S(2)}, u32[]{:S(2)}) collective-permute-start(bf16[272,2048]{1,0:T(8,128)(2,1)} %shard_map.130.refs_5_), channel_id=1, source_target_pairs={{32,0},{64,32},{96,64},{128,96},{160,128},{192,160},{224,192},{33,... | collective-permute-start | bytes 3342344 | tf_op jit(solution)/shard_map/ppermute | solution.py:415
  28.9 0.8 copy-start.5
  29.7 16.0 %copy-start.15 = (f32[32]{0:T(128)S(1)}, f32[32]{0:T(128)}, u32[]{:S(2)}) copy-start(f32[32]{0:T(128)} %param.13) | copy-start | bytes 388
  35.4 38.2 %collective-permute-start.1 = (bf16[144,2048]{1,0:T(8,128)(2,1)}, bf16[144,2048]{1,0:T(8,128)(2,1)S(1)}, u32[]{:S(2)}, u32[]{:S(2)}) collective-permute-start(bf16[144,2048]{1,0:T(8,128)(2,1)} %get-tuple-element.35), channel_id=1, source_target_pairs={{0,64},{64,128},{128,192},{192,0},{1,65},{65,129},{129,193},{193,1... | collective-permute-start | bytes 1769480 | tf_op jit(solution)/shard_map/ppermute | solution.py:430
  41.5 32.1 %collective-permute-start.2 = (bf16[144,2048]{1,0:T(8,128)(2,1)}, bf16[144,2048]{1,0:T(8,128)(2,1)S(1)}, u32[]{:S(2)}, u32[]{:S(2)}) collective-permute-start(bf16[144,2048]{1,0:T(8,128)(2,1)} %get-tuple-element.36), channel_id=1, source_target_pairs={{0,128},{64,192},{128,0},{192,64},{1,129},{65,193},{129,1},{193,65... | collective-permute-start | bytes 1769480 | tf_op jit(solution)/shard_map/ppermute | solution.py:430
  44.4 29.3 %collective-permute-start.3 = (bf16[144,2048]{1,0:T(8,128)(2,1)}, bf16[144,2048]{1,0:T(8,128)(2,1)S(1)}, u32[]{:S(2)}, u32[]{:S(2)}) collective-permute-start(bf16[144,2048]{1,0:T(8,128)(2,1)} %get-tuple-element.37), channel_id=1, source_target_pairs={{0,192},{64,0},{128,64},{192,128},{1,193},{65,1},{129,65},{193,129... | collective-permute-start | bytes 1769480 | tf_op jit(solution)/shard_map/ppermute | solution.py:430
  65.3 1.1 copy-start
  73.6 0.8 copy-start.2
  73.7 1.0 copy-start.3
  73.7 1.3 copy-start.4
  74.9 5.9 %copy-start.17 = (f32[4,16,128]{2,1,0:T(8,128)S(1)}, f32[4,16,128]{2,1,0:T(8,128)}, u32[]{:S(2)}) copy-start(f32[4,16,128]{2,1,0:T(8,128)} %get-tuple-element.55) | copy-start | bytes 98308
  80.8 40.1 %copy-start.6 = (bf16[4,4,64,256]{3,2,1,0:T(8,128)(2,1)S(1)}, bf16[4,4,64,256]{3,2,1,0:T(8,128)(2,1)}, u32[]{:S(2)}) copy-start(bf16[4,4,64,256]{3,2,1,0:T(8,128)(2,1)} %get-tuple-element.53) | copy-start | bytes 1572868
  80.8 40.1 %collective-permute-start.6 = (bf16[4,4,64,256]{3,2,1,0:T(8,128)(2,1)}, bf16[4,4,64,256]{3,2,1,0:T(8,128)(2,1)S(1)}, u32[]{:S(2)}, u32[]{:S(2)}) collective-permute-start(bf16[4,4,64,256]{3,2,1,0:T(8,128)(2,1)} %get-tuple-element.54), channel_id=1, source_target_pairs={{0,1},{1,0},{2,3},{3,2},{4,5},{5,4},{6,7},{7,6},{8,9},{9,8},{10,11... | collective-permute-start | bytes 1572872 | tf_op jit(solution)/shard_map/ppermute | solution.py:456
  80.9 31.0 %collective-permute-start.7 = (f32[4,16,128]{2,1,0:T(8,128)S(1)}, f32[4,16,128]{2,1,0:T(8,128)S(1)}, u32[]{:S(2)}, u32[]{:S(2)}) collective-permute-start(f32[4,16,128]{2,1,0:T(8,128)S(1)} %copy-done.17), channel_id=1, source_target_pairs={{0,32},{32,64},{64,96},{96,128},{128,160},{160,192},{192,224},{1,3... | collective-permute-start | bytes 98312 | tf_op jit(solution)/shard_map/ppermute | solution.py:463
  111.9 0.6 copy-start.13
  112.5 47.0 %collective-permute-start.8 = (bf16[128,2048]{1,0:T(8,128)(2,1)}, bf16[128,2048]{1,0:T(8,128)(2,1)S(1)}, u32[]{:S(2)}, u32[]{:S(2)}) collective-permute-start(bf16[128,2048]{1,0:T(8,128)(2,1)} %shard_map.137), channel_id=1, source_target_pairs={{0,32},{32,64},{64,96},{96,128},{128,160},{160,192},{192,224},{1,3... | collective-permute-start | bytes 1572872 | tf_op jit(solution)/shard_map/ppermute | solution.py:464
  120.9 8.1 %copy-start.16 = (bf16[64,2048]{1,0:T(8,128)(2,1)S(1)}, bf16[64,2048]{1,0:T(8,128)(2,1)}, u32[]{:S(2)}) copy-start(bf16[64,2048]{1,0:T(8,128)(2,1)} %get-tuple-element.52) | copy-start | bytes 786436
  121.8 22.2 %all-to-all-start = ((bf16[16,64,256]{2,1,0:T(8,128)(2,1)}), bf16[16,64,256]{2,1,0:T(8,128)(2,1)S(1)}, u32[]{:S(2)}, u32[]{:S(2)}) async-start(bf16[16,64,256]{2,1,0:T(8,128)(2,1)} %bitcast.5.refs_9_), calls=%async_computation | async-start | bytes 1048576 | tf_op jit(solution)/shard_map/all_to_all | solution.py:458
  129.0 31.8 %collective-permute-start.5 = (bf16[64,2048]{1,0:T(8,128)(2,1)S(1)}, bf16[64,2048]{1,0:T(8,128)(2,1)S(1)}, u32[]{:S(2)}, u32[]{:S(2)}) collective-permute-start(bf16[64,2048]{1,0:T(8,128)(2,1)S(1)} %copy-done.16), channel_id=1, source_target_pairs={{0,32},{32,0},{1,33},{33,1},{2,34},{34,2},{3,35},{35,3},{4,36},{36... | collective-permute-start | bytes 786440 | tf_op jit(solution)/shard_map/ppermute | solution.py:454
  140.6 2.3 %copy-start.11 = (bf16[128,2048]{1,0:T(8,128)(2,1)S(1)}, bf16[128,2048]{1,0:T(8,128)(2,1)}, u32[]{:S(2)}) copy-start(bf16[128,2048]{1,0:T(8,128)(2,1)} %get-tuple-element.60) | copy-start | bytes 1572868
  140.6 18.9 %copy-start.1 = (f32[128,2048]{1,0:T(8,128)S(1)}, f32[128,2048]{1,0:T(8,128)}, u32[]{:S(2)}) copy-start(f32[128,2048]{1,0:T(8,128)} %get-tuple-element.58) | copy-start | bytes 3145732
  144.8 22.8 %all-to-all-start.1 = ((bf16[8,8,256]{2,1,0:T(8,128)(2,1)}), bf16[8,8,256]{2,1,0:T(8,128)(2,1)S(1)}, u32[]{:S(2)}, u32[]{:S(2)}) async-start(bf16[8,8,256]{2,1,0:T(8,128)(2,1)} %bitcast.6.refs_3_), calls=%async_computation.1 | async-start | bytes 65536 | tf_op jit(solution)/shard_map/all_to_all | solution.py:460
  160.8 0.7 copy-start.12

commit v9 on v8

--- a/solution.py
+++ b/solution.py
@@ -45,17 +45,6 @@
         cost_estimate=pl.CostEstimate(flops=1, bytes_accessed=1, transcendentals=0),
         compiler_params=pltpu.CompilerParams(vmem_limit_bytes=VMEM_BYTES),
     )(*scalars, *arrays, *first)
-
-
-def held_until(value, event):
-    anywhere = pl.BlockSpec(memory_space=pl.ANY)
-    return pl.pallas_call(
-        lambda *refs: None,
-        out_shape=jax.ShapeDtypeStruct(value.shape, value.dtype),
-        in_specs=[anywhere, anywhere],
-        out_specs=anywhere,
-        input_output_aliases={0: 0},
-    )(value, event)
 
 
 def nn(a, b):
@@ -443,13 +432,14 @@
         [qg_next, k2, v2],
         steps=steps,
     )
+    stats_far = lax.ppermute(stats_out, TM, to_next)
     order = 1.0 / (rows * tm * lax.axis_size(("zl", "x", "c")))
     keep, give, mine, yours = call(
         lambda at_ref, *refs: carry_body(at_ref, order, *refs),
         [((rows // 2, width), BF)] * 2 + [((ny, nx, nz * 8, 2 * LANES), BF)] * 2,
         [at],
         [m1, m2, m3, rate_wide, gain_wide, bc_weight, gs, bc, scaled_x, scaled_g, leave, gx, gb, gc, x_t],
-        [gq_out],
+        [stats_far],
     )
     gx_far = lax.ppermute(give, "zh", flip)
 
@@ -460,8 +450,7 @@
     spread = lax.all_to_all(plane, ("zh", "zl"), 0, 0, tiled=True)
     grad_bc = jnp.sum(spread.astype(F32), axis=0)
 
-    stats_far = lax.ppermute(stats_out, TM, to_next)
-    gq_far = lax.ppermute(held_until(gq_out, stats_far), TM, to_next)
+    gq_far = lax.ppermute(gq_out, TM, to_next)
     gq, gk, gv = call(
         own_body,
         [(wide, F32), (wide, BF), (wide, BF)],

time: 169 us -> 189 us (1.12)
  waiting for transfers between devices: 20.6 us -> 47 us
  starting transfers between devices: 83.1 us -> 76.4 us
  other arithmetic: 3.02 us -> 5.34 us
  local copies, waits for them, and re-layouts: 18.8 us -> 16.9 us
    ppermute x1, waiting for transfers between devices: 2.13 us -> 43.3 us  [local(): got = lax.ppermute(out, 'zh', flip)]
    ppermute x1, starting transfers between devices: 29.4 us -> 8.21 us  [local(): stats_far = lax.ppermute(stats_out, TM, to_next)]
    ppermute x3, starting transfers between devices: 10.4 us -> 28.3 us  [local(): lax.ppermute(m, 'y', [(i, (i + s) % ny) for i in range(ny)])]
    ppermute x1, waiting for transfers between devices: 15.2 us -> 0.01 us  [local(): qg_next = lax.ppermute(qg, TM, to_prev)]
    ppermute x1, starting transfers between devices: 4.52 us -> 0.09 us  [local(): gx_far = lax.ppermute(give, 'zh', flip)]
    ppermute x1, starting transfers between devices: 8.33 us -> 12 us  [local(): gq_far = lax.ppermute(gq_out, TM, to_next)]
    all_to_all x1, waiting for transfers between devices: 0.01 us -> 3.32 us  [local(): spread = lax.all_to_all(chip, ('y', 'x'), 0, 0, tiled=True)]
    all_to_all x1, starting transfers between devices: 14.8 us -> 12.4 us  [local(): spread = lax.all_to_all(plane, ('zh', 'zl'), 0, 0, tiled=True)]
  transfers between devices with their start and end apart: 11 -> 11, of which waited for: 4 -> 3; matrix products, arithmetic and copies ran while one was open for 8% -> 7% of each run, Pallas kernels for 20% -> 15%
where the time goes in v9:
time: 189 us; the launch traced here: 188 us
  starting transfers between devices  76.4 us (40%)
  waiting for transfers between devices  47 us (25%)
  Pallas kernels  42 us (22%)
  local copies, waits for them, and re-layouts  16.9 us (9%)
  other arithmetic  5.34 us (3%)
    ppermute x1, waiting for transfers between devices, local(): got = lax.ppermute(out, 'zh', flip)  43.3 us
    pallas_call x9, Pallas kernels, call(): pl.pallas_call(run, out_shape=[jax.ShapeDtypeStruct(s, d) for s, d in out...  42 us
    ppermute x3, starting transfers between devices, local(): lax.ppermute(m, 'y', [(i, (i + s) % ny) for i in range(ny)])  28.3 us
    all_to_all x1, starting transfers between devices, local(): spread = lax.all_to_all(plane, ('zh', 'zl'), 0, 0, tiled=True)  12.4 us
    ppermute x1, starting transfers between devices, local(): gq_far = lax.ppermute(gq_out, TM, to_next)  12 us
    ppermute x1, starting transfers between devices, local(): stats_far = lax.ppermute(stats_out, TM, to_next)  8.21 us
    ppermute x1, starting transfers between devices, local(): got = lax.ppermute(out, 'zh', flip)  7.82 us
    all_to_all x1, starting transfers between devices, local(): spread = lax.all_to_all(chip, ('y', 'x'), 0, 0, tiled=True)  6.19 us
  transfers between devices with their start and end apart: 11, of which 3 were waited for; matrix products, arithmetic and copies ran while one was open for 7% of the time, Pallas kernels for 15%

profile of v9, /device:TPU:2, one launch (start us, length us, event | category | flops | bytes accessed | tf_op | source)
XLA Modules:
  0.0 188.5 jit_solution(12966280919799489580)
XLA Ops:
  0.7 2.1 %reshape.44.refs_2_.refs_3_.refs_1_.refs_4_ = bf16[128,2048]{1,0:T(8,128)(2,1)} reshape(bf16[64,2,2048]{2,1,0:T(2,128)(2,1)} %param.17) | data formatting | bytes 1048576 | tf_op jit(solution)/shard_map/reshape | solution.py:389
  2.8 1.0 reshape.45.refs_0_.refs_1_
  3.8 1.0 reshape.46.refs_1_.refs_2_
  4.8 1.0 reshape.47.refs_2_.refs_3_
  5.8 4.1 %shard_map.129.refs_2_.refs_5_ = f32[4,16,128]{2,1,0:T(8,128)} custom-call(bf16[128,2048]{1,0:T(8,128)(2,1)} %reshape.45.refs_0_.refs_1_, bf16[128,2048]{1,0:T(8,128)(2,1)} %reshape.46.refs_1_.refs_2_, bf16[128,2048]{1,0:T(8,128)(2,1)} %reshape.47.refs_2_.refs_3_, bf16[128,2048]{1,0:T(8,128)(2,1)} %reshape.44.refs_2_.refs_3_.refs_1_.refs_4_), custom_call_target="tpu_custom_call" | custom-call | flops 1 | bytes 1 | tf_op jit(solution)/shard_map/pallas_call | solution.py:37
  9.9 3.6 %shard_map.130.refs_5_ = bf16[272,2048]{1,0:T(8,128)(2,1)} custom-call(bf16[128,2048]{1,0:T(8,128)(2,1)} %reshape.45.refs_0_.refs_1_, bf16[128,2048]{1,0:T(8,128)(2,1)} %reshape.44.refs_2_.refs_3_.refs_1_.refs_4_, f32[4,16,128]{2,1,0:T(8,128)} %shard_map.129.refs_2_.refs_5_), custom_call_target="tpu_custom_call" | custom-call | flops 1 | bytes 1 | tf_op jit(solution)/shard_map/pallas_call | solution.py:37
  13.5 1.4 collective-permute-start.4
  14.9 0.6 pad_add_fusion.refs_0_
  15.5 1.0 reshape.43.refs_1_
  16.5 2.5 %shard_map.128 = (bf16[64,4224]{1,0:T(8,128)(2,1)}, bf16[64,4224]{1,0:T(8,128)(2,1)}) custom-call(s32[4]{0:T(128)} %pad_add_fusion.refs_0_, bf16[128,2048]{1,0:T(8,128)(2,1)} %reshape.43.refs_1_, bf16[128,2048]{1,0:T(8,128)(2,1)} %reshape.44.refs_2_.refs_3_.refs_1_.refs_4_, s32[2,32,64]{2,1,0:T(8,128)} %bitcast.7), custom_call_target="tpu_custom_call" | custom-call | flops 1 | bytes 1 | tf_op jit(solution)/shard_map/pallas_call | solution.py:37
  19.0 7.8 %collective-permute-start = (bf16[64,4224]{1,0:T(8,128)(2,1)}, bf16[64,4224]{1,0:T(8,128)(2,1)S(1)}, u32[]{:S(2)}, u32[]{:S(2)}) collective-permute-start(bf16[64,4224]{1,0:T(8,128)(2,1)} %get-tuple-element.34), channel_id=1, source_target_pairs={{0,32},{32,0},{1,33},{33,1},{2,34},{34,2},{3,35},{35,3},{4,36},{36... | collective-permute-start | bytes 1622024 | tf_op jit(solution)/shard_map/ppermute | solution.py:398
  26.8 0.1 broadcast_in_dim.6
  26.9 0.7 broadcast_in_dim_reshape.6.refs_4_
  27.6 43.3 %collective-permute-done.refs_2_ = bf16[64,4224]{1,0:T(8,128)(2,1)S(1)} collective-permute-done((bf16[64,4224]{1,0:T(8,128)(2,1)}, bf16[64,4224]{1,0:T(8,128)(2,1)S(1)}, u32[]{:S(2)}, u32[]{:S(2)}) %collective-permute-start) | collective-permute-done | bytes 540704 | tf_op jit(solution)/shard_map/ppermute | solution.py:398
  70.9 0.8 copy-done.4
  71.7 5.7 %shard_map.131 = (bf16[128,2048]{1,0:T(8,128)(2,1)}, bf16[128,2048]{1,0:T(8,128)(2,1)}, bf16[128,256]{1,0:T(8,128)(2,1)}, f32[128,128]{1,0:T(8,128)}, f32[128,12...) custom-call(s32[4]{0:T(128)} %pad_add_fusion.refs_0_, ...), custom_call_target="tpu_custom_call" | custom-call | flops 1 | bytes 1 | tf_op jit(solution)/shard_map/pallas_call | solution.py:37
  77.4 24.0 %collective-permute-start.1 = (bf16[144,2048]{1,0:T(8,128)(2,1)}, bf16[144,2048]{1,0:T(8,128)(2,1)S(1)}, u32[]{:S(2)}, u32[]{:S(2)}) collective-permute-start(bf16[144,2048]{1,0:T(8,128)(2,1)} %get-tuple-element.35), channel_id=1, source_target_pairs={{0,64},{64,128},{128,192},{192,0},{1,65},{65,129},{129,193},{193,1... | collective-permute-start | bytes 1769480 | tf_op jit(solution)/shard_map/ppermute | solution.py:419
  101.5 3.8 %collective-permute-start.2 = (bf16[144,2048]{1,0:T(8,128)(2,1)}, bf16[144,2048]{1,0:T(8,128)(2,1)S(1)}, u32[]{:S(2)}, u32[]{:S(2)}) collective-permute-start(bf16[144,2048]{1,0:T(8,128)(2,1)} %get-tuple-element.36), channel_id=1, source_target_pairs={{0,128},{64,192},{128,0},{192,64},{1,129},{65,193},{129,1},{193,65... | collective-permute-start | bytes 1769480 | tf_op jit(solution)/shard_map/ppermute | solution.py:419
  105.2 0.5 collective-permute-start.3
  105.7 0.0 collective-permute-done.4.refs_0_
  105.7 1.0 copy-done
  106.7 7.3 %shard_map.133 = (f32[4,16,128]{2,1,0:T(8,128)}, bf16[128,2048]{1,0:T(8,128)(2,1)}, bf16[128,2048]{1,0:T(8,128)(2,1)}, bf16[128,2048]{1,0:T(8,128)(2,1)}) custom-call(bf16[272,2048]{1,0:T(8,128)(2,1)} %copy-done, bf16[128,2048]{1,0:T(8,128)(2,1)} %reshape.46.refs_1_.refs_2_, bf16[128,2048]{1,0:T(8,128)(2,1)} %reshape.47.refs_2_.refs_3_), custom_call_target="tpu_custom_call" | custom-call | flops 1 | bytes 1 | tf_op jit(solution)/shard_map/pallas_call | solution.py:37
  113.9 8.2 %collective-permute-start.5 = (f32[4,16,128]{2,1,0:T(8,128)}, f32[4,16,128]{2,1,0:T(8,128)S(1)}, u32[]{:S(2)}, u32[]{:S(2)}) collective-permute-start(f32[4,16,128]{2,1,0:T(8,128)} %get-tuple-element.50), channel_id=1, source_target_pairs={{0,32},{32,64},{64,96},{96,128},{128,160},{160,192},{192,224},{1,3... | collective-permute-start | bytes 98312 | tf_op jit(solution)/shard_map/ppermute | solution.py:435
  122.2 0.1 broadcast_in_dim.7
  122.2 0.7 broadcast_in_dim_reshape.7.refs_5_
  122.9 3.5 %shard_map.132 = (bf16[128,2048]{1,0:T(8,128)(2,1)}, f32[128,128]{1,0:T(8,128)}, f32[128,128]{1,0:T(8,128)}, bf16[2048,128]{1,0:T(8,128)(2,1)}) custom-call(f32[32]{0:T(128)} %refs_0_.1, bf16[128,2048]{1,0:T(8,128)(2,1)} %get-tuple-element.43.refs_1_, bf16[128,2048]{1,0:T(8,128)(2,1)} %get-tuple-element.38.refs_2_.refs_7_, ...), custom_call_target="tpu_custom_call" | custom-call | flops 1 | bytes 1 | tf_op jit(solution)/shard_map/pallas_call | solution.py:37
  126.5 0.8 copy-done.1
  127.3 0.2 copy-done.2
  127.5 0.2 copy-done.3
  127.7 0.0 copy-done.12
  127.8 5.9 %shard_map.134 = (bf16[64,2048]{1,0:T(8,128)(2,1)}, bf16[64,2048]{1,0:T(8,128)(2,1)}, bf16[4,4,64,256]{3,2,1,0:T(8,128)(2,1)}, bf16[4,4,64,256]{3,2,1,0:T(8,128)(2,1)}) custom-call(s32[4]{0:T(128)} %pad_add_fusion.refs_0_, bf16[144,2048]{1,0:T(8,128)(2,1)} %copy-done.1, bf16[144,2048]{1,0:T(8,128)(2,1)} %copy-done.2, bf16[144,2048]{1,0:T(8,128)(2,1)} %copy-done.3, ...), custom_call_target="tpu_custom_call" | custom-call | flops 1 | bytes 1 | tf_op jit(solution)/shard_map/pallas_call | solution.py:37
  133.7 12.0 %collective-permute-start.8 = (bf16[128,2048]{1,0:T(8,128)(2,1)S(1)}, bf16[128,2048]{1,0:T(8,128)(2,1)S(1)}, u32[]{:S(2)}, u32[]{:S(2)}) collective-permute-start(bf16[128,2048]{1,0:T(8,128)(2,1)S(1)} %copy-done.15), channel_id=1, source_target_pairs={{0,32},{32,64},{64,96},{96,128},{128,160},{160,192},{192,224},{1,3... | collective-permute-start | bytes 1572872 | tf_op jit(solution)/shard_map/ppermute | solution.py:453
  145.7 2.0 %add_convert_fusion.1 = bf16[4,4,64,256]{3,2,1,0:T(8,128)(2,1)} fusion(bf16[4,4,64,256]{3,2,1,0:T(8,128)(2,1)S(1)} %collective-permute-done.7, bf16[4,4,64,256]{3,2,1,0:T(8,128)(2,1)} %get-tuple-element.53), kind=kLoop, calls=%fused_computation.1 | loop fusion | flops 1048576 | bytes 1572864 | tf_op jit(solution)/shard_map/convert_element_type | solution.py:446
  147.8 6.2 %all-to-all-start = ((bf16[16,64,256]{2,1,0:T(8,128)(2,1)}), bf16[16,64,256]{2,1,0:T(8,128)(2,1)S(1)}, u32[]{:S(2)}, u32[]{:S(2)}) async-start(bf16[16,64,256]{2,1,0:T(8,128)(2,1)} %bitcast.5.refs_9_), calls=%async_computation | async-start | bytes 1048576 | tf_op jit(solution)/shard_map/all_to_all | solution.py:448
  154.0 0.1 collective-permute-start.6
  154.1 7.1 %shard_map.136 = (f32[128,2048]{1,0:T(8,128)}, bf16[128,2048]{1,0:T(8,128)(2,1)}, bf16[128,2048]{1,0:T(8,128)(2,1)}) custom-call(s32[4]{0:T(128)} %pad_add_fusion.refs_0_, bf16[128,2048]{1,0:T(8,128)(2,1)} %reshape.45.refs_0_.refs_1_, bf16[128,2048]{1,0:T(8,128)(2,1)} %reshape.46.refs_1_.refs_2_, bf16[128,2048]{1,0:T(8,128)(2,1)} %reshape.47.refs_2_.refs_3_, ...), custom_call_target="tpu_custom_call" | custom-call | flops 1 | bytes 1 | tf_op jit(solution)/shard_map/pallas_call | solution.py:37
  161.2 3.3 %all-to-all-done = bf16[16,64,256]{2,1,0:T(8,128)(2,1)S(1)} async-done(((bf16[16,64,256]{2,1,0:T(8,128)(2,1)}), bf16[16,64,256]{2,1,0:T(8,128)(2,1)S(1)}, u32[]{:S(2)}, u32[]{:S(2)}) %all-to-all-start) | async-done | bytes 524320 | tf_op jit(solution)/shard_map/all_to_all | solution.py:448
  164.5 0.7 reduce_sum.21
  165.2 12.4 %all-to-all-start.1 = ((bf16[8,8,256]{2,1,0:T(8,128)(2,1)}), bf16[8,8,256]{2,1,0:T(8,128)(2,1)S(1)}, u32[]{:S(2)}, u32[]{:S(2)}) async-start(bf16[8,8,256]{2,1,0:T(8,128)(2,1)} %bitcast.6.refs_3_), calls=%async_computation.1 | async-start | bytes 65536 | tf_op jit(solution)/shard_map/all_to_all | solution.py:450
  177.6 1.4 add_convert_fusion
  179.0 1.1 reshape.51
  180.2 1.1 reshape.52
  181.3 1.1 reshape.53
  182.4 0.3 collective-permute-done.6.refs_2_
  182.7 0.7 copy-done.11
  183.4 2.3 %shard_map.135 = bf16[128,2048]{1,0:T(8,128)(2,1)} custom-call(s32[4]{0:T(128)} %pad_add_fusion.refs_0_, bf16[64,2048]{1,0:T(8,128)(2,1)} %get-tuple-element.51.refs_1_, bf16[64,2048]{1,0:T(8,128)(2,1)} %copy-done.11, bf16[8,8,256]{2,1,0:T(8,128)(2,1)} %bitcast.6.refs_3_), custom_call_target="tpu_custom_call" | custom-call | flops 1 | bytes 1 | tf_op jit(solution)/shard_map/pallas_call | solution.py:37
  185.7 2.2 %reshape.50 = bf16[64,2,2048]{2,1,0:T(2,128)(2,1)} reshape(bf16[128,2048]{1,0:T(8,128)(2,1)} %shard_map.135) | data formatting | bytes 1048576 | tf_op jit(solution)/shard_map/reshape | solution.py:465
  187.9 0.6 convert_reduce_fusion
  (35 shorter events, 0.1 us)
Async XLA Ops:
  0.6 2.1 %copy-start.5 = (bf16[64,2,2048]{2,1,0:T(2,128)(2,1)S(1)}, bf16[64,2,2048]{2,1,0:T(2,128)(2,1)}, u32[]{:S(2)}) copy-start(bf16[64,2,2048]{2,1,0:T(2,128)(2,1)} %param.14) | copy-start | bytes 1572868
  0.6 3.1 %copy-start.6 = (bf16[64,2,2048]{2,1,0:T(2,128)(2,1)S(1)}, bf16[64,2,2048]{2,1,0:T(2,128)(2,1)}, u32[]{:S(2)}) copy-start(bf16[64,2,2048]{2,1,0:T(2,128)(2,1)} %param.15) | copy-start | bytes 1572868
  2.8 2.0 %copy-start.7 = (bf16[64,2,2048]{2,1,0:T(2,128)(2,1)S(1)}, bf16[64,2,2048]{2,1,0:T(2,128)(2,1)}, u32[]{:S(2)}) copy-start(bf16[64,2,2048]{2,1,0:T(2,128)(2,1)} %param.16) | copy-start | bytes 1572868
  9.9 5.7 %copy-start.8 = (bf16[64,2,2048]{2,1,0:T(2,128)(2,1)S(1)}, bf16[64,2,2048]{2,1,0:T(2,128)(2,1)}, u32[]{:S(2)}) copy-start(bf16[64,2,2048]{2,1,0:T(2,128)(2,1)} %param.9) | copy-start | bytes 1572868
  13.5 13.4 %copy-start.13 = (f32[32]{0:T(128)S(1)}, f32[32]{0:T(128)}, u32[]{:S(2)}) copy-start(f32[32]{0:T(128)} %refs_0_.1) | copy-start | bytes 388
  13.5 92.2 %collective-permute-start.4 = (bf16[272,2048]{1,0:T(8,128)(2,1)}, bf16[272,2048]{1,0:T(8,128)(2,1)S(1)}, u32[]{:S(2)}, u32[]{:S(2)}) collective-permute-start(bf16[272,2048]{1,0:T(8,128)(2,1)} %shard_map.130.refs_5_), channel_id=1, source_target_pairs={{32,0},{64,32},{96,64},{128,96},{160,128},{192,160},{224,192},{33,... | collective-permute-start | bytes 3342344 | tf_op jit(solution)/shard_map/ppermute | solution.py:404
  19.0 51.9 %collective-permute-start = (bf16[64,4224]{1,0:T(8,128)(2,1)}, bf16[64,4224]{1,0:T(8,128)(2,1)S(1)}, u32[]{:S(2)}, u32[]{:S(2)}) collective-permute-start(bf16[64,4224]{1,0:T(8,128)(2,1)} %get-tuple-element.34), channel_id=1, source_target_pairs={{0,32},{32,0},{1,33},{33,1},{2,34},{34,2},{3,35},{35,3},{4,36},{36... | collective-permute-start | bytes 1622024 | tf_op jit(solution)/shard_map/ppermute | solution.py:398
  70.9 0.8 copy-start.4
  77.4 44.7 %copy-start.14 = (f32[32]{0:T(128)S(1)}, f32[32]{0:T(128)}, u32[]{:S(2)}) copy-start(f32[32]{0:T(128)} %param.13) | copy-start | bytes 388
  77.4 49.0 %collective-permute-start.1 = (bf16[144,2048]{1,0:T(8,128)(2,1)}, bf16[144,2048]{1,0:T(8,128)(2,1)S(1)}, u32[]{:S(2)}, u32[]{:S(2)}) collective-permute-start(bf16[144,2048]{1,0:T(8,128)(2,1)} %get-tuple-element.35), channel_id=1, source_target_pairs={{0,64},{64,128},{128,192},{192,0},{1,65},{65,129},{129,193},{193,1... | collective-permute-start | bytes 1769480 | tf_op jit(solution)/shard_map/ppermute | solution.py:419
  101.5 25.0 %collective-permute-start.2 = (bf16[144,2048]{1,0:T(8,128)(2,1)}, bf16[144,2048]{1,0:T(8,128)(2,1)S(1)}, u32[]{:S(2)}, u32[]{:S(2)}) collective-permute-start(bf16[144,2048]{1,0:T(8,128)(2,1)} %get-tuple-element.36), channel_id=1, source_target_pairs={{0,128},{64,192},{128,0},{192,64},{1,129},{65,193},{129,1},{193,65... | collective-permute-start | bytes 1769480 | tf_op jit(solution)/shard_map/ppermute | solution.py:419
  105.2 21.2 %collective-permute-start.3 = (bf16[144,2048]{1,0:T(8,128)(2,1)}, bf16[144,2048]{1,0:T(8,128)(2,1)S(1)}, u32[]{:S(2)}, u32[]{:S(2)}) collective-permute-start(bf16[144,2048]{1,0:T(8,128)(2,1)} %get-tuple-element.37), channel_id=1, source_target_pairs={{0,192},{64,0},{128,64},{192,128},{1,193},{65,1},{129,65},{193,129... | collective-permute-start | bytes 1769480 | tf_op jit(solution)/shard_map/ppermute | solution.py:419
  105.7 1.0 copy-start
  113.9 12.6 %collective-permute-start.5 = (f32[4,16,128]{2,1,0:T(8,128)}, f32[4,16,128]{2,1,0:T(8,128)S(1)}, u32[]{:S(2)}, u32[]{:S(2)}) collective-permute-start(f32[4,16,128]{2,1,0:T(8,128)} %get-tuple-element.50), channel_id=1, source_target_pairs={{0,32},{32,64},{64,96},{96,128},{128,160},{160,192},{192,224},{1,3... | collective-permute-start | bytes 98312 | tf_op jit(solution)/shard_map/ppermute | solution.py:435
  126.5 0.8 copy-start.1
  126.5 1.1 copy-start.2
  126.5 1.2 copy-start.3
  126.5 1.2 copy-start.12
  127.8 5.9 %copy-start.15 = (bf16[128,2048]{1,0:T(8,128)(2,1)S(1)}, bf16[128,2048]{1,0:T(8,128)(2,1)}, u32[]{:S(2)}) copy-start(bf16[128,2048]{1,0:T(8,128)(2,1)} %get-tuple-element.58) | copy-start | bytes 1572868
  133.7 12.1 %collective-permute-start.7 = (bf16[4,4,64,256]{3,2,1,0:T(8,128)(2,1)}, bf16[4,4,64,256]{3,2,1,0:T(8,128)(2,1)S(1)}, u32[]{:S(2)}, u32[]{:S(2)}) collective-permute-start(bf16[4,4,64,256]{3,2,1,0:T(8,128)(2,1)} %get-tuple-element.54), channel_id=1, source_target_pairs={{0,1},{1,0},{2,3},{3,2},{4,5},{5,4},{6,7},{7,6},{8,9},{9,8},{10,11... | collective-permute-start | bytes 1572872 | tf_op jit(solution)/shard_map/ppermute | solution.py:446
  133.7 43.9 %collective-permute-start.8 = (bf16[128,2048]{1,0:T(8,128)(2,1)S(1)}, bf16[128,2048]{1,0:T(8,128)(2,1)S(1)}, u32[]{:S(2)}, u32[]{:S(2)}) collective-permute-start(bf16[128,2048]{1,0:T(8,128)(2,1)S(1)} %copy-done.15), channel_id=1, source_target_pairs={{0,32},{32,64},{64,96},{96,128},{128,160},{160,192},{192,224},{1,3... | collective-permute-start | bytes 1572872 | tf_op jit(solution)/shard_map/ppermute | solution.py:453
  145.7 8.2 %copy-start.16 = (bf16[64,2048]{1,0:T(8,128)(2,1)S(1)}, bf16[64,2048]{1,0:T(8,128)(2,1)}, u32[]{:S(2)}) copy-start(bf16[64,2048]{1,0:T(8,128)(2,1)} %get-tuple-element.52) | copy-start | bytes 786436
  147.8 16.7 %all-to-all-start = ((bf16[16,64,256]{2,1,0:T(8,128)(2,1)}), bf16[16,64,256]{2,1,0:T(8,128)(2,1)S(1)}, u32[]{:S(2)}, u32[]{:S(2)}) async-start(bf16[16,64,256]{2,1,0:T(8,128)(2,1)} %bitcast.5.refs_9_), calls=%async_computation | async-start | bytes 1048576 | tf_op jit(solution)/shard_map/all_to_all | solution.py:448
  154.0 28.8 %collective-permute-start.6 = (bf16[64,2048]{1,0:T(8,128)(2,1)S(1)}, bf16[64,2048]{1,0:T(8,128)(2,1)S(1)}, u32[]{:S(2)}, u32[]{:S(2)}) collective-permute-start(bf16[64,2048]{1,0:T(8,128)(2,1)S(1)} %copy-done.16), channel_id=1, source_target_pairs={{0,32},{32,0},{1,33},{33,1},{2,34},{34,2},{3,35},{35,3},{4,36},{36... | collective-permute-start | bytes 786440 | tf_op jit(solution)/shard_map/ppermute | solution.py:444
  165.2 22.7 %all-to-all-start.1 = ((bf16[8,8,256]{2,1,0:T(8,128)(2,1)}), bf16[8,8,256]{2,1,0:T(8,128)(2,1)S(1)}, u32[]{:S(2)}, u32[]{:S(2)}) async-start(bf16[8,8,256]{2,1,0:T(8,128)(2,1)} %bitcast.6.refs_3_), calls=%async_computation.1 | async-start | bytes 65536 | tf_op jit(solution)/shard_map/all_to_all | solution.py:450
  177.6 2.6 %copy-start.10 = (bf16[128,2048]{1,0:T(8,128)(2,1)S(1)}, bf16[128,2048]{1,0:T(8,128)(2,1)}, u32[]{:S(2)}) copy-start(bf16[128,2048]{1,0:T(8,128)(2,1)} %get-tuple-element.59) | copy-start | bytes 1572868
  179.0 2.3 %copy-start.9 = (bf16[128,2048]{1,0:T(8,128)(2,1)S(1)}, bf16[128,2048]{1,0:T(8,128)(2,1)}, u32[]{:S(2)}) copy-start(bf16[128,2048]{1,0:T(8,128)(2,1)} %get-tuple-element.60) | copy-start | bytes 1572868
  182.7 0.7 copy-start.11

commit v10 on v7

--- a/solution.py
+++ b/solution.py
@@ -28,6 +28,8 @@
         body(*refs[:used], *refs[used + len(first) :])
 
     def spec(shape):
+        if steps > 1 and len(shape) == 3 and shape[2] > GROUP:
+            return pl.BlockSpec(tuple(shape[:2]) + (GROUP,), lambda i: (0, 0, i))
         if steps == 1:
             return pl.BlockSpec(shape, lambda i: (0,) * len(shape))
         if len(shape) == 3:
@@ -342,6 +344,10 @@
     add_pieces(jnp.concatenate(logs + deltas, axis=0), gq, rows)
 
 
+def apart(value):
+    return value.reshape(value.shape[0] // 2, 2, value.shape[1]).astype(BF)
+
+
 def own_body(at_ref, q, k, v, g, ours, gq_far, gk_far, gv_far, gq, gk, gv):
     rows, width = q.shape
     heads = width // HEAD
@@ -366,9 +372,9 @@
             ps.append(prob.astype(BF))
             ds.append((prob * (d - delta)).astype(BF))
         a, b, c = products(ps, ds, q_pair, k_pair, g_pair)
-        gq[:, at] = (a + gq_far[:rows, at].astype(F32)).astype(BF)
-        gk[:, at] = (b + gk_far[:, at].astype(F32)).astype(BF)
-        gv[:, at] = (c + gv_far[:, at].astype(F32)).astype(BF)
+        gq[:, :, at] = apart(a + gq_far[:rows, at].astype(F32))
+        gk[:, :, at] = apart(b + gk_far[:, at].astype(F32))
+        gv[:, :, at] = apart(c + gv_far[:, at].astype(F32))
 
 
 def local(
@@ -452,7 +458,7 @@
     gq_far = lax.ppermute(gq_out, TM, to_next)
     gq, gk, gv = call(
         own_body,
-        [(wide, BF)] * 3,
+        [((length, blocks, width), BF)] * 3,
         [at],
         [q2, k2, v2, g2, stats_own, gq_far, gk_far, gv_far],
         [chip],

time: 164 us -> 162 us (0.988)
  local copies, waits for them, and re-layouts: 16.6 us -> 14.3 us
    reshape x3 -> x0, local copies, waits for them, and re-layouts: 3.4 us -> none  [the longest x1 1.13 us: local(): gk.reshape(shape)]
    unnamed x38 -> x30, local copies, waits for them, and re-layouts: 4.53 us -> 4.56 us
  transfers between devices with their start and end apart: 10 -> 10, of which waited for: 3 -> 3; matrix products, arithmetic and copies ran while one was open for 7% -> 6% of each run, Pallas kernels for 21% -> 21%
where the time goes in v10:
time: 162 us; the launch traced here: 160 us
  starting transfers between devices  75.3 us (46%)
  Pallas kernels  41.9 us (26%)
  waiting for transfers between devices  24.1 us (15%)
  local copies, waits for them, and re-layouts  14.3 us (9%)
  other arithmetic  3.9 us (2%)
    pallas_call x9, Pallas kernels, call(): pl.pallas_call(run, out_shape=[jax.ShapeDtypeStruct(s, d) for s, d in out...  41.9 us
    ppermute x1, starting transfers between devices, local(): gq_far = lax.ppermute(gq_out, TM, to_next)  29.5 us
    all_to_all x1, starting transfers between devices, local(): spread = lax.all_to_all(plane, ('zh', 'zl'), 0, 0, tiled=True)  16.2 us
    ppermute x1, waiting for transfers between devices, local(): qg_next = lax.ppermute(qg, TM, to_prev)  15.2 us
    ppermute x3, starting transfers between devices, local(): lax.ppermute(m, 'y', [(i, (i + s) % ny) for i in range(ny)])  10.4 us
    ppermute x1, starting transfers between devices, local(): got = lax.ppermute(out, 'zh', flip)  7.18 us
    all_to_all x1, starting transfers between devices, local(): spread = lax.all_to_all(chip, ('y', 'x'), 0, 0, tiled=True)  7.13 us
    all_to_all x1, waiting for transfers between devices, local(): spread = lax.all_to_all(chip, ('y', 'x'), 0, 0, tiled=True)  6.86 us
  transfers between devices with their start and end apart: 10, of which 3 were waited for; matrix products, arithmetic and copies ran while one was open for 6% of the time, Pallas kernels for 21%

profile of v10, /device:TPU:2, one launch (start us, length us, event | category | flops | bytes accessed | tf_op | source)
XLA Modules:
  0.0 160.3 jit_solution(4100583171011919072)
XLA Ops:
  0.6 2.1 %reshape.35.refs_2_.refs_3_.refs_1_.refs_4_ = bf16[128,2048]{1,0:T(8,128)(2,1)} reshape(bf16[64,2,2048]{2,1,0:T(2,128)(2,1)} %param.17) | data formatting | bytes 1048576 | tf_op jit(solution)/shard_map/reshape | solution.py:395
  2.8 1.0 reshape.34.refs_1_
  3.7 0.6 pad_add_fusion.refs_0_
  4.3 2.5 %shard_map.128 = (bf16[64,4224]{1,0:T(8,128)(2,1)}, bf16[64,4224]{1,0:T(8,128)(2,1)}) custom-call(s32[4]{0:T(128)} %pad_add_fusion.refs_0_, bf16[128,2048]{1,0:T(8,128)(2,1)} %reshape.34.refs_1_, bf16[128,2048]{1,0:T(8,128)(2,1)} %reshape.35.refs_2_.refs_3_.refs_1_.refs_4_, s32[2,32,64]{2,1,0:T(8,128)} %bitcast.7), custom_call_target="tpu_custom_call" | custom-call | flops 1 | bytes 1 | tf_op jit(solution)/shard_map/pallas_call | solution.py:39
  6.8 7.2 %collective-permute-start = (bf16[64,4224]{1,0:T(8,128)(2,1)}, bf16[64,4224]{1,0:T(8,128)(2,1)S(1)}, u32[]{:S(2)}, u32[]{:S(2)}) collective-permute-start(bf16[64,4224]{1,0:T(8,128)(2,1)} %get-tuple-element.33), channel_id=1, source_target_pairs={{0,32},{32,0},{1,33},{33,1},{2,34},{34,2},{3,35},{35,3},{4,36},{36... | collective-permute-start | bytes 1622024 | tf_op jit(solution)/shard_map/ppermute | solution.py:404
  14.0 1.0 reshape.36.refs_0_.refs_1_
  15.0 1.0 reshape.37.refs_1_.refs_2_
  16.0 1.0 reshape.38.refs_2_.refs_3_
  17.0 4.1 %shard_map.129.refs_2_.refs_5_ = f32[4,16,128]{2,1,0:T(8,128)} custom-call(bf16[128,2048]{1,0:T(8,128)(2,1)} %reshape.36.refs_0_.refs_1_, bf16[128,2048]{1,0:T(8,128)(2,1)} %reshape.37.refs_1_.refs_2_, bf16[128,2048]{1,0:T(8,128)(2,1)} %reshape.38.refs_2_.refs_3_, bf16[128,2048]{1,0:T(8,128)(2,1)} %reshape.35.refs_2_.refs_3_.refs_1_.refs_4_), custom_call_target="tpu_custom_call" | custom-call | flops 1 | bytes 1 | tf_op jit(solution)/shard_map/pallas_call | solution.py:39
  21.1 3.5 %shard_map.130.refs_5_ = bf16[272,2048]{1,0:T(8,128)(2,1)} custom-call(bf16[128,2048]{1,0:T(8,128)(2,1)} %reshape.36.refs_0_.refs_1_, bf16[128,2048]{1,0:T(8,128)(2,1)} %reshape.35.refs_2_.refs_3_.refs_1_.refs_4_, f32[4,16,128]{2,1,0:T(8,128)} %shard_map.129.refs_2_.refs_5_), custom_call_target="tpu_custom_call" | custom-call | flops 1 | bytes 1 | tf_op jit(solution)/shard_map/pallas_call | solution.py:39
  24.6 1.3 collective-permute-start.4
  25.9 0.1 broadcast_in_dim.6
  26.0 0.7 broadcast_in_dim_reshape.6.refs_4_
  26.7 2.0 %collective-permute-done.refs_2_ = bf16[64,4224]{1,0:T(8,128)(2,1)S(1)} collective-permute-done((bf16[64,4224]{1,0:T(8,128)(2,1)}, bf16[64,4224]{1,0:T(8,128)(2,1)S(1)}, u32[]{:S(2)}, u32[]{:S(2)}) %collective-permute-start) | collective-permute-done | bytes 540704 | tf_op jit(solution)/shard_map/ppermute | solution.py:404
  28.7 0.8 copy-done.6
  29.5 5.7 %shard_map.131 = (bf16[128,2048]{1,0:T(8,128)(2,1)}, bf16[128,2048]{1,0:T(8,128)(2,1)}, bf16[128,256]{1,0:T(8,128)(2,1)}, f32[128,128]{1,0:T(8,128)}, f32[128,12...) custom-call(s32[4]{0:T(128)} %pad_add_fusion.refs_0_, ...), custom_call_target="tpu_custom_call" | custom-call | flops 1 | bytes 1 | tf_op jit(solution)/shard_map/pallas_call | solution.py:39
  35.3 6.1 %collective-permute-start.1 = (bf16[144,2048]{1,0:T(8,128)(2,1)}, bf16[144,2048]{1,0:T(8,128)(2,1)S(1)}, u32[]{:S(2)}, u32[]{:S(2)}) collective-permute-start(bf16[144,2048]{1,0:T(8,128)(2,1)} %get-tuple-element.34), channel_id=1, source_target_pairs={{0,64},{64,128},{128,192},{192,0},{1,65},{65,129},{129,193},{193,1... | collective-permute-start | bytes 1769480 | tf_op jit(solution)/shard_map/ppermute | solution.py:425
  41.4 2.9 %collective-permute-start.2 = (bf16[144,2048]{1,0:T(8,128)(2,1)}, bf16[144,2048]{1,0:T(8,128)(2,1)S(1)}, u32[]{:S(2)}, u32[]{:S(2)}) collective-permute-start(bf16[144,2048]{1,0:T(8,128)(2,1)} %get-tuple-element.35), channel_id=1, source_target_pairs={{0,128},{64,192},{128,0},{192,64},{1,129},{65,193},{129,1},{193,65... | collective-permute-start | bytes 1769480 | tf_op jit(solution)/shard_map/ppermute | solution.py:425
  44.3 1.4 collective-permute-start.3
  45.6 0.1 broadcast_in_dim.7
  45.7 0.7 broadcast_in_dim_reshape.7.refs_5_
  46.4 3.7 %shard_map.132 = (bf16[128,2048]{1,0:T(8,128)(2,1)}, f32[128,128]{1,0:T(8,128)}, f32[128,128]{1,0:T(8,128)}, bf16[2048,128]{1,0:T(8,128)(2,1)}) custom-call(f32[32]{0:T(128)} %refs_0_.1, bf16[128,2048]{1,0:T(8,128)(2,1)} %get-tuple-element.42.refs_1_, bf16[128,2048]{1,0:T(8,128)(2,1)} %get-tuple-element.37.refs_2_.refs_7_, ...), custom_call_target="tpu_custom_call" | custom-call | flops 1 | bytes 1 | tf_op jit(solution)/shard_map/pallas_call | solution.py:39
  50.0 15.2 %collective-permute-done.4.refs_0_ = bf16[272,2048]{1,0:T(8,128)(2,1)S(1)} collective-permute-done((bf16[272,2048]{1,0:T(8,128)(2,1)}, bf16[272,2048]{1,0:T(8,128)(2,1)S(1)}, u32[]{:S(2)}, u32[]{:S(2)}) %collective-permute-start.4) | collective-permute-done | bytes 1114144 | tf_op jit(solution)/shard_map/ppermute | solution.py:410
  65.2 1.0 copy-done
  66.2 7.3 %shard_map.133 = (bf16[144,2048]{1,0:T(8,128)(2,1)}, bf16[128,2048]{1,0:T(8,128)(2,1)}, bf16[128,2048]{1,0:T(8,128)(2,1)}) custom-call(bf16[272,2048]{1,0:T(8,128)(2,1)} %copy-done, bf16[128,2048]{1,0:T(8,128)(2,1)} %reshape.37.refs_1_.refs_2_, bf16[128,2048]{1,0:T(8,128)(2,1)} %reshape.38.refs_2_.refs_3_), custom_call_target="tpu_custom_call" | custom-call | flops 1 | bytes 1 | tf_op jit(solution)/shard_map/pallas_call | solution.py:39
  73.5 0.0 collective-permute-done.1.refs_1_
  73.5 0.0 collective-permute-done.2.refs_2_
  73.5 0.8 copy-done.3
  74.3 0.2 copy-done.4
  74.5 0.2 copy-done.5
  74.7 5.9 %shard_map.134 = (bf16[64,2048]{1,0:T(8,128)(2,1)}, bf16[64,2048]{1,0:T(8,128)(2,1)}, bf16[4,4,64,256]{3,2,1,0:T(8,128)(2,1)}, bf16[4,4,64,256]{3,2,1,0:T(8,128)(2,1)}) custom-call(s32[4]{0:T(128)} %pad_add_fusion.refs_0_, bf16[144,2048]{1,0:T(8,128)(2,1)} %copy-done.3, bf16[144,2048]{1,0:T(8,128)(2,1)} %copy-done.4, bf16[144,2048]{1,0:T(8,128)(2,1)} %copy-done.5, ...), custom_call_target="tpu_custom_call" | custom-call | flops 1 | bytes 1 | tf_op jit(solution)/shard_map/pallas_call | solution.py:39
  80.6 0.0 collective-permute-start.7
  80.6 29.5 %collective-permute-start.6 = (bf16[144,2048]{1,0:T(8,128)(2,1)S(1)}, bf16[144,2048]{1,0:T(8,128)(2,1)S(1)}, u32[]{:S(2)}, u32[]{:S(2)}) collective-permute-start(bf16[144,2048]{1,0:T(8,128)(2,1)S(1)} %copy-done.2), channel_id=1, source_target_pairs={{0,32},{32,64},{64,96},{96,128},{128,160},{160,192},{192,224},{1,3... | collective-permute-start | bytes 1769480 | tf_op jit(solution)/shard_map/ppermute | solution.py:458
  110.1 2.1 %add_convert_fusion = bf16[4,4,64,256]{3,2,1,0:T(8,128)(2,1)} fusion(bf16[4,4,64,256]{3,2,1,0:T(8,128)(2,1)S(1)} %collective-permute-done.7, bf16[4,4,64,256]{3,2,1,0:T(8,128)(2,1)} %get-tuple-element.54), kind=kLoop, calls=%fused_computation | loop fusion | flops 1048576 | bytes 1572864 | tf_op jit(solution)/shard_map/convert_element_type | solution.py:451
  112.1 7.1 %all-to-all-start = ((bf16[16,64,256]{2,1,0:T(8,128)(2,1)}), bf16[16,64,256]{2,1,0:T(8,128)(2,1)S(1)}, u32[]{:S(2)}, u32[]{:S(2)}) async-start(bf16[16,64,256]{2,1,0:T(8,128)(2,1)} %bitcast.5.refs_9_), calls=%async_computation | async-start | bytes 1048576 | tf_op jit(solution)/shard_map/all_to_all | solution.py:453
  119.3 3.7 %collective-permute-start.5 = (bf16[64,2048]{1,0:T(8,128)(2,1)S(1)}, bf16[64,2048]{1,0:T(8,128)(2,1)S(1)}, u32[]{:S(2)}, u32[]{:S(2)}) collective-permute-start(bf16[64,2048]{1,0:T(8,128)(2,1)S(1)} %copy-done.14), channel_id=1, source_target_pairs={{0,32},{32,0},{1,33},{33,1},{2,34},{34,2},{3,35},{35,3},{4,36},{36... | collective-permute-start | bytes 786440 | tf_op jit(solution)/shard_map/ppermute | solution.py:449
  122.9 6.9 %all-to-all-done = bf16[16,64,256]{2,1,0:T(8,128)(2,1)S(1)} async-done(((bf16[16,64,256]{2,1,0:T(8,128)(2,1)}), bf16[16,64,256]{2,1,0:T(8,128)(2,1)S(1)}, u32[]{:S(2)}, u32[]{:S(2)}) %all-to-all-start) | async-done | bytes 524320 | tf_op jit(solution)/shard_map/all_to_all | solution.py:453
  129.8 0.7 reduce_sum.21
  130.5 16.2 %all-to-all-start.1 = ((bf16[8,8,256]{2,1,0:T(8,128)(2,1)}), bf16[8,8,256]{2,1,0:T(8,128)(2,1)S(1)}, u32[]{:S(2)}, u32[]{:S(2)}) async-start(bf16[8,8,256]{2,1,0:T(8,128)(2,1)} %bitcast.6), calls=%async_computation.1 | async-start | bytes 65536 | tf_op jit(solution)/shard_map/all_to_all | solution.py:455
  146.7 0.0 collective-permute-done.6.refs_6_
  146.7 0.8 copy-done.1
  147.5 7.0 %shard_map.135 = (bf16[64,2,2048]{2,1,0:T(2,128)(2,1)}, bf16[64,2,2048]{2,1,0:T(2,128)(2,1)}, bf16[64,2,2048]{2,1,0:T(2,128)(2,1)}) custom-call(s32[4]{0:T(128)} %pad_add_fusion.refs_0_, bf16[128,2048]{1,0:T(8,128)(2,1)} %reshape.36.refs_0_.refs_1_, bf16[128,2048]{1,0:T(8,128)(2,1)} %reshape.37.refs_1_.refs_2_, bf16[128,2048]{1,0:T(8,128)(2,1)} %reshape.38.refs_2_.refs_3_, ...), custom_call_target="tpu_custom_call" | custom-call | flops 1 | bytes 1 | tf_op jit(solution)/shard_map/pallas_call | solution.py:39
  154.6 0.0 copy-start.11
  154.6 0.7 copy-done.11
  155.3 2.3 %shard_map.136 = bf16[128,2048]{1,0:T(8,128)(2,1)} custom-call(s32[4]{0:T(128)} %pad_add_fusion.refs_0_, bf16[64,2048]{1,0:T(8,128)(2,1)} %get-tuple-element.50.refs_1_, bf16[64,2048]{1,0:T(8,128)(2,1)} %copy-done.11, bf16[64,2,2048]{2,1,0:T(2,128)(2,1)} %get-tuple-element.29.refs_3_), custom_call_target="tpu_custom_call" | custom-call | flops 1 | bytes 1 | tf_op jit(solution)/shard_map/pallas_call | solution.py:39
  157.5 2.2 %reshape.40 = bf16[64,2,2048]{2,1,0:T(2,128)(2,1)} reshape(bf16[128,2048]{1,0:T(8,128)(2,1)} %shard_map.136) | data formatting | bytes 1048576 | tf_op jit(solution)/shard_map/reshape | solution.py:469
  159.7 0.0 all-to-all-done.1
  159.7 0.6 convert_reduce_fusion
  (25 shorter events, 0.0 us)
Async XLA Ops:
  0.6 2.1 %copy-start.7 = (bf16[64,2,2048]{2,1,0:T(2,128)(2,1)S(1)}, bf16[64,2,2048]{2,1,0:T(2,128)(2,1)}, u32[]{:S(2)}) copy-start(bf16[64,2,2048]{2,1,0:T(2,128)(2,1)} %param.9) | copy-start | bytes 1572868
  2.7 11.2 %copy-start.8 = (bf16[64,2,2048]{2,1,0:T(2,128)(2,1)S(1)}, bf16[64,2,2048]{2,1,0:T(2,128)(2,1)}, u32[]{:S(2)}) copy-start(bf16[64,2,2048]{2,1,0:T(2,128)(2,1)} %param.14) | copy-start | bytes 1572868
  3.7 11.2 %copy-start.9 = (bf16[64,2,2048]{2,1,0:T(2,128)(2,1)S(1)}, bf16[64,2,2048]{2,1,0:T(2,128)(2,1)}, u32[]{:S(2)}) copy-start(bf16[64,2,2048]{2,1,0:T(2,128)(2,1)} %param.15) | copy-start | bytes 1572868
  6.8 9.2 %copy-start.10 = (bf16[64,2,2048]{2,1,0:T(2,128)(2,1)S(1)}, bf16[64,2,2048]{2,1,0:T(2,128)(2,1)}, u32[]{:S(2)}) copy-start(bf16[64,2,2048]{2,1,0:T(2,128)(2,1)} %param.16) | copy-start | bytes 1572868
  6.8 21.9 %collective-permute-start = (bf16[64,4224]{1,0:T(8,128)(2,1)}, bf16[64,4224]{1,0:T(8,128)(2,1)S(1)}, u32[]{:S(2)}, u32[]{:S(2)}) collective-permute-start(bf16[64,4224]{1,0:T(8,128)(2,1)} %get-tuple-element.33), channel_id=1, source_target_pairs={{0,32},{32,0},{1,33},{33,1},{2,34},{34,2},{3,35},{35,3},{4,36},{36... | collective-permute-start | bytes 1622024 | tf_op jit(solution)/shard_map/ppermute | solution.py:404
  21.1 4.8 %copy-start.12 = (f32[32]{0:T(128)S(1)}, f32[32]{0:T(128)}, u32[]{:S(2)}) copy-start(f32[32]{0:T(128)} %refs_0_.1) | copy-start | bytes 388
  24.6 40.5 %collective-permute-start.4 = (bf16[272,2048]{1,0:T(8,128)(2,1)}, bf16[272,2048]{1,0:T(8,128)(2,1)S(1)}, u32[]{:S(2)}, u32[]{:S(2)}) collective-permute-start(bf16[272,2048]{1,0:T(8,128)(2,1)} %shard_map.130.refs_5_), channel_id=1, source_target_pairs={{32,0},{64,32},{96,64},{128,96},{160,128},{192,160},{224,192},{33,... | collective-permute-start | bytes 3342344 | tf_op jit(solution)/shard_map/ppermute | solution.py:410
  28.7 0.8 copy-start.6
  29.5 16.1 %copy-start.13 = (f32[32]{0:T(128)S(1)}, f32[32]{0:T(128)}, u32[]{:S(2)}) copy-start(f32[32]{0:T(128)} %param.13) | copy-start | bytes 388
  35.3 38.2 %collective-permute-start.1 = (bf16[144,2048]{1,0:T(8,128)(2,1)}, bf16[144,2048]{1,0:T(8,128)(2,1)S(1)}, u32[]{:S(2)}, u32[]{:S(2)}) collective-permute-start(bf16[144,2048]{1,0:T(8,128)(2,1)} %get-tuple-element.34), channel_id=1, source_target_pairs={{0,64},{64,128},{128,192},{192,0},{1,65},{65,129},{129,193},{193,1... | collective-permute-start | bytes 1769480 | tf_op jit(solution)/shard_map/ppermute | solution.py:425
  41.4 32.1 %collective-permute-start.2 = (bf16[144,2048]{1,0:T(8,128)(2,1)}, bf16[144,2048]{1,0:T(8,128)(2,1)S(1)}, u32[]{:S(2)}, u32[]{:S(2)}) collective-permute-start(bf16[144,2048]{1,0:T(8,128)(2,1)} %get-tuple-element.35), channel_id=1, source_target_pairs={{0,128},{64,192},{128,0},{192,64},{1,129},{65,193},{129,1},{193,65... | collective-permute-start | bytes 1769480 | tf_op jit(solution)/shard_map/ppermute | solution.py:425
  44.3 29.2 %collective-permute-start.3 = (bf16[144,2048]{1,0:T(8,128)(2,1)}, bf16[144,2048]{1,0:T(8,128)(2,1)S(1)}, u32[]{:S(2)}, u32[]{:S(2)}) collective-permute-start(bf16[144,2048]{1,0:T(8,128)(2,1)} %get-tuple-element.36), channel_id=1, source_target_pairs={{0,192},{64,0},{128,64},{192,128},{1,193},{65,1},{129,65},{193,129... | collective-permute-start | bytes 1769480 | tf_op jit(solution)/shard_map/ppermute | solution.py:425
  65.2 1.0 copy-start
  73.5 0.8 copy-start.3
  73.5 1.0 copy-start.4
  73.5 1.2 copy-start.5
  74.7 5.9 %copy-start.2 = (bf16[144,2048]{1,0:T(8,128)(2,1)S(1)}, bf16[144,2048]{1,0:T(8,128)(2,1)}, u32[]{:S(2)}) copy-start(bf16[144,2048]{1,0:T(8,128)(2,1)} %get-tuple-element.49.refs_16_) | copy-start | bytes 1769476
  80.6 29.5 %collective-permute-start.7 = (bf16[4,4,64,256]{3,2,1,0:T(8,128)(2,1)}, bf16[4,4,64,256]{3,2,1,0:T(8,128)(2,1)S(1)}, u32[]{:S(2)}, u32[]{:S(2)}) collective-permute-start(bf16[4,4,64,256]{3,2,1,0:T(8,128)(2,1)} %get-tuple-element.55), channel_id=1, source_target_pairs={{0,1},{1,0},{2,3},{3,2},{4,5},{5,4},{6,7},{7,6},{8,9},{9,8},{10,11... | collective-permute-start | bytes 1572872 | tf_op jit(solution)/shard_map/ppermute | solution.py:451
  80.6 66.1 %collective-permute-start.6 = (bf16[144,2048]{1,0:T(8,128)(2,1)S(1)}, bf16[144,2048]{1,0:T(8,128)(2,1)S(1)}, u32[]{:S(2)}, u32[]{:S(2)}) collective-permute-start(bf16[144,2048]{1,0:T(8,128)(2,1)S(1)} %copy-done.2), channel_id=1, source_target_pairs={{0,32},{32,64},{64,96},{96,128},{128,160},{160,192},{192,224},{1,3... | collective-permute-start | bytes 1769480 | tf_op jit(solution)/shard_map/ppermute | solution.py:458
  110.1 9.2 %copy-start.14 = (bf16[64,2048]{1,0:T(8,128)(2,1)S(1)}, bf16[64,2048]{1,0:T(8,128)(2,1)}, u32[]{:S(2)}) copy-start(bf16[64,2048]{1,0:T(8,128)(2,1)} %get-tuple-element.51) | copy-start | bytes 786436
  112.1 17.7 %all-to-all-start = ((bf16[16,64,256]{2,1,0:T(8,128)(2,1)}), bf16[16,64,256]{2,1,0:T(8,128)(2,1)S(1)}, u32[]{:S(2)}, u32[]{:S(2)}) async-start(bf16[16,64,256]{2,1,0:T(8,128)(2,1)} %bitcast.5.refs_9_), calls=%async_computation | async-start | bytes 1048576 | tf_op jit(solution)/shard_map/all_to_all | solution.py:453
  119.3 35.3 %collective-permute-start.5 = (bf16[64,2048]{1,0:T(8,128)(2,1)S(1)}, bf16[64,2048]{1,0:T(8,128)(2,1)S(1)}, u32[]{:S(2)}, u32[]{:S(2)}) collective-permute-start(bf16[64,2048]{1,0:T(8,128)(2,1)S(1)} %copy-done.14), channel_id=1, source_target_pairs={{0,32},{32,0},{1,33},{33,1},{2,34},{34,2},{3,35},{35,3},{4,36},{36... | collective-permute-start | bytes 786440 | tf_op jit(solution)/shard_map/ppermute | solution.py:449
  130.5 29.2 %all-to-all-start.1 = ((bf16[8,8,256]{2,1,0:T(8,128)(2,1)}), bf16[8,8,256]{2,1,0:T(8,128)(2,1)S(1)}, u32[]{:S(2)}, u32[]{:S(2)}) async-start(bf16[8,8,256]{2,1,0:T(8,128)(2,1)} %bitcast.6), calls=%async_computation.1 | async-start | bytes 65536 | tf_op jit(solution)/shard_map/all_to_all | solution.py:455
  146.7 0.8 copy-start.1
  154.6 0.7 copy-start.11
